TPU v7x, 256 devices: a whole 4x4x8 slice. The times are simulated.
256 devices in a mesh: segment: 2 (over core), seq: 128 (over z, x, y).
Axes of the slice: x: 4, y: 4, z: 8, core: 2. Of those that a mesh axis runs over, the one named last changes fastest.
Arguments:
- residual_in: bfloat16 [32768, 2048], P('seq'), may hold values from -6 to 6
- queries: bfloat16 [2, 32768, 2048], P('segment', 'seq'), may hold values from -6 to 6
- keys: bfloat16 [2, 32768, 2048], P('segment', 'seq'), may hold values from -6 to 6
- values: bfloat16 [2, 32768, 2048], P('segment', 'seq'), may hold values from -6 to 6
- head_offset: float32 [2, 16], P('segment'), may hold values from -4 to -2
- head_slope: float32 [2, 16], P('segment'), may hold values from 0.2 to 4
- key_lists: int32 [2, 256, 16, 4], P('segment', 'seq'), may hold values from 0 to 255, as said below
- shard_span: int32 [128], replicated, may hold values from 0 to 127, each once
- out_weight: bfloat16 [2, 2048, 2048], P('segment', 'seq'), may hold values from -0.125 to 0.125
Outputs:
- sections_out: bfloat16 [2, 32768, 2048], P('segment', 'seq')
Inputs may be any that keep to these rules, and one draw needn't show every extreme that they name: Entry key_lists[s, b, h, j] names a key block stored on another shard than query block b (block c lies on shard c // 2); the 4 entries of one query block and head lie on 4 different shards; in each section the entries of one shard's query blocks name blocks of any one other shard at most 2 * 1 times, every shard reaches that count for some other shard, and one shard is named that often by every other shard. Each shard number appears once; shard i holds the positions from shard_span[i] * 256 on.
All inputs are finite; a program needn't handle non-finite values.
Results may differ from a plain program's by a relative error of at most 0.015.
Values may be sent and summed in bfloat16 or wider, within the bound.
No kernel may reach another device: no remote copies, remote signals or barrier semaphores. Data moves between devices by JAX's collectives and lax.ppermute only.
A program may use at most 128 MiB of HBM per device.

v0:
```python
import jax
import jax.numpy as jnp
from jax import lax
from jax.sharding import PartitionSpec as P


def shifted(block, axis, distance):
    devices = range(lax.axis_size(axis))
    route = [(i - distance, i) for i in devices if i - distance in devices]
    return lax.ppermute(block, axis, route)


def pair_weights(query_rows, key_rows, offsets, slopes, query_pos, key_pos, total_len):
    head_size = query_rows.shape[-1]
    raw_dot = jnp.einsum(
        "...qd,...kd->...qk", query_rows, key_rows, preferred_element_type=jnp.float32
    )
    distance = (
        jnp.abs(query_pos[..., :, None] - key_pos[..., None, :]).astype(jnp.float32) / total_len
    )
    scores = (
        raw_dot * head_size ** (-0.5)
        + offsets[..., None, None]
        - slopes[..., None, None] * distance
    )
    return jax.nn.sigmoid(scores).astype(jnp.bfloat16)


def head_blocks(matrix, per_shard, head_count):
    tokens_here, row_width = matrix.shape
    shaped = matrix.reshape(
        per_shard, tokens_here // per_shard, head_count, row_width // head_count
    )
    return shaped.transpose(0, 2, 1, 3).reshape(
        per_shard * head_count, tokens_here // per_shard, row_width // head_count
    )


def per_device(
    residual_in, queries, keys, values, head_offset, head_slope, key_lists, shard_span, out_weight
):
    query_part = queries[0]
    key_part = keys[0]
    value_part = values[0]
    offsets = head_offset[0]
    slopes = head_slope[0]
    entries = key_lists[0]
    per_shard, head_count, listed = entries.shape
    tok_here, feature_width = query_part.shape
    block_len = tok_here // per_shard
    head_size = feature_width // head_count
    shards = lax.axis_size("seq")
    total_len = tok_here * shards
    own_span = shard_span[lax.axis_index("seq")]
    positions = own_span * tok_here + jnp.arange(tok_here, dtype=jnp.int32)
    block_rows = jnp.arange(block_len, dtype=jnp.int32)
    query_heads = query_part.reshape(tok_here, head_count, head_size)
    key_heads = key_part.reshape(tok_here, head_count, head_size)
    value_head_rows = value_part.reshape(tok_here, head_count, head_size)
    segment_weights = pair_weights(
        query_heads.transpose(1, 0, 2),
        key_heads.transpose(1, 0, 2),
        offsets,
        slopes,
        positions,
        positions,
        total_len,
    )
    segment_output = jnp.einsum(
        "uzi,iuc->zuc", segment_weights, value_head_rows, preferred_element_type=jnp.float32
    )
    query_blocks = head_blocks(query_part, per_shard, head_count)
    key_blocks = head_blocks(key_part, per_shard, head_count)
    value_blocks = head_blocks(value_part, per_shard, head_count)
    item_count = per_shard * head_count * listed
    flat_keys = entries.reshape(item_count)
    item_ids = jnp.arange(item_count, dtype=jnp.int32)
    item_block = item_ids // listed
    item_head = item_block % head_count
    item_start = own_span * tok_here + item_ids // (head_count * listed) * block_len
    owners = flat_keys // per_shard
    key_local = flat_keys % per_shard
    capacity = 2 * item_count // shards
    onehot = (owners[:, None] == jnp.arange(shards, dtype=jnp.int32)[None, :]).astype(jnp.int32)
    before = jnp.cumsum(onehot, axis=0) - onehot
    slot_ids = jnp.sum(before * onehot, axis=1)
    places = owners * capacity + slot_ids
    filled = jnp.full((shards * capacity,), item_count - 1, jnp.int32).at[places].set(item_ids)
    sent_queries = query_blocks[item_block[filled]].reshape(shards, capacity, block_len, head_size)
    item_tags = jnp.stack(
        [key_local[filled], item_head[filled], item_start[filled]], axis=-1
    ).reshape(shards, capacity, 3)
    got_query = lax.all_to_all(sent_queries, "seq", split_axis=0, concat_axis=0, tiled=True)
    got_tags = lax.all_to_all(item_tags, "seq", split_axis=0, concat_axis=0, tiled=True)
    key_position_index = got_tags[..., 0] * head_count + got_tags[..., 1]
    query_pos = got_tags[..., 2][..., None] + block_rows
    key_pos = (own_span * tok_here + got_tags[..., 0] * block_len)[..., None] + block_rows
    weights = pair_weights(
        got_query,
        key_blocks[key_position_index],
        offsets[got_tags[..., 1]],
        slopes[got_tags[..., 1]],
        query_pos,
        key_pos,
        total_len,
    )
    partial_value = jnp.einsum(
        "scqk,sckd->scqd",
        weights,
        value_blocks[key_position_index],
        preferred_element_type=jnp.float32,
    )
    returned = lax.all_to_all(
        partial_value.astype(jnp.bfloat16), "seq", split_axis=0, concat_axis=0, tiled=True
    )
    per_item = returned.reshape(shards * capacity, block_len, head_size)[places]
    remote = (
        per_item.astype(jnp.float32)
        .reshape(per_shard, head_count, listed, block_len, head_size)
        .sum(axis=2)
    )
    merged = segment_output.reshape(per_shard, block_len, head_count, head_size) + remote.transpose(
        0, 2, 1, 3
    )
    attended = merged.reshape(tok_here, feature_width).astype(jnp.bfloat16)
    projected = jnp.dot(
        attended,
        lax.all_gather(out_weight[0], "seq", axis=0, tiled=True),
        preferred_element_type=jnp.float32,
    )
    first_out = (residual_in.astype(jnp.float32) + projected).astype(jnp.bfloat16)
    handed = shifted(first_out, "segment", 1)
    latter_section = (handed.astype(jnp.float32) + projected).astype(jnp.bfloat16)
    segment_at = lax.axis_index("segment")
    result = jnp.where(segment_at == 0, first_out, latter_section)
    return result[None]


def solution(mesh):
    in_specs = (
        P("seq", None),
        P("segment", "seq", None),
        P("segment", "seq", None),
        P("segment", "seq", None),
        P("segment", None),
        P("segment", None),
        P("segment", "seq", None, None),
        P(),
        P("segment", "seq", None),
    )
    out_specs = P("segment", "seq", None)
    return jax.shard_map(
        per_device, mesh=mesh, in_specs=in_specs, out_specs=out_specs, check_vma=False
    )
```

profile of v0, /device:TPU:1, one launch (start us, length us, event | category | flops | bytes accessed | tf_op | source)
XLA Modules:
  0.0 524.8 jit_solution(1081117083060173411)
XLA Ops:
  6.5 0.8 copy.80
  8.0 1.0 scatter_custom_fusion
  9.0 1.2 dynamic_slice.3
  10.9 1.9 gather_fusion.4
  13.0 1.9 gather_fusion.2
  15.0 1.9 gather_fusion.3
  17.0 1.5 copy.83
  18.5 16.3 %all-to-all-start.1 = ((s32[128,2,3]{2,1,0:T(2,128)}), s32[128,2,3]{2,1,0:T(2,128)S(1)}, u32[]{:S(2)}, u32[]{:S(2)}) async-start(s32[128,2,3]{2,1,0:T(2,128)} %copy.83), calls=%async_computation.1 | async-start | bytes 262144 | tf_op jit(solution)/shard_map/all_to_all | solution.py:94
  34.9 1.9 gather_fusion
  36.8 1.5 copy.97
  38.7 8.5 %gather_fusion.1 = bf16[256,128,128]{2,1,0:T(8,128)(2,1)} fusion(bf16[32,128,128]{2,1,0:T(8,128)(2,1)S(1)} %bitcast.199, s32[1024]{0:T(1024)S(1)} %pad_clamp_fusion.2), kind=kCustom, calls=%fused_computation.1 | custom fusion | bytes 16778240 | tf_op jit(solution)/shard_map/gather | solution.py:89
  47.2 14.0 %all-to-all-start = ((bf16[128,2,128,128]{3,2,1,0:T(8,128)(2,1)}), bf16[128,2,128,128]{3,2,1,0:T(8,128)(2,1)}, u32[]{:S(2)}, u32[]{:S(2)}) async-start(bf16[128,2,128,128]{3,2,1,0:T(8,128)(2,1)} %bitcast.200), calls=%async_computation | async-start | bytes 16777216 | tf_op jit(solution)/shard_map/all_to_all | solution.py:93
  62.0 1.5 copy.99
  63.5 1.0 copy-done.2
  66.3 1.0 fusion.33
  67.3 1.0 copy.96
  68.3 9.8 %bitcast_select_fusion.17 = f32[128,2]{0,1:T(2,128)S(1)} fusion(f32[]{:T(128)} %bitcast.35, f32[]{:T(128)} %bitcast.36, f32[]{:T(128)} %bitcast.37, f32[]{:T(128)} %bitcast.38, f32[]{:T(128)} %bitcast.39, f32[]{:T(128)} %bitcast.41, f32[]{:T(128)} %bitcast.40, f32[]{:T(128)} %bitcast.18, f32[]{:T(128)} %bitcast.20, f32[]{:T(128)} %bitcast.22, f32[]{:T(128)} %bitcast.24, ...), kind=kLoop, calls=%fused_computation.69 | loop fusion | flops 8448 | bytes 2112 | tf_op jit(solution)/shard_map/gather | solution.py:101
  78.1 0.7 copy.87
  78.9 10.2 %fusion.22 = f32[128,2]{0,1:T(2,128)S(1)} fusion(f32[]{:T(128)} %bitcast.54, f32[]{:T(128)} %bitcast.55, f32[]{:T(128)} %bitcast.56, f32[]{:T(128)} %bitcast.57, f32[]{:T(128)} %bitcast.58, f32[]{:T(128)} %bitcast.60, f32[]{:T(128)} %bitcast.59, f32[]{:T(128)} %bitcast.45, f32[]{:T(128)} %bitcast.46, f32[]{:T(128)} %bitcast.47, f32[]{:T(128)} %bitcast.48, ...), kind=kLoop, calls=%fused_computation.82 | loop fusion | flops 8704 | bytes 2112 | tf_op jit(solution)/shard_map/mul | solution.py:24
  90.5 8.6 %gather_fusion.5 = bf16[256,128,128]{2,1,0:T(8,128)(2,1)} fusion(bf16[32,128,128]{2,1,0:T(8,128)(2,1)S(1)} %bitcast.197, s32[1024]{0:T(1024)S(1)} %pad_clamp_fusion.1), kind=kCustom, calls=%fused_computation.5 | custom fusion | bytes 16778240 | tf_op jit(solution)/shard_map/gather | solution.py:100
  99.1 8.6 %gather_fusion.6 = bf16[256,128,128]{2,1,0:T(8,128)(2,1)} fusion(bf16[32,128,128]{2,1,0:T(8,128)(2,1)S(1)} %bitcast.198, s32[1024]{0:T(1024)S(1)} %pad_clamp_fusion.1), kind=kCustom, calls=%fused_computation.6 | custom fusion | bytes 16778240 | tf_op jit(solution)/shard_map/gather | solution.py:110
  108.0 136.6 %all-to-all-done = bf16[128,2,128,128]{3,2,1,0:T(8,128)(2,1)} async-done(((bf16[128,2,128,128]{3,2,1,0:T(8,128)(2,1)}), bf16[128,2,128,128]{3,2,1,0:T(8,128)(2,1)}, u32[]{:S(2)}, u32[]{:S(2)}) %all-to-all-start) | async-done | bytes 8388640 | tf_op jit(solution)/shard_map/all_to_all | solution.py:93
  244.6 16.2 %fusion.5 = bf16[128,2,128,128]{3,2,1,0:T(8,128)(2,1)} fusion(bf16[128,2,128,128]{3,2,1,0:T(8,128)(2,1)} %bitcast.202, f32[128,2]{1,0:T(8,128)S(1)} %copy-done.8, f32[128,2]{1,0:T(8,128)S(1)} %copy-done.9, s32[128,2,128]{2,1,0:T(2,128)S(1)} %get-tuple-element.46, s32[128,2,128]{2,1,0:T(2,128)S(1)} %get-tuple-element.47, ...), kind=kOutput, calls=%fused_computation.15 | convolution fusion | flops 2197815296 | bytes 33818624 | tf_op jit(solution)/shard_map/scqk,sckd->scqd/dot_general | solution.py:107
  260.8 11.8 %all-to-all-start.2 = ((bf16[128,2,128,128]{3,2,1,0:T(8,128)(2,1)}), bf16[128,2,128,128]{3,2,1,0:T(8,128)(2,1)}, u32[]{:S(2)}, u32[]{:S(2)}) async-start(bf16[128,2,128,128]{3,2,1,0:T(8,128)(2,1)} %fusion.5), calls=%async_computation.2 | async-start | bytes 16777216 | tf_op jit(solution)/shard_map/all_to_all | solution.py:113
  273.5 3.5 fusion.7
  277.1 212.8 %all-to-all-done.2 = bf16[128,2,128,128]{3,2,1,0:T(8,128)(2,1)} async-done(((bf16[128,2,128,128]{3,2,1,0:T(8,128)(2,1)}), bf16[128,2,128,128]{3,2,1,0:T(8,128)(2,1)}, u32[]{:S(2)}, u32[]{:S(2)}) %all-to-all-start.2) | async-done | bytes 8388640 | tf_op jit(solution)/shard_map/all_to_all | solution.py:113
  489.9 6.4 %gather_fusion.7 = bf16[128,128,128]{2,1,0:T(8,128)(2,1)} fusion(bf16[256,128,128]{2,1,0:T(8,128)(2,1)} %bitcast.65, s32[1024]{0:T(1024)S(1)} %pad_clamp_fusion), kind=kCustom, calls=%fused_computation.7 | custom fusion | bytes 8389120 | tf_op jit(solution)/shard_map/gather | solution.py:116
  496.3 3.2 convert_reduce_fusion
  500.6 6.9 %add_convert_fusion.1 = (bf16[256,2048]{1,0:T(8,128)(2,1)}, f32[256,2048]{1,0:T(8,128)S(1)}) fusion(bf16[256,2048]{1,0:T(8,128)(2,1)} %param.9, bf16[1,2048,2048]{2,1,0:T(8,128)(2,1)} %all-gather.3.cloned.1.call-done, bf16[32,8,16,128]{3,2,1,0:T(8,128)(2,1)S(1)} %bitcast.213), kind=kOutput, calls=%fused_computation.20 | convolution fusion | flops 2149056512 | bytes 13631488 | tf_op jit(solution)/shard_map/dot_general | solution.py:126
  507.6 1.3 collective-permute-start
  508.8 7.6 %collective-permute-done = bf16[256,2048]{1,0:T(8,128)(2,1)S(1)} collective-permute-done((bf16[256,2048]{1,0:T(8,128)(2,1)}, bf16[256,2048]{1,0:T(8,128)(2,1)S(1)}, u32[]{:S(2)}, u32[]{:S(2)}) %collective-permute-start) | collective-permute-done | bytes 1048608 | tf_op jit(solution)/shard_map/ppermute | solution.py:10
  516.5 1.4 fusion.9
  (66 shorter events, 7.8 us)
Async XLA Ops:
  18.5 28.7 %all-to-all-start.1 = ((s32[128,2,3]{2,1,0:T(2,128)}), s32[128,2,3]{2,1,0:T(2,128)S(1)}, u32[]{:S(2)}, u32[]{:S(2)}) async-start(s32[128,2,3]{2,1,0:T(2,128)} %copy.83), calls=%async_computation.1 | async-start | bytes 262144 | tf_op jit(solution)/shard_map/all_to_all | solution.py:94
  47.2 14.1 %copy-start.5 = (bf16[1,256,2048]{2,1,0:T(8,128)(2,1)S(1)}, bf16[1,256,2048]{2,1,0:T(8,128)(2,1)}, u32[]{:S(2)}) copy-start(bf16[1,256,2048]{2,1,0:T(8,128)(2,1)} %param.11) | copy-start | bytes 3145732
  47.2 197.4 %all-to-all-start = ((bf16[128,2,128,128]{3,2,1,0:T(8,128)(2,1)}), bf16[128,2,128,128]{3,2,1,0:T(8,128)(2,1)}, u32[]{:S(2)}, u32[]{:S(2)}) async-start(bf16[128,2,128,128]{3,2,1,0:T(8,128)(2,1)} %bitcast.200), calls=%async_computation | async-start | bytes 16777216 | tf_op jit(solution)/shard_map/all_to_all | solution.py:93
  61.3 3.6 copy-start.6
  61.3 4.3 copy-start.7
  61.5 2.0 copy-start
  63.5 1.0 copy-start.2
  99.1 145.5 %copy-start.8 = (f32[128,2]{1,0:T(8,128)S(1)}, f32[128,2]{1,0:T(8,128)}, u32[]{:S(2)}) copy-start(f32[128,2]{1,0:T(8,128)} %copy.87) | copy-start | bytes 3076
  99.1 145.5 %copy-start.9 = (f32[128,2]{1,0:T(8,128)S(1)}, f32[128,2]{1,0:T(8,128)}, u32[]{:S(2)}) copy-start(f32[128,2]{1,0:T(8,128)} %copy.91) | copy-start | bytes 3076
  260.8 12.7 %copy-start.1 = (bf16[32,8,16,128]{3,2,1,0:T(8,128)(2,1)S(1)}, bf16[32,8,16,128]{3,2,1,0:T(8,128)(2,1)}, u32[]{:S(2)}) copy-start(bf16[32,8,16,128]{3,2,1,0:T(8,128)(2,1)} %copy-done) | copy-start | bytes 3145732
  260.8 12.7 %copy-start.3 = (bf16[32,8,16,128]{3,2,1,0:T(8,128)(2,1)S(1)}, bf16[32,8,16,128]{3,2,1,0:T(8,128)(2,1)}, u32[]{:S(2)}) copy-start(bf16[32,8,16,128]{3,2,1,0:T(8,128)(2,1)} %copy-done.2) | copy-start | bytes 3145732
  260.8 229.0 %all-to-all-start.2 = ((bf16[128,2,128,128]{3,2,1,0:T(8,128)(2,1)}), bf16[128,2,128,128]{3,2,1,0:T(8,128)(2,1)}, u32[]{:S(2)}, u32[]{:S(2)}) async-start(bf16[128,2,128,128]{3,2,1,0:T(8,128)(2,1)} %fusion.5), calls=%async_computation.2 | async-start | bytes 16777216 | tf_op jit(solution)/shard_map/all_to_all | solution.py:113
  272.6 228.0 %all-gather.3.cloned.1.call-start = ((), (), s32[]{:S(2)}) async-start(), calls=%async_computation.3 | async-start | bytes 8454144 | tf_op jit(solution)/shard_map/all_gather | solution.py:128
  277.1 222.5 %copy-start.4 = (f32[16,256,128]{2,1,0:T(8,128)S(1)}, f32[16,256,128]{2,1,0:T(8,128)}, u32[]{:S(2)}) copy-start(f32[16,256,128]{2,1,0:T(8,128)} %fusion.7) | copy-start | bytes 6291460
  507.6 8.9 %collective-permute-start = (bf16[256,2048]{1,0:T(8,128)(2,1)}, bf16[256,2048]{1,0:T(8,128)(2,1)S(1)}, u32[]{:S(2)}, u32[]{:S(2)}) collective-permute-start(bf16[256,2048]{1,0:T(8,128)(2,1)} %get-tuple-element.44), channel_id=1, source_target_pairs={{0,128},{1,129},{2,130},{3,131},{4,132},{5,133},{6,134},{7,135},{8... | collective-permute-start | bytes 3145736 | tf_op jit(solution)/shard_map/ppermute | solution.py:10
Sparse Core Ops, SparseCore 0:
  277.0 211.8 all-gather.2
where the time goes:
time: 526 us; the launch traced here: 525 us
  waiting for transfers between devices  358 us (68%)
  local copies, waits for them, and re-layouts  56.4 us (11%)
  starting transfers between devices  43.5 us (8%)
  matrix products  26.7 us (5%)
  other arithmetic  26 us (5%)
  between operations  14.5 us (3%)
    all_to_all x1, waiting for transfers between devices, per_device(): lax.all_to_all(partial_value.astype(jnp.bfloat16), 'seq', split_axis=0, c...  213 us
    all_to_all x1, waiting for transfers between devices, per_device(): lax.all_to_all(sent_queries, 'seq', split_axis=0, concat_axis=0, tiled=True)  137 us
    all_to_all x1, starting transfers between devices, per_device(): lax.all_to_all(item_tags, 'seq', split_axis=0, concat_axis=0, tiled=True)  16.3 us
    dot_general x1, matrix products, per_device(): jnp.einsum('scqk,sckd->scqd', weights, value_blocks[key_position_index],...  16.2 us
    all_to_all x1, starting transfers between devices, per_device(): lax.all_to_all(sent_queries, 'seq', split_axis=0, concat_axis=0, tiled=True)  14 us
    all_to_all x1, starting transfers between devices, per_device(): lax.all_to_all(partial_value.astype(jnp.bfloat16), 'seq', split_axis=0, c...  11.8 us
  transfers between devices with their start and end apart: 5, of which 3 were waited for; matrix products, arithmetic and copies ran while one was open for 14% of the time, Pallas kernels for 0%

commit v1 on v0

v1 whole, which is shorter than its diff:
```python
import jax
import jax.numpy as jnp
from jax import lax
from jax.experimental import pallas as pl
from jax.experimental.pallas import tpu as pltpu
from jax.sharding import Mesh, PartitionSpec as P

NZ, NX, NY = 8, 4, 4
PLANE = NX * NY
SEQ = ("z", "x", "y")
CHUNKS = ((0,), (-1, 1), (-2, 2), (-3, 3), (4,))
AHEAD = 3


def pack_kernel(slots, half, sel_ref, *refs):
    sources, out_ref, sem = refs[:-2], refs[-2], refs[-1]

    def copies(i):
        idx = sel_ref[i]
        if half:
            low, high = sources

            @pl.when(idx < half)
            def _():
                pltpu.make_async_copy(low.at[idx], out_ref.at[i], sem).start()

            @pl.when(idx >= half)
            def _():
                pltpu.make_async_copy(high.at[idx - half], out_ref.at[i], sem).start()
        else:
            for n, source in enumerate(sources):

                @pl.when(lax.rem(i // slots, len(sources)) == n)
                def _(source=source):
                    pltpu.make_async_copy(source.at[idx], out_ref.at[i], sem).start()

    total = out_ref.shape[0]

    @pl.loop(0, total)
    def _(i):
        copies(i)

    pltpu.make_async_copy(out_ref, out_ref, sem).wait()


def pack(sel, sources, half=0):
    _, shards, slots = sel.shape
    total = sel.size
    block = sources[0].shape[1:]
    out = pl.pallas_call(
        lambda *refs: pack_kernel(slots, half, *refs),
        out_shape=jax.ShapeDtypeStruct((total,) + block, sources[0].dtype),
        in_specs=[pl.BlockSpec(memory_space=pltpu.SMEM)]
        + [pl.BlockSpec(memory_space=pl.ANY)] * len(sources),
        out_specs=pl.BlockSpec(memory_space=pl.ANY),
        scratch_shapes=[pltpu.SemaphoreType.DMA],
        name="pack_blocks",
    )(sel.reshape(total), *sources)
    return out


def attend_kernel(
    per_shard, listed, scale, chunk_ref, slot_ref, base_ref, offset_ref, slope_ref,
    q_ref, k_ref, v_ref, *refs
):
    got, out_ref, held, sems = refs[:-3], refs[-3], refs[-2], refs[-1]
    h = pl.program_id(0)
    heads = pl.num_programs(0)
    blk = q_ref.shape[0] // per_shard
    items = per_shard * listed
    depth = AHEAD + 1

    def fetch(head):
        place = lax.rem(head, depth)
        for b in range(per_shard):
            for j in range(listed):
                i = (b * heads + head) * listed + j
                for c, buffer in enumerate(got):

                    @pl.when(chunk_ref[i] == c)
                    def _(buffer=buffer, i=i, n=b * listed + j):
                        pltpu.make_async_copy(
                            buffer.at[slot_ref[i]], held.at[place, n], sems.at[place]
                        ).start()

    @pl.when(h == 0)
    def _():
        for ahead in range(AHEAD):
            fetch(jnp.int32(ahead))

    @pl.when(h + AHEAD < heads)
    def _():
        fetch(h + AHEAD)

    offset = offset_ref[h]
    slope = slope_ref[h] / (1.0 * TOTAL)

    def weights(q, k, base):
        raw = lax.dot_general(q, k, (((1,), (1,)), ((), ())), preferred_element_type=jnp.float32)
        rows = lax.broadcasted_iota(jnp.int32, raw.shape, 0)
        cols = lax.broadcasted_iota(jnp.int32, raw.shape, 1)
        distance = jnp.abs(rows - cols + base).astype(jnp.float32)
        score = raw * scale + offset - slope * distance
        return (1.0 / (1.0 + jnp.exp(-score))).astype(jnp.bfloat16)

    local_w = weights(q_ref[...], k_ref[...], 0)
    local = jnp.dot(local_w, v_ref[...], preferred_element_type=jnp.float32)
    place = lax.rem(h, depth)
    pltpu.make_async_copy(held.at[place], held.at[place], sems.at[place]).wait()
    for b in range(per_shard):
        q = q_ref[b * blk:(b + 1) * blk, :]
        total = local[b * blk:(b + 1) * blk, :]
        for j in range(listed):
            i = (b * heads + h) * listed + j
            n = b * listed + j
            w = weights(q, held[place, n, 0], base_ref[i])
            total += jnp.dot(w, held[place, n, 1], preferred_element_type=jnp.float32)
        out_ref[b * blk:(b + 1) * blk, :] = total.astype(out_ref.dtype)


TOTAL = 32768


def attend(chunk, slot, base, offsets, slopes, q, k, v, got, per_shard, listed):
    tokens, width = q.shape
    heads = offsets.shape[0]
    head_size = width // heads
    blk = tokens // per_shard
    column = pl.BlockSpec((tokens, head_size), lambda h: (0, h))
    smem = pl.BlockSpec(memory_space=pltpu.SMEM)
    return pl.pallas_call(
        lambda *refs: attend_kernel(per_shard, listed, head_size ** (-0.5), *refs),
        grid=(heads,),
        out_shape=jax.ShapeDtypeStruct((tokens, width), jnp.bfloat16),
        in_specs=[smem] * 5 + [column] * 3 + [pl.BlockSpec(memory_space=pl.ANY)] * len(got),
        out_specs=column,
        scratch_shapes=[
            pltpu.VMEM((AHEAD + 1, per_shard * listed, 2, blk, head_size), jnp.bfloat16),
            pltpu.SemaphoreType.DMA((AHEAD + 1,)),
        ],
        compiler_params=pltpu.CompilerParams(vmem_limit_bytes=32 * 1024 * 1024),
        name="attend",
    )(chunk, slot, base, offsets, slopes, q, k, v, *got)


def per_device(
    residual_in, queries, keys, values, head_offset, head_slope, key_lists, shard_span, out_weight
):
    q, k, v = queries[0], keys[0], values[0]
    offsets, slopes, entries = head_offset[0], head_slope[0], key_lists[0]
    per_shard, heads, listed = entries.shape
    tokens, width = q.shape
    head_size = width // heads
    blk = tokens // per_shard
    rows = per_shard * heads
    items = rows * listed
    slots = 2
    my_z = lax.axis_index("z")
    my_p = lax.axis_index("x") * NY + lax.axis_index("y")

    def blocked(a):
        return a.reshape(per_shard, blk, heads, head_size).transpose(0, 2, 1, 3)

    kv = jnp.stack([blocked(k), blocked(v)], axis=2).reshape(rows, 2, blk, head_size)

    up = [(i, (i + 1) % NZ) for i in range(NZ)]
    down = [(i, (i - 1) % NZ) for i in range(NZ)]
    shards = {0: kv}
    a = b = kv
    for n in (1, 2, 3):
        a, b = lax.ppermute(a, "z", up), lax.ppermute(b, "z", down)
        shards[-n], shards[n] = a, b
    half = rows // 2
    far = (lax.ppermute(a[:half], "z", up), lax.ppermute(b[half:], "z", down))

    mine = entries.reshape(items)
    asked = lax.all_gather(mine, ("x", "y"), axis=0)
    item_ids = jnp.arange(items, dtype=jnp.int32)
    item_head = item_ids // listed % heads

    def ranks(owner):
        earlier = item_ids[:, None] > item_ids[None, :]
        same = owner[..., :, None] == owner[..., None, :]
        return jnp.sum((same & earlier).astype(jnp.int32), axis=-1)

    asked_owner = asked // per_shard
    asked_rank = ranks(asked_owner)
    asked_block = asked % per_shard * heads + item_head

    def selection(dz):
        z = (my_z + dz) % NZ
        here = (asked_owner == z * PLANE + my_p)[:, None, :] & (
            asked_rank[:, None, :] == jnp.arange(slots, dtype=jnp.int32)[None, :, None]
        )
        return jnp.sum(jnp.where(here, asked_block[:, None, :], 0), axis=-1)

    got = []
    for chunk in CHUNKS:
        sel = jnp.stack([selection(dz) for dz in chunk], axis=1)
        if chunk == (4,):
            sent = pack(sel, far, half)
        else:
            sent = pack(sel, [shards[dz] for dz in chunk])
        got.append(lax.all_to_all(sent, ("x", "y"), split_axis=0, concat_axis=0, tiled=True))

    owner = mine // per_shard
    rank = ranks(owner)
    dz = (owner // PLANE - my_z) % NZ
    chunk_of = jnp.minimum(dz, NZ - dz)
    count = jnp.where((dz == 0) | (dz == 4), 1, 2)
    within = jnp.where((dz > 0) & (dz < 4), 1, 0)
    slot_of = (owner % PLANE * count + within) * slots + rank
    own_span = shard_span[my_z * PLANE + my_p]
    query_at = own_span * tokens + item_ids // (heads * listed) * blk
    key_at = shard_span[owner] * tokens + mine % per_shard * blk
    base = query_at - key_at

    weight = lax.all_gather(out_weight[0], ("x", "y"), axis=0, tiled=True)
    weight, _ = lax.optimization_barrier((weight, far))
    weight = lax.all_gather(weight, "z", axis=0, tiled=True)

    attended = attend(
        chunk_of, slot_of, base, offsets, slopes, q, k, v, got, per_shard, listed
    )
    projected = jnp.dot(attended, weight, preferred_element_type=jnp.float32)
    first_out = (residual_in.astype(jnp.float32) + projected).astype(jnp.bfloat16)
    handed = lax.ppermute(first_out, "segment", [(0, 1)])
    latter = (handed.astype(jnp.float32) + projected).astype(jnp.bfloat16)
    return jnp.where(lax.axis_index("segment") == 0, first_out, latter)[None]


def solution(mesh):
    fine = Mesh(mesh.devices.reshape(2, NZ, NX, NY), ("segment",) + SEQ)
    in_specs = (
        P(SEQ, None),
        P("segment", SEQ, None),
        P("segment", SEQ, None),
        P("segment", SEQ, None),
        P("segment", None),
        P("segment", None),
        P("segment", SEQ, None, None),
        P(),
        P("segment", SEQ, None),
    )
    return jax.shard_map(
        per_device, mesh=fine, in_specs=in_specs, out_specs=P("segment", SEQ, None), check_vma=False
    )
```

time: 526 us -> 838 us (1.59)
  Pallas kernels: 0 us -> 566 us
  waiting for transfers between devices: 358 us -> 164 us
  local copies, waits for them, and re-layouts: 56.4 us -> 17.5 us
  other arithmetic: 26 us -> 4.22 us
  matrix products: 26.7 us -> 6.25 us
  blocking collectives: 0 us -> 18.7 us
    pallas_call x0 -> x6, Pallas kernels: none -> 566 us  [the longest x5 540 us: pack(): pl.pallas_call(lambda *refs: pack_kernel(slots, half, *refs), out_shape=j...]
    all_to_all x3 -> x5, waiting for transfers between devices: 349 us -> 40.7 us  [per_device(): lax.all_to_all(sent, ('x', 'y'), split_axis=0, concat_axis=0, tiled=True)]
    ppermute x1 -> x9, waiting for transfers between devices: 7.63 us -> 123 us  [the longest x6 89.9 us: per_device(): a, b = (lax.ppermute(a, 'z', up), lax.ppermute(b, 'z', down))]
    gather x11 -> x1, local copies, waits for them, and re-layouts: 41.8 us -> 1.23 us  [per_device(): key_at = shard_span[owner] * tokens + mine % per_shard * blk]
    dot_general x3 -> x1, matrix products: 26.7 us -> 6.25 us  [per_device(): projected = jnp.dot(attended, weight, preferred_element_type=jnp.float32)]
    all_gather x0 -> x1, blocking collectives: none -> 18.7 us  [per_device(): asked = lax.all_gather(mine, ('x', 'y'), axis=0)]
    ppermute x1 -> x9, starting transfers between devices: 1.28 us -> 14.5 us  [the longest x6 10.5 us: per_device(): a, b = (lax.ppermute(a, 'z', up), lax.ppermute(b, 'z', down))]
    all_to_all x3 -> x5, starting transfers between devices: 42.2 us -> 30.3 us  [per_device(): lax.all_to_all(sent, ('x', 'y'), split_axis=0, concat_axis=0, tiled=True)]
  transfers between devices with their start and end apart: 5 -> 16, of which waited for: 3 -> 7; matrix products, arithmetic and copies ran while one was open for 14% -> 1% of each run, Pallas kernels for 0% -> 68%
where the time goes in v1:
time: 838 us; the launch traced here: 836 us
  Pallas kernels  566 us (68%)
  waiting for transfers between devices  164 us (20%)
  starting transfers between devices  44.8 us (5%)
  blocking collectives  18.7 us (2%)
  local copies, waits for them, and re-layouts  17.5 us (2%)
  between operations  14.6 us (2%)
    pallas_call x5, Pallas kernels, pack(): pl.pallas_call(lambda *refs: pack_kernel(slots, half, *refs), out_shape=j...  540 us
    ppermute x6, waiting for transfers between devices, per_device(): a, b = (lax.ppermute(a, 'z', up), lax.ppermute(b, 'z', down))  89.9 us
    all_to_all x5, waiting for transfers between devices, per_device(): lax.all_to_all(sent, ('x', 'y'), split_axis=0, concat_axis=0, tiled=True)  40.7 us
    all_to_all x5, starting transfers between devices, per_device(): lax.all_to_all(sent, ('x', 'y'), split_axis=0, concat_axis=0, tiled=True)  30.3 us
    pallas_call x1, Pallas kernels, attend(): pl.pallas_call(lambda *refs: attend_kernel(per_shard, listed, head_size *...  26.1 us
    all_gather x1, blocking collectives, per_device(): asked = lax.all_gather(mine, ('x', 'y'), axis=0)  18.7 us
    ppermute x1, waiting for transfers between devices, per_device(): handed = lax.ppermute(first_out, 'segment', [(0, 1)])  16.8 us
  transfers between devices with their start and end apart: 16, of which 7 were waited for; matrix products, arithmetic and copies ran while one was open for 1% of the time, Pallas kernels for 68%

profile of v1, /device:TPU:1, one launch (start us, length us, event | category | flops | bytes accessed | tf_op | source)
XLA Modules:
  0.0 835.9 jit_solution(8533953797636438720)
XLA Ops:
  6.5 1.5 copy.45
  9.1 2.5 collective-permute-start
  11.7 4.0 collective-permute-start.1
  15.7 45.3 %collective-permute-done.refs_1_ = bf16[32,2,128,128]{3,2,1,0:T(8,128)(2,1)S(1)} collective-permute-done((bf16[32,2,128,128]{3,2,1,0:T(8,128)(2,1)S(1)}, bf16[32,2,128,128]{3,2,1,0:T(8,128)(2,1)S(1)}, u32[]{:S(2)}, u32[]{:S(2)}) %collective-permute-start) | collective-permute-done | bytes 2097184 | tf_op jit(solution)/shard_map/ppermute | solution.py:171
  61.0 1.4 copy-done.8
  62.3 1.4 collective-permute-start.3
  63.7 44.5 %collective-permute-done.2.refs_1_ = bf16[32,2,128,128]{3,2,1,0:T(8,128)(2,1)} collective-permute-done((bf16[32,2,128,128]{3,2,1,0:T(8,128)(2,1)S(1)}, bf16[32,2,128,128]{3,2,1,0:T(8,128)(2,1)}, u32[]{:S(2)}, u32[]{:S(2)}) %collective-permute-start.2) | collective-permute-done | bytes 2097184 | tf_op jit(solution)/shard_map/ppermute | solution.py:171
  108.3 2.5 collective-permute-start.5
  111.3 18.7 %all-gather.1 = s32[16,1,128]{2,1,0:T(1,128)S(1)} all-gather(s32[1,1,128]{2,1,0:T(1,128)S(1)} %reshape.192), channel_id=1, replica_groups=mesh['segment'=2,'z'=8,'x'=4,'y'=4] {'x','y'}, dimensions={0}, use_global_device_ids=true | all-gather | bytes 8704 | tf_op jit(solution)/shard_map/all_gather | solution.py:177
  131.7 65.3 %pack_blocks.5 = bf16[32,2,128,128]{3,2,1,0:T(8,128)(2,1)} custom-call(s32[32]{0:T(128)} %reshape_stack.6.refs_0_, bf16[32,2,128,128]{3,2,1,0:T(8,128)(2,1)} %copy-done.7), custom_call_target="tpu_custom_call" | custom-call | tf_op jit(solution)/shard_map/pack_blocks/pallas_call | solution.py:50
  197.1 4.1 all-to-all-start
  201.2 2.3 slice.10
  203.5 2.3 slice.11
  205.8 2.7 collective-permute-start.7
  208.5 15.1 %collective-permute-done.6.refs_1_ = bf16[16,2,128,128]{3,2,1,0:T(8,128)(2,1)} collective-permute-done((bf16[16,2,128,128]{3,2,1,0:T(8,128)(2,1)}, bf16[16,2,128,128]{3,2,1,0:T(8,128)(2,1)}, u32[]{:S(2)}, u32[]{:S(2)}) %collective-permute-start.6) | collective-permute-done | bytes 1048608 | tf_op jit(solution)/shard_map/ppermute | solution.py:174
  223.6 1.3 collective-permute-done.7.refs_2_
  225.7 128.8 %pack_blocks.6 = bf16[64,2,128,128]{3,2,1,0:T(8,128)(2,1)} custom-call(s32[64]{0:T(128)} %reshape.180.refs_0_, bf16[32,2,128,128]{3,2,1,0:T(8,128)(2,1)} %copy-done.8, bf16[32,2,128,128]{3,2,1,0:T(8,128)(2,1)} %copy-done.9), custom_call_target="tpu_custom_call" | custom-call | tf_op jit(solution)/shard_map/pack_blocks/pallas_call | solution.py:50
  354.5 6.4 all-to-all-start.1
  361.7 151.7 %pack_blocks.7 = bf16[64,2,128,128]{3,2,1,0:T(8,128)(2,1)} custom-call(s32[64]{0:T(128)} %reshape.181.refs_0_, bf16[32,2,128,128]{3,2,1,0:T(8,128)(2,1)} %collective-permute-done.2.refs_1_, bf16[32,2,128,128]{3,2,1,0:T(8,128)(2,1)} %collective-permute-done.3.refs_2_), custom_call_target="tpu_custom_call" | custom-call | tf_op jit(solution)/shard_map/pack_blocks/pallas_call | solution.py:50
  513.4 6.4 all-to-all-start.2
  520.5 65.3 %pack_blocks.9 = bf16[32,2,128,128]{3,2,1,0:T(8,128)(2,1)} custom-call(s32[32]{0:T(128)} %reshape_stack.7.refs_0_, bf16[16,2,128,128]{3,2,1,0:T(8,128)(2,1)} %collective-permute-done.6.refs_1_, bf16[16,2,128,128]{3,2,1,0:T(8,128)(2,1)} %collective-permute-done.7.refs_2_), custom_call_target="tpu_custom_call" | custom-call | tf_op jit(solution)/shard_map/pack_blocks/pallas_call | solution.py:50
  585.8 6.7 all-to-all-start.4
  593.2 128.8 %pack_blocks.8 = bf16[64,2,128,128]{3,2,1,0:T(8,128)(2,1)} custom-call(s32[64]{0:T(128)} %reshape.182.refs_0_, bf16[32,2,128,128]{3,2,1,0:T(8,128)(2,1)} %collective-permute-done.4.refs_1_, bf16[32,2,128,128]{3,2,1,0:T(8,128)(2,1)} %collective-permute-done.5.refs_2_), custom_call_target="tpu_custom_call" | custom-call | tf_op jit(solution)/shard_map/pack_blocks/pallas_call | solution.py:50
  722.1 6.7 all-to-all-start.3
  729.1 1.2 gather_fusion
  731.8 40.7 %all-to-all-done.3.refs_11_ = bf16[64,2,128,128]{3,2,1,0:T(8,128)(2,1)} async-done(((bf16[64,2,128,128]{3,2,1,0:T(8,128)(2,1)}), bf16[64,2,128,128]{3,2,1,0:T(8,128)(2,1)}, u32[]{:S(2)}, u32[]{:S(2)}) %all-to-all-start.3) | async-done | bytes 4194336 | tf_op jit(solution)/shard_map/all_to_all | solution.py:204
  772.5 1.2 copy-done.1
  774.9 26.1 %attend.1 = bf16[256,2048]{1,0:T(8,128)(2,1)S(1)} custom-call(s32[128]{0:T(128)S(1)} %subtract_minimum_fusion.refs_0_, s32[128]{0:T(128)S(1)} %get-tuple-element.17.refs_1_, s32[128]{0:T(128)S(1)} %get-tuple-element.26.refs_2_, f32[16]{0:T(128)S(1)} %bitcast.45, f32[16]{0:T(128)S(1)} %bitcast.46, bf16[256,2048]{1,0:T(8,128)(2,1)S(1)} %bitcast.44, ...), custom_call_target="tpu_custom_call" | custom-call | tf_op jit(solution)/shard_map/attend/pallas_call | solution.py:131
  802.0 6.2 add_convert_fusion.1
  808.2 1.3 collective-permute-start.8
  809.5 16.8 %collective-permute-done.8 = bf16[256,2048]{1,0:T(8,128)(2,1)} collective-permute-done((bf16[256,2048]{1,0:T(8,128)(2,1)S(1)}, bf16[256,2048]{1,0:T(8,128)(2,1)}, u32[]{:S(2)}, u32[]{:S(2)}) %collective-permute-start.8) | collective-permute-done | bytes 1048608 | tf_op jit(solution)/shard_map/ppermute | solution.py:227
  826.4 2.7 fusion.1
  (72 shorter events, 9.3 us)
Async XLA Ops:
  6.5 202.0 %all-gather.7.cloned.1.call-start = ((), (), s32[]{:S(2)}) async-start(), calls=%async_computation.6 | async-start | bytes 1114112 | tf_op jit(solution)/shard_map/all_gather | solution.py:218
  6.5 1.8 copy-start
  8.9 102.1 %copy-start.10 = (s32[1,2,16,4]{2,3,1,0:T(4,128)S(1)}, s32[1,2,16,4]{2,3,1,0:T(4,128)}, u32[]{:S(2)}) copy-start(s32[1,2,16,4]{2,3,1,0:T(4,128)} %param.15) | copy-start | bytes 1540
  9.1 122.6 %copy-start.7 = (bf16[32,2,128,128]{3,2,1,0:T(8,128)(2,1)}, bf16[32,2,128,128]{3,2,1,0:T(8,128)(2,1)S(1)}, u32[]{:S(2)}) copy-start(bf16[32,2,128,128]{3,2,1,0:T(8,128)(2,1)S(1)} %pad_maximum_fusion.refs_1_) | copy-start | bytes 6291460
  9.1 51.8 %collective-permute-start = (bf16[32,2,128,128]{3,2,1,0:T(8,128)(2,1)S(1)}, bf16[32,2,128,128]{3,2,1,0:T(8,128)(2,1)S(1)}, u32[]{:S(2)}, u32[]{:S(2)}) collective-permute-start(bf16[32,2,128,128]{3,2,1,0:T(8,128)(2,1)S(1)} %pad_maximum_fusion.refs_1_), channel_id=1, source_target_pairs={{0,16},{16,32},{32,48},{48,64},{64,80},{80,96},{96,112},{112,0},{1... | collective-permute-start | bytes 6291464 | tf_op jit(solution)/shard_map/ppermute | solution.py:171
  11.7 49.3 %collective-permute-start.1 = (bf16[32,2,128,128]{3,2,1,0:T(8,128)(2,1)S(1)}, bf16[32,2,128,128]{3,2,1,0:T(8,128)(2,1)S(1)}, u32[]{:S(2)}, u32[]{:S(2)}) collective-permute-start(bf16[32,2,128,128]{3,2,1,0:T(8,128)(2,1)S(1)} %pad_maximum_fusion.refs_1_), channel_id=1, source_target_pairs={{0,112},{16,0},{32,16},{48,32},{64,48},{80,64},{96,80},{112,96},{1... | collective-permute-start | bytes 6291464 | tf_op jit(solution)/shard_map/ppermute | solution.py:171
  61.0 1.4 copy-start.8
  61.0 47.2 %collective-permute-start.2 = (bf16[32,2,128,128]{3,2,1,0:T(8,128)(2,1)S(1)}, bf16[32,2,128,128]{3,2,1,0:T(8,128)(2,1)}, u32[]{:S(2)}, u32[]{:S(2)}) collective-permute-start(bf16[32,2,128,128]{3,2,1,0:T(8,128)(2,1)S(1)} %collective-permute-done.refs_1_), channel_id=1, source_target_pairs={{0,16},{16,32},{32,48},{48,64},{64,80},{80,96},{96,112},{112,0},{1... | collective-permute-start | bytes 6291464 | tf_op jit(solution)/shard_map/ppermute | solution.py:171
  62.3 45.8 %copy-start.9 = (bf16[32,2,128,128]{3,2,1,0:T(8,128)(2,1)}, bf16[32,2,128,128]{3,2,1,0:T(8,128)(2,1)S(1)}, u32[]{:S(2)}) copy-start(bf16[32,2,128,128]{3,2,1,0:T(8,128)(2,1)S(1)} %collective-permute-done.1.refs_2_) | copy-start | bytes 6291460
  62.3 46.0 %collective-permute-start.3 = (bf16[32,2,128,128]{3,2,1,0:T(8,128)(2,1)S(1)}, bf16[32,2,128,128]{3,2,1,0:T(8,128)(2,1)}, u32[]{:S(2)}, u32[]{:S(2)}) collective-permute-start(bf16[32,2,128,128]{3,2,1,0:T(8,128)(2,1)S(1)} %collective-permute-done.1.refs_2_), channel_id=1, source_target_pairs={{0,112},{16,0},{32,16},{48,32},{64,48},{80,64},{96,80},{112,96},{1... | collective-permute-start | bytes 6291464 | tf_op jit(solution)/shard_map/ppermute | solution.py:171
  108.2 93.0 %collective-permute-start.4 = (bf16[32,2,128,128]{3,2,1,0:T(8,128)(2,1)}, bf16[32,2,128,128]{3,2,1,0:T(8,128)(2,1)}, u32[]{:S(2)}, u32[]{:S(2)}) collective-permute-start(bf16[32,2,128,128]{3,2,1,0:T(8,128)(2,1)} %collective-permute-done.2.refs_1_), channel_id=1, source_target_pairs={{0,16},{16,32},{32,48},{48,64},{64,80},{80,96},{96,112},{112,0},{1... | collective-permute-start | bytes 6291464 | tf_op jit(solution)/shard_map/ppermute | solution.py:171
  108.3 95.2 %collective-permute-start.5 = (bf16[32,2,128,128]{3,2,1,0:T(8,128)(2,1)}, bf16[32,2,128,128]{3,2,1,0:T(8,128)(2,1)}, u32[]{:S(2)}, u32[]{:S(2)}) collective-permute-start(bf16[32,2,128,128]{3,2,1,0:T(8,128)(2,1)} %collective-permute-done.3.refs_2_), channel_id=1, source_target_pairs={{0,112},{16,0},{32,16},{48,32},{64,48},{80,64},{96,80},{112,96},{1... | collective-permute-start | bytes 6291464 | tf_op jit(solution)/shard_map/ppermute | solution.py:171
  197.1 157.4 %all-to-all-start = ((bf16[32,2,128,128]{3,2,1,0:T(8,128)(2,1)}), bf16[32,2,128,128]{3,2,1,0:T(8,128)(2,1)S(1)}, u32[]{:S(2)}, u32[]{:S(2)}) async-start(bf16[32,2,128,128]{3,2,1,0:T(8,128)(2,1)} %pack_blocks.5), calls=%async_computation | async-start | bytes 4194304 | tf_op jit(solution)/shard_map/all_to_all | solution.py:204
  201.1 600.9 %all-gather.5.cloned.1.call-start = ((), (), s32[]{:S(2)}) async-start(), calls=%async_computation.5 | async-start | bytes 9437184 | tf_op jit(solution)/shard_map/all_gather | solution.py:220
  203.5 20.1 %collective-permute-start.6 = (bf16[16,2,128,128]{3,2,1,0:T(8,128)(2,1)}, bf16[16,2,128,128]{3,2,1,0:T(8,128)(2,1)}, u32[]{:S(2)}, u32[]{:S(2)}) collective-permute-start(bf16[16,2,128,128]{3,2,1,0:T(8,128)(2,1)} %slice.10), channel_id=1, source_target_pairs={{0,16},{16,32},{32,48},{48,64},{64,80},{80,96},{96,112},{112,0},{1... | collective-permute-start | bytes 3145736 | tf_op jit(solution)/shard_map/ppermute | solution.py:174
  205.8 19.1 %collective-permute-start.7 = (bf16[16,2,128,128]{3,2,1,0:T(8,128)(2,1)}, bf16[16,2,128,128]{3,2,1,0:T(8,128)(2,1)}, u32[]{:S(2)}, u32[]{:S(2)}) collective-permute-start(bf16[16,2,128,128]{3,2,1,0:T(8,128)(2,1)} %slice.11), channel_id=1, source_target_pairs={{0,112},{16,0},{32,16},{48,32},{64,48},{80,64},{96,80},{112,96},{1... | collective-permute-start | bytes 3145736 | tf_op jit(solution)/shard_map/ppermute | solution.py:174
  354.5 158.9 %all-to-all-start.1 = ((bf16[64,2,128,128]{3,2,1,0:T(8,128)(2,1)}), bf16[64,2,128,128]{3,2,1,0:T(8,128)(2,1)}, u32[]{:S(2)}, u32[]{:S(2)}) async-start(bf16[64,2,128,128]{3,2,1,0:T(8,128)(2,1)} %pack_blocks.6), calls=%async_computation.1 | async-start | bytes 8388608 | tf_op jit(solution)/shard_map/all_to_all | solution.py:204
  513.4 72.4 %all-to-all-start.2 = ((bf16[64,2,128,128]{3,2,1,0:T(8,128)(2,1)}), bf16[64,2,128,128]{3,2,1,0:T(8,128)(2,1)}, u32[]{:S(2)}, u32[]{:S(2)}) async-start(bf16[64,2,128,128]{3,2,1,0:T(8,128)(2,1)} %pack_blocks.7), calls=%async_computation.2 | async-start | bytes 8388608 | tf_op jit(solution)/shard_map/all_to_all | solution.py:204
  585.8 136.3 %all-to-all-start.4 = ((bf16[32,2,128,128]{3,2,1,0:T(8,128)(2,1)}), bf16[32,2,128,128]{3,2,1,0:T(8,128)(2,1)}, u32[]{:S(2)}, u32[]{:S(2)}) async-start(bf16[32,2,128,128]{3,2,1,0:T(8,128)(2,1)} %pack_blocks.9), calls=%async_computation.4 | async-start | bytes 4194304 | tf_op jit(solution)/shard_map/all_to_all | solution.py:204
  722.1 7.0 copy-start.6
  722.1 50.4 %copy-start.4 = (f32[1,16]{1,0:T(1,128)S(1)}, f32[1,16]{1,0:T(1,128)}, u32[]{:S(2)}) copy-start(f32[1,16]{1,0:T(1,128)} %param.13) | copy-start | bytes 196
  722.1 50.3 %copy-start.5 = (f32[1,16]{1,0:T(1,128)S(1)}, f32[1,16]{1,0:T(1,128)}, u32[]{:S(2)}) copy-start(f32[1,16]{1,0:T(1,128)} %param.14) | copy-start | bytes 196
  722.1 50.3 %all-to-all-start.3 = ((bf16[64,2,128,128]{3,2,1,0:T(8,128)(2,1)}), bf16[64,2,128,128]{3,2,1,0:T(8,128)(2,1)}, u32[]{:S(2)}, u32[]{:S(2)}) async-start(bf16[64,2,128,128]{3,2,1,0:T(8,128)(2,1)} %pack_blocks.8), calls=%async_computation.3 | async-start | bytes 8388608 | tf_op jit(solution)/shard_map/all_to_all | solution.py:204
  772.5 1.2 copy-start.1
  773.7 1.2 copy-start.2
  801.0 1.0 copy-start.3
  808.2 18.1 %collective-permute-start.8 = (bf16[256,2048]{1,0:T(8,128)(2,1)S(1)}, bf16[256,2048]{1,0:T(8,128)(2,1)}, u32[]{:S(2)}, u32[]{:S(2)}) collective-permute-start(bf16[256,2048]{1,0:T(8,128)(2,1)S(1)} %get-tuple-element.28), channel_id=1, source_target_pairs={{0,128},{1,129},{2,130},{3,131},{4,132},{5,133},{6,134},{7,135},{8... | collective-permute-start | bytes 3145736 | tf_op jit(solution)/shard_map/ppermute | solution.py:227
Sparse Core Ops, SparseCore 0:
  111.0 48.0 all-gather.6
  225.0 161.4 all-gather.4

commit v2 on v1

v2 whole, which is shorter than its diff:
```python
import jax
import jax.numpy as jnp
from jax import lax
from jax.experimental import pallas as pl
from jax.experimental.pallas import tpu as pltpu
from jax.sharding import Mesh, PartitionSpec as P

NZ, NX, NY = 8, 4, 4
PLANE = NX * NY
SEQ = ("z", "x", "y")
CHUNKS = ((0,), (-1, 1), (-2, 2), (-3, 3), (4,))
ORDER = sum(CHUNKS, ())


def pack_kernel(slots, half, sel_ref, *refs):
    sources, out_ref, sem = refs[:-2], refs[-2], refs[-1]

    def copy(source, idx, i):
        pltpu.make_async_copy(source.at[idx], out_ref.at[i], sem).start()

    @pl.loop(0, out_ref.shape[0] // (slots * (1 if half else len(sources))))
    def _(p):
        if half:
            low, high = sources
            for s in range(slots):
                i = p * slots + s
                idx = sel_ref[i]

                @pl.when(idx < half)
                def _(idx=idx, i=i):
                    copy(low, idx, i)

                @pl.when(idx >= half)
                def _(idx=idx, i=i):
                    copy(high, idx - half, i)
        else:
            for n, source in enumerate(sources):
                for s in range(slots):
                    i = (p * len(sources) + n) * slots + s
                    copy(source, sel_ref[i], i)

    pltpu.make_async_copy(out_ref, out_ref, sem).wait()


def pack(sel, sources, half=0):
    slots = sel.shape[-1]
    total = sel.size
    block = sources[0].shape[1:]
    moved = 2 * total * block[0] * block[1] * block[2] * 2
    return pl.pallas_call(
        lambda *refs: pack_kernel(slots, half, *refs),
        out_shape=jax.ShapeDtypeStruct((total,) + block, sources[0].dtype),
        in_specs=[pl.BlockSpec(memory_space=pltpu.SMEM)]
        + [pl.BlockSpec(memory_space=pltpu.VMEM)] * len(sources),
        out_specs=pl.BlockSpec(memory_space=pl.ANY),
        scratch_shapes=[pltpu.SemaphoreType.DMA],
        compiler_params=pltpu.CompilerParams(vmem_limit_bytes=24 * 1024 * 1024),
        cost_estimate=pl.CostEstimate(flops=0, bytes_accessed=moved, transcendentals=0),
        name="pack_blocks",
    )(sel.reshape(total), *sources)


LOG2E = 1.4426950408889634


def local_kernel(scale, offset_ref, slope_ref, q_ref, k_ref, v_ref, out_ref):
    h = pl.program_id(0)
    raw = lax.dot_general(
        q_ref[...], k_ref[...], (((1,), (1,)), ((), ())), preferred_element_type=jnp.float32
    )
    rows = lax.broadcasted_iota(jnp.int32, raw.shape, 0)
    cols = lax.broadcasted_iota(jnp.int32, raw.shape, 1)
    distance = jnp.abs(rows - cols).astype(jnp.float32)
    power = raw * (-scale * LOG2E) + (distance * slope_ref[h] - offset_ref[h])
    w = (1.0 / (1.0 + jnp.exp2(power))).astype(jnp.bfloat16)
    out_ref[...] = jnp.dot(w, v_ref[...], preferred_element_type=jnp.float32)


def local_part(offsets, slopes, q, k, v, heads):
    tokens, width = q.shape
    head_size = width // heads
    column = pl.BlockSpec((tokens, head_size), lambda h: (0, h))
    smem = pl.BlockSpec(memory_space=pltpu.SMEM)
    return pl.pallas_call(
        lambda *refs: local_kernel(head_size ** (-0.5), *refs),
        grid=(heads,),
        out_shape=jax.ShapeDtypeStruct((tokens, width), jnp.float32),
        in_specs=[smem] * 2 + [column] * 3,
        out_specs=column,
        cost_estimate=pl.CostEstimate(
            flops=4 * tokens * tokens * width, bytes_accessed=10 * tokens * width,
            transcendentals=2 * heads * tokens * tokens,
        ),
        name="local_part",
    )(offsets, slopes, q, k, v)


GROUP = 4


def listed_kernel(
    scale, heads, listed, item_ref, near_ref, far_ref, q_ref, got_ref, acc_ref, out_ref, total
):
    step = pl.program_id(0)
    blk, head_size = got_ref.shape[2:]

    @pl.when(step == 0)
    def _():
        total[...] = acc_ref[...]

    found = [item_ref[step * GROUP + n] for n in range(GROUP)]
    some = found[0]
    for item in found[1:]:
        some = some + item

    @pl.when(some > 0)
    def _():
        rows = lax.broadcasted_iota(jnp.int32, (blk, blk), 0)
        cols = lax.broadcasted_iota(jnp.int32, (blk, blk), 1)
        apart = (rows - cols).astype(jnp.float32)
        parts = []
        for n, item in enumerate(found):
            i = jnp.maximum(item - 1, 0)
            row, head = i // (heads * listed), lax.rem(i // listed, heads)
            at = (
                pl.ds(pl.multiple_of(row * blk, blk), blk),
                pl.ds(pl.multiple_of(head * head_size, head_size), head_size),
            )
            raw = lax.dot_general(
                q_ref[at], got_ref[n, 0], (((1,), (1,)), ((), ())),
                preferred_element_type=jnp.float32,
            )
            power = raw * (-scale * LOG2E) + (apart * far_ref[i] + near_ref[i])
            w = (1.0 / (1.0 + jnp.exp2(power))).astype(jnp.bfloat16)
            parts.append((item, at, jnp.dot(w, got_ref[n, 1], preferred_element_type=jnp.float32)))
        for item, at, part in parts:

            @pl.when(item > 0)
            def _(at=at, part=part):
                total[at] += part

    @pl.when(step == pl.num_programs(0) - 1)
    def _():
        out_ref[...] = total[...].astype(out_ref.dtype)


def listed_part(found, near, far, q, got, acc, heads, listed, dtype):
    slots = got.shape[0]
    tokens, width = q.shape
    blk, head_size = got.shape[2:]
    smem = pl.BlockSpec(memory_space=pltpu.SMEM)
    whole = pl.BlockSpec((tokens, width), lambda n: (0, 0))
    return pl.pallas_call(
        lambda *refs: listed_kernel(head_size ** (-0.5), heads, listed, *refs),
        grid=(slots // GROUP,),
        out_shape=jax.ShapeDtypeStruct((tokens, width), dtype),
        in_specs=[smem] * 3
        + [whole, pl.BlockSpec((GROUP,) + got.shape[1:], lambda n: (n, 0, 0, 0)), whole],
        out_specs=whole,
        scratch_shapes=[pltpu.VMEM((tokens, width), jnp.float32)],
        compiler_params=pltpu.CompilerParams(vmem_limit_bytes=32 * 1024 * 1024),
        cost_estimate=pl.CostEstimate(
            flops=4 * slots * blk * blk * head_size, bytes_accessed=got.size * 2 + 10 * q.size,
            transcendentals=2 * slots * blk * blk,
        ),
        name="listed_part",
    )(found, near, far, q, got, acc)


def ring_steps(block, axis):
    size = lax.axis_size(axis)
    up = [(i, (i + 1) % size) for i in range(size)]
    down = [(i, (i - 1) % size) for i in range(size)]
    held = {0: block}
    a = b = block
    for n in range(1, size // 2):
        a, b = lax.ppermute(a, axis, up), lax.ppermute(b, axis, down)
        held[-n], held[n] = a, b
    half = block.shape[0] // 2
    held[size // 2] = jnp.concatenate(
        [lax.ppermute(a[:half], axis, up), lax.ppermute(b[half:], axis, down)]
    )
    return held


def ring_gather(block, axis):
    size = lax.axis_size(axis)
    at = lax.axis_index(axis)
    out = jnp.zeros((size,) + block.shape, block.dtype)
    for n, part in ring_steps(block, axis).items():
        out = lax.dynamic_update_index_in_dim(out, part, (at + n) % size, 0)
    return out.reshape((size * block.shape[0],) + block.shape[1:])


def after(x, *others):
    return lax.optimization_barrier((x, others))[0]


def per_device(
    residual_in, queries, keys, values, head_offset, head_slope, key_lists, shard_span, out_weight
):
    q, k, v = queries[0], keys[0], values[0]
    offsets, slopes, entries = head_offset[0], head_slope[0], key_lists[0]
    per_shard, heads, listed = entries.shape
    tokens, width = q.shape
    head_size = width // heads
    blk = tokens // per_shard
    rows = per_shard * heads
    items = rows * listed
    slots = 2
    my_z = lax.axis_index("z")
    my_p = lax.axis_index("x") * NY + lax.axis_index("y")

    def blocked(a):
        return a.reshape(per_shard, blk, heads, head_size).transpose(0, 2, 1, 3)

    kv = jnp.stack([blocked(k), blocked(v)], axis=2).reshape(rows, 2, blk, head_size)

    mine = entries.reshape(items)
    asked = lax.all_gather(mine, ("x", "y"), axis=0)
    item_ids = jnp.arange(items, dtype=jnp.int32)
    item_head = item_ids // listed % heads

    def ranks(owner):
        earlier = item_ids[:, None] > item_ids[None, :]
        same = owner[..., :, None] == owner[..., None, :]
        return jnp.sum((same & earlier).astype(jnp.int32), axis=-1)

    asked_owner = asked // per_shard
    asked_rank = ranks(asked_owner)
    asked_block = asked % per_shard * heads + item_head

    zs = (my_z + jnp.array(ORDER, jnp.int32)) % NZ
    slot_ids = jnp.arange(slots, dtype=jnp.int32)
    here = (asked_owner[:, None, None, :] == (zs * PLANE + my_p)[None, :, None, None]) & (
        asked_rank[:, None, None, :] == slot_ids[None, None, :, None]
    )
    selected = jnp.sum(jnp.where(here, asked_block[:, None, None, :], 0), axis=-1)

    owner = mine // per_shard
    rank = ranks(owner)
    own_span = shard_span[my_z * PLANE + my_p]
    query_at = own_span * tokens + item_ids // (heads * listed) * blk
    key_at = shard_span[owner] * tokens + mine % per_shard * blk
    base = (query_at - key_at).astype(jnp.float32)
    slope = slopes * (LOG2E / (tokens * NZ * PLANE))
    offset = offsets * LOG2E
    def by_item(a):
        return jnp.broadcast_to(a[None, :, None], (per_shard, heads, listed)).reshape(items)

    far_item = jnp.where(base > 0, 1.0, -1.0) * by_item(slope)
    near_item = far_item * base - by_item(offset)
    here = (
        (owner // PLANE == zs[None, :, None, None])
        & (owner % PLANE == jnp.arange(PLANE, dtype=jnp.int32)[:, None, None, None])
        & (rank == slot_ids[None, None, :, None])
    )
    found = jnp.sum(jnp.where(here, item_ids + 1, 0), axis=-1)
    selected, found, near_item, far_item = lax.optimization_barrier(
        (selected, found, near_item, far_item)
    )

    def part_of(table, n):
        first = sum(len(chunk) for chunk in CHUNKS[:n])
        return table[:, first:first + len(CHUNKS[n])]

    up = [(i, (i + 1) % NZ) for i in range(NZ)]
    down = [(i, (i - 1) % NZ) for i in range(NZ)]
    half = rows // 2

    def served(sent):
        return lax.all_to_all(sent, ("x", "y"), split_axis=0, concat_axis=0, tiled=True)

    def chosen(n, *sources, cut=0):
        return pack(part_of(selected, n), sources, cut)

    def added(n, got, acc, dtype=jnp.float32):
        slot_items = part_of(found, n).reshape(-1)
        return listed_part(
            slot_items, near_item, far_item, q, got, acc, heads, listed, dtype
        )

    def step(pair):
        return lax.ppermute(pair[0], "z", up), lax.ppermute(pair[1], "z", down)

    ring = step((kv, kv))
    got = served(chosen(0, kv))
    weight = ring_gather(ring_gather(out_weight[0], "y"), "x")
    acc = local_part(offset, slope, q, k, v, heads)
    ring = after(ring, got, acc, weight)
    for n in (1, 2, 3):
        later = step(ring) if n < 3 else step((ring[0][:half], ring[1][half:]))
        sent = after(chosen(n, *ring), got)
        acc = added(n - 1, got, after(acc, sent))
        got = served(sent)
        ring = after(later, acc)
    whole_weight = lax.all_gather(after(weight, ring), "z", axis=0, tiled=True)
    sent = after(chosen(4, *ring, cut=half), got)
    acc = added(3, got, after(acc, sent))
    attended = added(4, served(sent), acc, jnp.bfloat16)

    first, latter = [], []
    cut = width // 2
    for n in range(2):
        columns = slice(n * cut, (n + 1) * cut)
        projected = jnp.dot(attended, whole_weight[:, columns], preferred_element_type=jnp.float32)
        first.append((residual_in[:, columns].astype(jnp.float32) + projected).astype(jnp.bfloat16))
        handed = lax.ppermute(first[-1], "segment", [(0, 1)])
        latter.append((handed.astype(jnp.float32) + projected).astype(jnp.bfloat16))
    first, latter = jnp.concatenate(first, axis=1), jnp.concatenate(latter, axis=1)
    return jnp.where(lax.axis_index("segment") == 0, first, latter)[None]


def solution(mesh):
    fine = Mesh(mesh.devices.reshape(2, NZ, NX, NY), ("segment",) + SEQ)
    in_specs = (
        P(SEQ, None),
        P("segment", SEQ, None),
        P("segment", SEQ, None),
        P("segment", SEQ, None),
        P("segment", None),
        P("segment", None),
        P("segment", SEQ, None, None),
        P(),
        P("segment", SEQ, None),
    )
    return jax.shard_map(
        per_device, mesh=fine, in_specs=in_specs, out_specs=P("segment", SEQ, None), check_vma=False
    )
```

time: 838 us -> 387 us (0.46)
  Pallas kernels: 566 us -> 106 us
  waiting for transfers between devices: 164 us -> 120 us
  starting transfers between devices: 44.8 us -> 79.5 us
  local copies, waits for them, and re-layouts: 17.5 us -> 32.5 us
    pallas_call x5, Pallas kernels: 540 us -> 32.1 us  [pack(): pl.pallas_call(lambda *refs: pack_kernel(slots, half, *refs), out_shape=j...]
    ppermute x9 -> x18, waiting for transfers between devices: 123 us -> 71.4 us  [the longest x8 56.4 us: step(): return (lax.ppermute(pair[0], 'z', up), lax.ppermute(pair[1], 'z', down))]
    pallas_call x1 -> x6, Pallas kernels: 26.1 us -> 74 us  [the longest x5 62 us: listed_part(): pl.pallas_call(lambda *refs: listed_kernel(head_size ** (-0.5), heads, li...]
    ppermute x9 -> x18, starting transfers between devices: 14.5 us -> 45.9 us  [the longest x4 23.9 us: ring_steps(): a, b = (lax.ppermute(a, axis, up), lax.ppermute(b, axis, down))]
    unnamed x26 -> x46, local copies, waits for them, and re-layouts: 6.77 us -> 17.8 us
  transfers between devices with their start and end apart: 16 -> 24, of which waited for: 7 -> 11; matrix products, arithmetic and copies ran while one was open for 1% -> 5% of each run, Pallas kernels for 68% -> 26%
where the time goes in v2:
time: 387 us; the launch traced here: 385 us
  waiting for transfers between devices  120 us (31%)
  Pallas kernels  106 us (27%)
  starting transfers between devices  79.5 us (21%)
  local copies, waits for them, and re-layouts  32.5 us (8%)
  blocking collectives  18.6 us (5%)
  between operations  14.9 us (4%)
  matrix products  7.06 us (2%)
  other arithmetic  6.22 us (2%)
    pallas_call x5, Pallas kernels, listed_part(): pl.pallas_call(lambda *refs: listed_kernel(head_size ** (-0.5), heads, li...  62 us
    ppermute x8, waiting for transfers between devices, step(): return (lax.ppermute(pair[0], 'z', up), lax.ppermute(pair[1], 'z', down))  56.4 us
    all_to_all x5, waiting for transfers between devices, served(): lax.all_to_all(sent, ('x', 'y'), split_axis=0, concat_axis=0, tiled=True)  40.2 us
    all_to_all x5, starting transfers between devices, served(): lax.all_to_all(sent, ('x', 'y'), split_axis=0, concat_axis=0, tiled=True)  33.6 us
    pallas_call x5, Pallas kernels, pack(): pl.pallas_call(lambda *refs: pack_kernel(slots, half, *refs), out_shape=j...  32.1 us
    ppermute x4, starting transfers between devices, ring_steps(): a, b = (lax.ppermute(a, axis, up), lax.ppermute(b, axis, down))  23.9 us
    all_gather x1, blocking collectives, per_device(): asked = lax.all_gather(mine, ('x', 'y'), axis=0)  18.6 us
    unnamed x46, local copies, waits for them, and re-layouts  17.8 us
  transfers between devices with their start and end apart: 24, of which 11 were waited for; matrix products, arithmetic and copies ran while one was open for 5% of the time, Pallas kernels for 26%

profile of v2, /device:TPU:1, one launch (start us, length us, event | category | flops | bytes accessed | tf_op | source)
XLA Modules:
  0.0 384.9 jit_solution(6292942350858849087)
XLA Ops:
  6.5 3.6 collective-permute-start.3
  12.7 5.7 %collective-permute-start.1 = (bf16[32,2,128,128]{3,2,1,0:T(8,128)(2,1)S(1)}, bf16[32,2,128,128]{3,2,1,0:T(8,128)(2,1)}, u32[]{:S(2)}, u32[]{:S(2)}) collective-permute-start(bf16[32,2,128,128]{3,2,1,0:T(8,128)(2,1)S(1)} %pad_maximum_fusion.refs_1_), channel_id=1, source_target_pairs={{0,112},{16,0},{32,16},{48,32},{64,48},{80,64},{96,80},{112,96},{1... | collective-permute-start | bytes 6291464 | tf_op jit(solution)/shard_map/ppermute | solution.py:284
  21.0 18.6 %all-gather = s32[16,1,128]{2,1,0:T(1,128)S(1)} all-gather(s32[1,1,128]{2,1,0:T(1,128)S(1)} %reshape.457), channel_id=1, replica_groups=mesh['segment'=2,'z'=8,'x'=4,'y'=4] {'x','y'}, dimensions={0}, use_global_device_ids=true | all-gather | bytes 8704 | tf_op jit(solution)/shard_map/all_gather | solution.py:220
  43.6 3.5 pack_blocks.5
  48.4 4.6 %all-to-all-start = ((bf16[32,2,128,128]{3,2,1,0:T(8,128)(2,1)}), bf16[32,2,128,128]{3,2,1,0:T(8,128)(2,1)}, u32[]{:S(2)}, u32[]{:S(2)}) async-start(bf16[32,2,128,128]{3,2,1,0:T(8,128)(2,1)} %copy-done.8), calls=%async_computation | async-start | bytes 4194304 | tf_op jit(solution)/shard_map/all_to_all | solution.py:272
  56.2 2.7 collective-permute-done.5
  60.5 20.3 %collective-permute-start.7 = (bf16[64,2048]{1,0:T(8,128)(2,1)S(1)}, bf16[64,2048]{1,0:T(8,128)(2,1)S(1)}, u32[]{:S(2)}, u32[]{:S(2)}) collective-permute-start(bf16[64,2048]{1,0:T(8,128)(2,1)S(1)} %bitcast.75), channel_id=1, source_target_pairs={{0,12},{4,0},{8,4},{12,8},{1,13},{5,1},{9,5},{13,9},{2,14},{6,2},{... | collective-permute-start | bytes 786440 | tf_op jit(solution)/shard_map/ppermute | solution.py:177
  80.9 12.0 %local_part.1.refs_5_ = f32[256,2048]{1,0:T(8,128)} custom-call(f32[16]{0:T(128)} %copy-done.14, f32[16]{0:T(128)} %copy-done.15, bf16[256,2048]{1,0:T(8,128)(2,1)} %bitcast.61, bf16[256,2048]{1,0:T(8,128)(2,1)} %bitcast.71, bf16[256,2048]{1,0:T(8,128)(2,1)} %bitcast.70), custom_call_target="tpu_custom_call" | custom-call | flops 536870912 | bytes 5242880 | tf_op jit(solution)/shard_map/local_part/pallas_call | solution.py:84
  94.7 2.9 collective-permute-start.9
  99.6 3.2 collective-permute-done.8
  103.5 8.0 %pack_blocks.6 = bf16[64,2,128,128]{3,2,1,0:T(8,128)(2,1)S(1)} custom-call(s32[64]{0:T(128)S(1)} %reshape.443.refs_0_, bf16[32,2,128,128]{3,2,1,0:T(8,128)(2,1)} %collective-permute-done.refs_1_, bf16[32,2,128,128]{3,2,1,0:T(8,128)(2,1)} %collective-permute-done.1.refs_2_), custom_call_target="tpu_custom_call" | custom-call | bytes 8388608 | tf_op jit(solution)/shard_map/pack_blocks/pallas_call | solution.py:50
  113.5 4.7 %all-to-all-start.1 = ((bf16[64,2,128,128]{3,2,1,0:T(8,128)(2,1)}), bf16[64,2,128,128]{3,2,1,0:T(8,128)(2,1)}, u32[]{:S(2)}, u32[]{:S(2)}) async-start(bf16[64,2,128,128]{3,2,1,0:T(8,128)(2,1)} %copy-done.3), calls=%async_computation.1 | async-start | bytes 8388608 | tf_op jit(solution)/shard_map/all_to_all | solution.py:272
  118.2 3.0 collective-permute-start.11
  123.9 8.4 %listed_part.5.refs_5_ = f32[256,2048]{1,0:T(8,128)S(1)} custom-call(s32[32]{0:T(128)S(1)} %reshape.442.refs_0_, f32[128]{0:T(128)S(1)} %multiply_subtract_fusion.refs_1_, f32[128]{0:T(128)S(1)} %get-tuple-element.28.refs_2_, bf16[256,2048]{1,0:T(8,128)(2,1)S(1)} %bitcast.62, bf16[32,2,128,128]{3,2,1,0:T(8,128)(2,1)} %all-to-all-done.refs_4_, ...), custom_call_target="tpu_custom_call" | custom-call | flops 268435456 | bytes 7340032 | tf_op jit(solution)/shard_map/listed_part/pallas_call | solution.py:153
  132.3 31.0 %collective-permute-done.10.refs_1_ = bf16[32,2,128,128]{3,2,1,0:T(8,128)(2,1)} collective-permute-done((bf16[32,2,128,128]{3,2,1,0:T(8,128)(2,1)}, bf16[32,2,128,128]{3,2,1,0:T(8,128)(2,1)}, u32[]{:S(2)}, u32[]{:S(2)}) %collective-permute-start.10) | collective-permute-done | bytes 2097184 | tf_op jit(solution)/shard_map/ppermute | solution.py:284
  163.3 8.0 %pack_blocks.7 = bf16[64,2,128,128]{3,2,1,0:T(8,128)(2,1)S(1)} custom-call(s32[64]{0:T(128)S(1)} %reshape.445.refs_0_, bf16[32,2,128,128]{3,2,1,0:T(8,128)(2,1)} %collective-permute-done.10.refs_1_, bf16[32,2,128,128]{3,2,1,0:T(8,128)(2,1)} %collective-permute-done.11.refs_2_), custom_call_target="tpu_custom_call" | custom-call | bytes 8388608 | tf_op jit(solution)/shard_map/pack_blocks/pallas_call | solution.py:50
  173.3 6.2 %all-to-all-start.2 = ((bf16[64,2,128,128]{3,2,1,0:T(8,128)(2,1)}), bf16[64,2,128,128]{3,2,1,0:T(8,128)(2,1)}, u32[]{:S(2)}, u32[]{:S(2)}) async-start(bf16[64,2,128,128]{3,2,1,0:T(8,128)(2,1)} %copy-done.1), calls=%async_computation.2 | async-start | bytes 8388608 | tf_op jit(solution)/shard_map/all_to_all | solution.py:272
  179.7 2.7 collective-permute-start.13
  182.8 14.8 %listed_part.6.refs_5_ = f32[256,2048]{1,0:T(8,128)S(1)} custom-call(s32[64]{0:T(128)S(1)} %reshape.444.refs_0_, f32[128]{0:T(128)S(1)} %multiply_subtract_fusion.refs_1_, f32[128]{0:T(128)S(1)} %get-tuple-element.28.refs_2_, bf16[256,2048]{1,0:T(8,128)(2,1)S(1)} %bitcast.63, bf16[64,2,128,128]{3,2,1,0:T(8,128)(2,1)} %all-to-all-done.1.refs_4_, ...), custom_call_target="tpu_custom_call" | custom-call | flops 536870912 | bytes 9437184 | tf_op jit(solution)/shard_map/listed_part/pallas_call | solution.py:153
  197.6 25.4 %collective-permute-done.12.refs_1_ = bf16[32,2,128,128]{3,2,1,0:T(8,128)(2,1)} collective-permute-done((bf16[32,2,128,128]{3,2,1,0:T(8,128)(2,1)}, bf16[32,2,128,128]{3,2,1,0:T(8,128)(2,1)}, u32[]{:S(2)}, u32[]{:S(2)}) %collective-permute-start.12) | collective-permute-done | bytes 2097184 | tf_op jit(solution)/shard_map/ppermute | solution.py:284
  230.7 8.0 %pack_blocks.8 = bf16[64,2,128,128]{3,2,1,0:T(8,128)(2,1)S(1)} custom-call(s32[64]{0:T(128)S(1)} %reshape.447.refs_0_, bf16[32,2,128,128]{3,2,1,0:T(8,128)(2,1)} %collective-permute-done.12.refs_1_, bf16[32,2,128,128]{3,2,1,0:T(8,128)(2,1)} %collective-permute-done.13.refs_2_), custom_call_target="tpu_custom_call" | custom-call | bytes 8388608 | tf_op jit(solution)/shard_map/pack_blocks/pallas_call | solution.py:50
  242.2 15.6 %listed_part.7.refs_5_ = f32[256,2048]{1,0:T(8,128)S(1)} custom-call(s32[64]{0:T(128)S(1)} %reshape.446.refs_0_, f32[128]{0:T(128)S(1)} %multiply_subtract_fusion.refs_1_, f32[128]{0:T(128)S(1)} %get-tuple-element.28.refs_2_, bf16[256,2048]{1,0:T(8,128)(2,1)S(1)} %bitcast.64, bf16[64,2,128,128]{3,2,1,0:T(8,128)(2,1)} %all-to-all-done.2.refs_4_, ...), custom_call_target="tpu_custom_call" | custom-call | flops 536870912 | bytes 9437184 | tf_op jit(solution)/shard_map/listed_part/pallas_call | solution.py:153
  257.9 6.4 %all-to-all-start.3 = ((bf16[64,2,128,128]{3,2,1,0:T(8,128)(2,1)}), bf16[64,2,128,128]{3,2,1,0:T(8,128)(2,1)}, u32[]{:S(2)}, u32[]{:S(2)}) async-start(bf16[64,2,128,128]{3,2,1,0:T(8,128)(2,1)} %copy-done.2), calls=%async_computation.3 | async-start | bytes 8388608 | tf_op jit(solution)/shard_map/all_to_all | solution.py:272
  264.3 4.7 %pack_blocks.9 = bf16[32,2,128,128]{3,2,1,0:T(8,128)(2,1)S(1)} custom-call(s32[32]{0:T(128)S(1)} %reshape.438.refs_0_, bf16[16,2,128,128]{3,2,1,0:T(8,128)(2,1)} %collective-permute-done.14.refs_1_, bf16[16,2,128,128]{3,2,1,0:T(8,128)(2,1)} %collective-permute-done.15.refs_2_), custom_call_target="tpu_custom_call" | custom-call | bytes 4194304 | tf_op jit(solution)/shard_map/pack_blocks/pallas_call | solution.py:50
  270.4 38.5 %all-to-all-done.3.refs_4_ = bf16[64,2,128,128]{3,2,1,0:T(8,128)(2,1)} async-done(((bf16[64,2,128,128]{3,2,1,0:T(8,128)(2,1)}), bf16[64,2,128,128]{3,2,1,0:T(8,128)(2,1)}, u32[]{:S(2)}, u32[]{:S(2)}) %all-to-all-start.3) | async-done | bytes 4194336 | tf_op jit(solution)/shard_map/all_to_all | solution.py:272
  308.9 11.7 %all-to-all-start.4 = ((bf16[32,2,128,128]{3,2,1,0:T(8,128)(2,1)}), bf16[32,2,128,128]{3,2,1,0:T(8,128)(2,1)}, u32[]{:S(2)}, u32[]{:S(2)}) async-start(bf16[32,2,128,128]{3,2,1,0:T(8,128)(2,1)} %copy-done.9), calls=%async_computation.4 | async-start | bytes 4194304 | tf_op jit(solution)/shard_map/all_to_all | solution.py:272
  321.0 14.8 %listed_part.8.refs_5_ = f32[256,2048]{1,0:T(8,128)S(1)} custom-call(s32[64]{0:T(128)S(1)} %reshape.448.refs_0_, f32[128]{0:T(128)S(1)} %multiply_subtract_fusion.refs_1_, f32[128]{0:T(128)S(1)} %get-tuple-element.28.refs_2_, bf16[256,2048]{1,0:T(8,128)(2,1)S(1)} %bitcast.65, bf16[64,2,128,128]{3,2,1,0:T(8,128)(2,1)} %all-to-all-done.3.refs_4_, ...), custom_call_target="tpu_custom_call" | custom-call | flops 536870912 | bytes 9437184 | tf_op jit(solution)/shard_map/listed_part/pallas_call | solution.py:153
  340.6 8.4 %listed_part.9 = bf16[256,2048]{1,0:T(8,128)(2,1)S(1)} custom-call(s32[32]{0:T(128)S(1)} %reshape.437.refs_0_, f32[128]{0:T(128)S(1)} %multiply_subtract_fusion.refs_1_, f32[128]{0:T(128)S(1)} %get-tuple-element.28.refs_2_, bf16[256,2048]{1,0:T(8,128)(2,1)S(1)} %bitcast.66, bf16[32,2,128,128]{3,2,1,0:T(8,128)(2,1)} %all-to-all-done.4.refs_4_, ...), custom_call_target="tpu_custom_call" | custom-call | flops 268435456 | bytes 7340032 | tf_op jit(solution)/shard_map/listed_part/pallas_call | solution.py:153
  349.0 8.3 %all-gather.3.cloned.1.call-done = bf16[2048,2048]{1,0:T(8,128)(2,1)} async-done(((bf16[256,2048]{1,0:T(8,128)(2,1)}), bf16[2048,2048]{1,0:T(8,128)(2,1)}) %all-gather.3.cloned.1.call-update) | async-done | bytes 8388624 | tf_op jit(solution)/shard_map/all_gather | solution.py:297
  357.3 3.6 fusion
  362.0 3.5 add_convert_fusion.3
  368.0 5.9 %collective-permute-done.17 = bf16[256,1024]{1,0:T(8,128)(2,1)S(1)} collective-permute-done((bf16[256,1024]{1,0:T(8,128)(2,1)}, bf16[256,1024]{1,0:T(8,128)(2,1)S(1)}, u32[]{:S(2)}, u32[]{:S(2)}) %collective-permute-start.17) | collective-permute-done | bytes 524320 | tf_op jit(solution)/shard_map/ppermute | solution.py:308
  (148 shorter events, 51.5 us)
Async XLA Ops:
  6.5 47.1 %collective-permute-start.3 = (bf16[16,2048]{1,0:T(8,128)(2,1)}, bf16[16,2048]{1,0:T(8,128)(2,1)S(1)}, u32[]{:S(2)}, u32[]{:S(2)}) collective-permute-start(bf16[16,2048]{1,0:T(8,128)(2,1)} %bitcast.78), channel_id=1, source_target_pairs={{0,3},{1,0},{2,1},{3,2},{4,7},{5,4},{6,5},{7,6},{8,11},{9,8},{10,9... | collective-permute-start | bytes 196616 | tf_op jit(solution)/shard_map/ppermute | solution.py:177
  10.1 46.0 %collective-permute-start.2 = (bf16[16,2048]{1,0:T(8,128)(2,1)}, bf16[16,2048]{1,0:T(8,128)(2,1)S(1)}, u32[]{:S(2)}, u32[]{:S(2)}) collective-permute-start(bf16[16,2048]{1,0:T(8,128)(2,1)} %bitcast.79), channel_id=1, source_target_pairs={{0,1},{1,2},{2,3},{3,0},{4,5},{5,6},{6,7},{7,4},{8,9},{9,10},{10,1... | collective-permute-start | bytes 196616 | tf_op jit(solution)/shard_map/ppermute | solution.py:177
  12.5 6.6 %copy-start.17 = (s32[8]{0:T(128)S(1)}, s32[8]{0:T(128)}, u32[]{:S(2)}) copy-start(s32[8]{0:T(128)} %constant.212.clone) | copy-start | bytes 100
  12.5 6.7 %copy-start.11 = (s32[128]{0:T(128)S(1)}, s32[128]{0:T(128)}, u32[]{:S(2)}) copy-start(s32[128]{0:T(128)} %param.17) | copy-start | bytes 1540
  12.5 27.1 %copy-start.18 = (f32[1,16]{1,0:T(1,128)S(1)}, f32[1,16]{1,0:T(1,128)}, u32[]{:S(2)}) copy-start(f32[1,16]{1,0:T(1,128)} %param.14) | copy-start | bytes 196
  12.5 27.1 %copy-start.19 = (f32[1,16]{1,0:T(1,128)S(1)}, f32[1,16]{1,0:T(1,128)}, u32[]{:S(2)}) copy-start(f32[1,16]{1,0:T(1,128)} %param.15) | copy-start | bytes 196
  12.7 90.7 %collective-permute-start.1 = (bf16[32,2,128,128]{3,2,1,0:T(8,128)(2,1)S(1)}, bf16[32,2,128,128]{3,2,1,0:T(8,128)(2,1)}, u32[]{:S(2)}, u32[]{:S(2)}) collective-permute-start(bf16[32,2,128,128]{3,2,1,0:T(8,128)(2,1)S(1)} %pad_maximum_fusion.refs_1_), channel_id=1, source_target_pairs={{0,112},{16,0},{32,16},{48,32},{64,48},{80,64},{96,80},{112,96},{1... | collective-permute-start | bytes 6291464 | tf_op jit(solution)/shard_map/ppermute | solution.py:284
  18.4 85.1 %collective-permute-start = (bf16[32,2,128,128]{3,2,1,0:T(8,128)(2,1)S(1)}, bf16[32,2,128,128]{3,2,1,0:T(8,128)(2,1)}, u32[]{:S(2)}, u32[]{:S(2)}) collective-permute-start(bf16[32,2,128,128]{3,2,1,0:T(8,128)(2,1)S(1)} %pad_maximum_fusion.refs_1_), channel_id=1, source_target_pairs={{0,16},{16,32},{32,48},{48,64},{64,80},{80,96},{96,112},{112,0},{1... | collective-permute-start | bytes 6291464 | tf_op jit(solution)/shard_map/ppermute | solution.py:284
  39.6 7.4 %copy-start.14 = (f32[16]{0:T(128)}, f32[16]{0:T(128)S(1)}, u32[]{:S(2)}) copy-start(f32[16]{0:T(128)S(1)} %get-tuple-element.69.refs_0_) | copy-start | bytes 196
  39.6 7.4 %copy-start.15 = (f32[16]{0:T(128)}, f32[16]{0:T(128)S(1)}, u32[]{:S(2)}) copy-start(f32[16]{0:T(128)S(1)} %get-tuple-element.70.refs_1_) | copy-start | bytes 196
  48.4 55.1 %all-to-all-start = ((bf16[32,2,128,128]{3,2,1,0:T(8,128)(2,1)}), bf16[32,2,128,128]{3,2,1,0:T(8,128)(2,1)}, u32[]{:S(2)}, u32[]{:S(2)}) async-start(bf16[32,2,128,128]{3,2,1,0:T(8,128)(2,1)} %copy-done.8), calls=%async_computation | async-start | bytes 4194304 | tf_op jit(solution)/shard_map/all_to_all | solution.py:272
  53.7 5.2 %collective-permute-start.5 = (bf16[8,2048]{1,0:T(8,128)(2,1)S(1)}, bf16[8,2048]{1,0:T(8,128)(2,1)S(1)}, u32[]{:S(2)}, u32[]{:S(2)}) collective-permute-start(bf16[8,2048]{1,0:T(8,128)(2,1)S(1)} %slice.83), channel_id=1, source_target_pairs={{0,3},{1,0},{2,1},{3,2},{4,7},{5,4},{6,5},{7,6},{8,11},{9,8},{10,9... | collective-permute-start | bytes 98312 | tf_op jit(solution)/shard_map/ppermute | solution.py:181
  56.1 4.4 %collective-permute-start.4 = (bf16[8,2048]{1,0:T(8,128)(2,1)S(1)}, bf16[8,2048]{1,0:T(8,128)(2,1)S(1)}, u32[]{:S(2)}, u32[]{:S(2)}) collective-permute-start(bf16[8,2048]{1,0:T(8,128)(2,1)S(1)} %slice.82), channel_id=1, source_target_pairs={{0,1},{1,2},{2,3},{3,0},{4,5},{5,6},{6,7},{7,4},{8,9},{9,10},{10,1... | collective-permute-start | bytes 98312 | tf_op jit(solution)/shard_map/ppermute | solution.py:181
  60.5 34.1 %collective-permute-start.7 = (bf16[64,2048]{1,0:T(8,128)(2,1)S(1)}, bf16[64,2048]{1,0:T(8,128)(2,1)S(1)}, u32[]{:S(2)}, u32[]{:S(2)}) collective-permute-start(bf16[64,2048]{1,0:T(8,128)(2,1)S(1)} %bitcast.75), channel_id=1, source_target_pairs={{0,12},{4,0},{8,4},{12,8},{1,13},{5,1},{9,5},{13,9},{2,14},{6,2},{... | collective-permute-start | bytes 786440 | tf_op jit(solution)/shard_map/ppermute | solution.py:177
  80.9 16.8 %collective-permute-start.6 = (bf16[64,2048]{1,0:T(8,128)(2,1)S(1)}, bf16[64,2048]{1,0:T(8,128)(2,1)S(1)}, u32[]{:S(2)}, u32[]{:S(2)}) collective-permute-start(bf16[64,2048]{1,0:T(8,128)(2,1)S(1)} %bitcast.76), channel_id=1, source_target_pairs={{0,4},{4,8},{8,12},{12,0},{1,5},{5,9},{9,13},{13,1},{2,6},{6,10},{... | collective-permute-start | bytes 786440 | tf_op jit(solution)/shard_map/ppermute | solution.py:177
  94.7 4.9 %collective-permute-start.9 = (bf16[32,2048]{1,0:T(8,128)(2,1)S(1)}, bf16[32,2048]{1,0:T(8,128)(2,1)S(1)}, u32[]{:S(2)}, u32[]{:S(2)}) collective-permute-start(bf16[32,2048]{1,0:T(8,128)(2,1)S(1)} %slice.85), channel_id=1, source_target_pairs={{0,12},{4,0},{8,4},{12,8},{1,13},{5,1},{9,5},{13,9},{2,14},{6,2},{... | collective-permute-start | bytes 393224 | tf_op jit(solution)/shard_map/ppermute | solution.py:181
  97.6 5.1 %collective-permute-start.8 = (bf16[32,2048]{1,0:T(8,128)(2,1)S(1)}, bf16[32,2048]{1,0:T(8,128)(2,1)S(1)}, u32[]{:S(2)}, u32[]{:S(2)}) collective-permute-start(bf16[32,2048]{1,0:T(8,128)(2,1)S(1)} %slice.84), channel_id=1, source_target_pairs={{0,4},{4,8},{8,12},{12,0},{1,5},{5,9},{9,13},{13,1},{2,6},{6,10},{... | collective-permute-start | bytes 393224 | tf_op jit(solution)/shard_map/ppermute | solution.py:181
  113.5 8.9 %copy-start = (bf16[1,256,2048]{2,1,0:T(8,128)(2,1)S(1)}, bf16[1,256,2048]{2,1,0:T(8,128)(2,1)}, u32[]{:S(2)}) copy-start(bf16[1,256,2048]{2,1,0:T(8,128)(2,1)} %param.11) | copy-start | bytes 3145732
  113.5 59.8 %all-to-all-start.1 = ((bf16[64,2,128,128]{3,2,1,0:T(8,128)(2,1)}), bf16[64,2,128,128]{3,2,1,0:T(8,128)(2,1)}, u32[]{:S(2)}, u32[]{:S(2)}) async-start(bf16[64,2,128,128]{3,2,1,0:T(8,128)(2,1)} %copy-done.3), calls=%async_computation.1 | async-start | bytes 8388608 | tf_op jit(solution)/shard_map/all_to_all | solution.py:272
  118.1 45.2 %collective-permute-start.10 = (bf16[32,2,128,128]{3,2,1,0:T(8,128)(2,1)}, bf16[32,2,128,128]{3,2,1,0:T(8,128)(2,1)}, u32[]{:S(2)}, u32[]{:S(2)}) collective-permute-start(bf16[32,2,128,128]{3,2,1,0:T(8,128)(2,1)} %collective-permute-done.refs_1_), channel_id=1, source_target_pairs={{0,16},{16,32},{32,48},{48,64},{64,80},{80,96},{96,112},{112,0},{1... | collective-permute-start | bytes 6291464 | tf_op jit(solution)/shard_map/ppermute | solution.py:284
  118.2 45.1 %collective-permute-start.11 = (bf16[32,2,128,128]{3,2,1,0:T(8,128)(2,1)}, bf16[32,2,128,128]{3,2,1,0:T(8,128)(2,1)}, u32[]{:S(2)}, u32[]{:S(2)}) collective-permute-start(bf16[32,2,128,128]{3,2,1,0:T(8,128)(2,1)} %collective-permute-done.1.refs_2_), channel_id=1, source_target_pairs={{0,112},{16,0},{32,16},{48,32},{64,48},{80,64},{96,80},{112,96},{1... | collective-permute-start | bytes 6291464 | tf_op jit(solution)/shard_map/ppermute | solution.py:284
  173.3 67.3 %all-to-all-start.2 = ((bf16[64,2,128,128]{3,2,1,0:T(8,128)(2,1)}), bf16[64,2,128,128]{3,2,1,0:T(8,128)(2,1)}, u32[]{:S(2)}, u32[]{:S(2)}) async-start(bf16[64,2,128,128]{3,2,1,0:T(8,128)(2,1)} %copy-done.1), calls=%async_computation.2 | async-start | bytes 8388608 | tf_op jit(solution)/shard_map/all_to_all | solution.py:272
  179.6 177.8 %all-gather.3.cloned.1.call-start = ((), (), s32[]{:S(2)}) async-start(), calls=%async_computation.5 | async-start | bytes 9437184 | tf_op jit(solution)/shard_map/all_gather | solution.py:297
  179.6 43.4 %collective-permute-start.12 = (bf16[32,2,128,128]{3,2,1,0:T(8,128)(2,1)}, bf16[32,2,128,128]{3,2,1,0:T(8,128)(2,1)}, u32[]{:S(2)}, u32[]{:S(2)}) collective-permute-start(bf16[32,2,128,128]{3,2,1,0:T(8,128)(2,1)} %collective-permute-done.10.refs_1_), channel_id=1, source_target_pairs={{0,16},{16,32},{32,48},{48,64},{64,80},{80,96},{96,112},{112,0},{1... | collective-permute-start | bytes 6291464 | tf_op jit(solution)/shard_map/ppermute | solution.py:284
  179.7 43.3 %collective-permute-start.13 = (bf16[32,2,128,128]{3,2,1,0:T(8,128)(2,1)}, bf16[32,2,128,128]{3,2,1,0:T(8,128)(2,1)}, u32[]{:S(2)}, u32[]{:S(2)}) collective-permute-start(bf16[32,2,128,128]{3,2,1,0:T(8,128)(2,1)} %collective-permute-done.11.refs_2_), channel_id=1, source_target_pairs={{0,112},{16,0},{32,16},{48,32},{64,48},{80,64},{96,80},{112,96},{1... | collective-permute-start | bytes 6291464 | tf_op jit(solution)/shard_map/ppermute | solution.py:284
  197.6 30.0 %copy-start.4 = (f32[256,2048]{1,0:T(8,128)}, f32[256,2048]{1,0:T(8,128)S(1)}, u32[]{:S(2)}) copy-start(f32[256,2048]{1,0:T(8,128)S(1)} %listed_part.6.refs_5_) | copy-start | bytes 6291460
  227.7 30.2 %collective-permute-start.15 = (bf16[16,2,128,128]{3,2,1,0:T(8,128)(2,1)}, bf16[16,2,128,128]{3,2,1,0:T(8,128)(2,1)}, u32[]{:S(2)}, u32[]{:S(2)}) collective-permute-start(bf16[16,2,128,128]{3,2,1,0:T(8,128)(2,1)} %slice.73), channel_id=1, source_target_pairs={{0,112},{16,0},{32,16},{48,32},{64,48},{80,64},{96,80},{112,96},{1... | collective-permute-start | bytes 3145736 | tf_op jit(solution)/shard_map/ppermute | solution.py:284
  230.0 27.8 %collective-permute-start.14 = (bf16[16,2,128,128]{3,2,1,0:T(8,128)(2,1)}, bf16[16,2,128,128]{3,2,1,0:T(8,128)(2,1)}, u32[]{:S(2)}, u32[]{:S(2)}) collective-permute-start(bf16[16,2,128,128]{3,2,1,0:T(8,128)(2,1)} %slice.72), channel_id=1, source_target_pairs={{0,16},{16,32},{32,48},{48,64},{64,80},{80,96},{96,112},{112,0},{1... | collective-permute-start | bytes 3145736 | tf_op jit(solution)/shard_map/ppermute | solution.py:284
  257.9 51.0 %all-to-all-start.3 = ((bf16[64,2,128,128]{3,2,1,0:T(8,128)(2,1)}), bf16[64,2,128,128]{3,2,1,0:T(8,128)(2,1)}, u32[]{:S(2)}, u32[]{:S(2)}) async-start(bf16[64,2,128,128]{3,2,1,0:T(8,128)(2,1)} %copy-done.2), calls=%async_computation.3 | async-start | bytes 8388608 | tf_op jit(solution)/shard_map/all_to_all | solution.py:272
  308.9 30.2 %all-to-all-start.4 = ((bf16[32,2,128,128]{3,2,1,0:T(8,128)(2,1)}), bf16[32,2,128,128]{3,2,1,0:T(8,128)(2,1)}, u32[]{:S(2)}, u32[]{:S(2)}) async-start(bf16[32,2,128,128]{3,2,1,0:T(8,128)(2,1)} %copy-done.9), calls=%async_computation.4 | async-start | bytes 4194304 | tf_op jit(solution)/shard_map/all_to_all | solution.py:272
  365.5 8.5 %collective-permute-start.17 = (bf16[256,1024]{1,0:T(8,128)(2,1)}, bf16[256,1024]{1,0:T(8,128)(2,1)S(1)}, u32[]{:S(2)}, u32[]{:S(2)}) collective-permute-start(bf16[256,1024]{1,0:T(8,128)(2,1)} %get-tuple-element.58), channel_id=1, source_target_pairs={{0,128},{1,129},{2,130},{3,131},{4,132},{5,133},{6,134},{7,135},{8... | collective-permute-start | bytes 1572872 | tf_op jit(solution)/shard_map/ppermute | solution.py:308
  366.7 8.6 %collective-permute-start.16 = (bf16[256,1024]{1,0:T(8,128)(2,1)}, bf16[256,1024]{1,0:T(8,128)(2,1)S(1)}, u32[]{:S(2)}, u32[]{:S(2)}) collective-permute-start(bf16[256,1024]{1,0:T(8,128)(2,1)} %get-tuple-element.57), channel_id=1, source_target_pairs={{0,128},{1,129},{2,130},{3,131},{4,132},{5,133},{6,134},{7,135},{8... | collective-permute-start | bytes 1572872 | tf_op jit(solution)/shard_map/ppermute | solution.py:308
  (13 other events, 32.0 us)
Sparse Core Ops, SparseCore 0:
  258.0 99.2 all-gather.2

commit v3 on v2

v3 whole, which is shorter than its diff:
```python
import jax
import jax.numpy as jnp
from jax import lax
from jax.experimental import pallas as pl
from jax.experimental.pallas import tpu as pltpu
from jax.sharding import Mesh, PartitionSpec as P

NZ, NX, NY = 8, 4, 4
PLANE = NX * NY
SEQ = ("z", "x", "y")
CHUNKS = ((0,), (-1, 1), (-2, 2), (-3, 3), (4,))
ORDER = sum(CHUNKS, ())
LIGHT = pl.CostEstimate(flops=1, bytes_accessed=1, transcendentals=0)
HEAVY = pl.CostEstimate(flops=50_000_000_000, bytes_accessed=150_000_000, transcendentals=0)


def pack_kernel(slots, half, extra, sel_ref, *refs):
    sources, out_ref, sem = refs[:-2], refs[-2], refs[-1]
    if extra:
        sources, extra_ref = sources[:-1], sources[-1]
    shards = 1 if half else len(sources)
    per_place = shards * slots + extra

    def copy(source, i):
        pltpu.make_async_copy(source, out_ref.at[i], sem).start()

    @pl.loop(0, PLANE)
    def _(p):
        for n in range(shards):
            for s in range(slots):
                i = p * per_place + n * slots + s
                idx = sel_ref[(p * shards + n) * slots + s]
                if half:

                    @pl.when(idx < half)
                    def _(idx=idx, i=i):
                        copy(sources[0].at[idx], i)

                    @pl.when(idx >= half)
                    def _(idx=idx, i=i):
                        copy(sources[1].at[idx - half], i)
                else:
                    copy(sources[n].at[idx], i)
        if extra:
            copy(extra_ref, p * per_place + per_place - 1)

    pltpu.make_async_copy(out_ref, out_ref, sem).wait()


def pack(sel, sources, half=0, extra=None):
    slots = sel.shape[-1]
    block = sources[0].shape[1:]
    extras = [] if extra is None else [extra]
    total = sel.size + PLANE * len(extras)
    return pl.pallas_call(
        lambda *refs: pack_kernel(slots, half, len(extras), *refs),
        out_shape=jax.ShapeDtypeStruct((total,) + block, sources[0].dtype),
        in_specs=[pl.BlockSpec(memory_space=pltpu.SMEM)]
        + [pl.BlockSpec(memory_space=pltpu.VMEM)] * (len(sources) + len(extras)),
        out_specs=pl.BlockSpec(memory_space=pl.ANY),
        scratch_shapes=[pltpu.SemaphoreType.DMA],
        compiler_params=pltpu.CompilerParams(vmem_limit_bytes=24 * 1024 * 1024),
        cost_estimate=HEAVY,
        name="pack_blocks",
    )(sel.reshape(sel.size), *sources, *extras)


LOG2E = 1.4426950408889634


def local_kernel(scale, offset_ref, slope_ref, q_ref, k_ref, v_ref, out_ref):
    h = pl.program_id(0)
    raw = lax.dot_general(
        q_ref[...], k_ref[...], (((1,), (1,)), ((), ())), preferred_element_type=jnp.float32
    )
    rows = lax.broadcasted_iota(jnp.int32, raw.shape, 0)
    cols = lax.broadcasted_iota(jnp.int32, raw.shape, 1)
    distance = jnp.abs(rows - cols).astype(jnp.float32)
    power = raw * (-scale * LOG2E) + (distance * slope_ref[h] - offset_ref[h])
    w = (1.0 / (1.0 + jnp.exp2(power))).astype(jnp.bfloat16)
    out_ref[...] = jnp.dot(w, v_ref[...], preferred_element_type=jnp.float32)


def local_part(offsets, slopes, q, k, v, heads):
    tokens, width = q.shape
    head_size = width // heads
    column = pl.BlockSpec((tokens, head_size), lambda h: (0, h))
    smem = pl.BlockSpec(memory_space=pltpu.SMEM)
    return pl.pallas_call(
        lambda *refs: local_kernel(head_size ** (-0.5), *refs),
        grid=(heads,),
        out_shape=jax.ShapeDtypeStruct((tokens, width), jnp.float32),
        in_specs=[smem] * 2 + [column] * 3,
        out_specs=column,
        cost_estimate=LIGHT,
        name="local_part",
    )(offsets, slopes, q, k, v)


GROUP = 8


def listed_kernel(
    scale, heads, listed, order_ref, bound_ref, slot_ref, near_ref, far_ref, q_ref, got_ref,
    acc_ref, out_ref, total
):
    blk, head_size = got_ref.shape[2:]
    items = order_ref.shape[0]
    begin, end = bound_ref[0], bound_ref[1]
    total[...] = acc_ref[...]

    @pl.loop(0, (end - begin + GROUP - 1) // GROUP)
    def _(group):
        rows = lax.broadcasted_iota(jnp.int32, (blk, blk), 0)
        cols = lax.broadcasted_iota(jnp.int32, (blk, blk), 1)
        apart = (rows - cols).astype(jnp.float32)
        parts = []
        for n in range(GROUP):
            at_order = begin + group * GROUP + n
            i = order_ref[jnp.minimum(at_order, items - 1)]
            slot = jnp.minimum(slot_ref[i], got_ref.shape[0] - 1)
            row, head = i // (heads * listed), lax.rem(i // listed, heads)
            at = (
                pl.ds(pl.multiple_of(row * blk, blk), blk),
                pl.ds(pl.multiple_of(head * head_size, head_size), head_size),
            )
            raw = lax.dot_general(
                q_ref[at], got_ref[slot, 0], (((1,), (1,)), ((), ())),
                preferred_element_type=jnp.float32,
            )
            power = raw * (-scale * LOG2E) + (apart * far_ref[i] + near_ref[i])
            w = (1.0 / (1.0 + jnp.exp2(power))).astype(jnp.bfloat16)
            part = jnp.dot(w, got_ref[slot, 1], preferred_element_type=jnp.float32)
            parts.append((at_order, at, part))
        for at_order, at, part in parts:

            @pl.when(at_order < end)
            def _(at=at, part=part):
                total[at] += part

    out_ref[...] = total[...].astype(out_ref.dtype)


def listed_part(order, bounds, slot, near, far, q, got, acc, heads, listed, dtype):
    tokens, width = q.shape
    smem = pl.BlockSpec(memory_space=pltpu.SMEM)
    vmem = pl.BlockSpec(memory_space=pltpu.VMEM)
    return pl.pallas_call(
        lambda *refs: listed_kernel((width // heads) ** (-0.5), heads, listed, *refs),
        out_shape=jax.ShapeDtypeStruct((tokens, width), dtype),
        in_specs=[smem] * 5 + [vmem] * 3,
        out_specs=vmem,
        scratch_shapes=[pltpu.VMEM((tokens, width), jnp.float32)],
        compiler_params=pltpu.CompilerParams(vmem_limit_bytes=32 * 1024 * 1024),
        cost_estimate=LIGHT,
        name="listed_part",
    )(order, bounds, slot, near, far, q, got, acc)


def after(x, *others):
    return lax.optimization_barrier((x, others))[0]


def per_device(
    residual_in, queries, keys, values, head_offset, head_slope, key_lists, shard_span, out_weight
):
    q, k, v = queries[0], keys[0], values[0]
    offsets, slopes, entries = head_offset[0], head_slope[0], key_lists[0]
    per_shard, heads, listed = entries.shape
    tokens, width = q.shape
    head_size = width // heads
    blk = tokens // per_shard
    rows = per_shard * heads
    items = rows * listed
    slots = 2
    my_z = lax.axis_index("z")
    my_p = lax.axis_index("x") * NY + lax.axis_index("y")

    def blocked(a):
        return a.reshape(per_shard, blk, heads, head_size).transpose(0, 2, 1, 3)

    kv = jnp.stack([blocked(k), blocked(v)], axis=2).reshape(rows, 2, blk, head_size)

    mine = after(entries, kv).reshape(items)
    item_ids = jnp.arange(items, dtype=jnp.int32)
    owner = mine // per_shard
    earlier = item_ids[:, None] > item_ids[None, :]
    rank = jnp.sum((earlier & (owner[:, None] == owner[None, :])).astype(jnp.int32), axis=-1)
    zs = (my_z + jnp.array(ORDER, jnp.int32)) % NZ
    slot_ids = jnp.arange(slots, dtype=jnp.int32)
    here = (
        (owner // PLANE == zs[None, :, None, None])
        & (owner % PLANE == jnp.arange(PLANE, dtype=jnp.int32)[:, None, None, None])
        & (rank == slot_ids[None, None, :, None])
    )
    block_ids = mine % per_shard * heads + item_ids // listed % heads
    wanted = jnp.sum(jnp.where(here, block_ids, 0), axis=-1)
    selected = lax.all_to_all(wanted, ("x", "y"), split_axis=0, concat_axis=0, tiled=True)

    own_span = shard_span[my_z * PLANE + my_p]
    query_at = own_span * tokens + item_ids // (heads * listed) * blk
    key_at = shard_span[owner] * tokens + mine % per_shard * blk
    base = (query_at - key_at).astype(jnp.float32)
    slope = slopes * (LOG2E / (tokens * NZ * PLANE))
    offset = offsets * LOG2E
    def by_item(a):
        return jnp.broadcast_to(a[None, :, None], (per_shard, heads, listed)).reshape(items)

    far_item = jnp.where(base > 0, 1.0, -1.0) * by_item(slope)
    near_item = far_item * base - by_item(offset)
    dz = (owner // PLANE - my_z) % NZ
    chunk = jnp.minimum(dz, NZ - dz)
    pair = (chunk > 0) & (chunk < len(CHUNKS) - 1)
    shard = jnp.where(pair, owner % PLANE * 2 + (dz < NZ // 2), owner % PLANE)
    slot = shard * jnp.where(chunk == 0, slots + 1, slots) + rank
    ahead = (chunk[:, None] < chunk[None, :]) | (
        (chunk[:, None] == chunk[None, :]) & (item_ids[:, None] < item_ids[None, :])
    )
    turn = jnp.sum(ahead.astype(jnp.int32), axis=0)
    order = jnp.sum(jnp.where(turn[:, None] == item_ids[None, :], item_ids[:, None], 0), axis=0)
    edges = jnp.arange(len(CHUNKS) + 1, dtype=jnp.int32)
    edges = jnp.sum((chunk[None, :] < edges[:, None]).astype(jnp.int32), axis=1)

    def part_of(table, n):
        first = sum(len(chunk) for chunk in CHUNKS[:n])
        return table[:, first:first + len(CHUNKS[n])]

    up = [(i, (i + 1) % NZ) for i in range(NZ)]
    down = [(i, (i - 1) % NZ) for i in range(NZ)]
    half = rows // 2

    def served(sent):
        return lax.all_to_all(sent, ("x", "y"), split_axis=0, concat_axis=0, tiled=True)

    def chosen(n, *sources, cut=0, extra=None):
        return pack(part_of(selected, n), sources, cut, extra)

    def added(n, got, acc, dtype=jnp.float32):
        bounds = edges[n:n + 2]
        return listed_part(
            order, bounds, slot, near_item, far_item, q, got, acc, heads, listed, dtype
        )

    def step(pair):
        return lax.ppermute(pair[0], "z", up), lax.ppermute(pair[1], "z", down)

    ring = step((kv, kv))
    packed = chosen(0, kv, extra=out_weight.reshape(kv.shape[1:]))
    got = served(packed)
    acc = local_part(offset, slope, q, k, v, heads)
    ring = after(ring, packed, acc)
    for n in (1, 2, 3):
        later = step(ring) if n < 3 else step((ring[0][:half], ring[1][half:]))
        packed = chosen(n, *ring)
        if n > 1:
            acc = added(n - 2, before, after(acc, packed))
        else:
            weight = got.reshape((PLANE, slots + 1) + kv.shape[1:])[:, slots]
            weight = weight.reshape(-1, width)
        if n == 3:
            later = after(later, acc)
            packed = after(packed, later)
        before, sent = got, after(packed, got)
        got = served(sent)
        ring = after(later, sent, acc)
    weight = lax.all_gather(after(weight, ring), "z", axis=0, tiled=True)
    packed = chosen(4, *ring, cut=half)
    acc = added(2, before, after(acc, packed))
    sent = after(packed, got, acc)
    acc = added(3, got, after(acc, sent))
    attended = added(4, served(sent), acc, jnp.bfloat16)

    first, latter = [], []
    cut = width // 2
    for n in range(2):
        columns = slice(n * cut, (n + 1) * cut)
        if n:
            attended = after(attended, first[-1])
        projected = jnp.dot(attended, weight[:, columns], preferred_element_type=jnp.float32)
        first.append((residual_in[:, columns].astype(jnp.float32) + projected).astype(jnp.bfloat16))
        handed = lax.ppermute(first[-1], "segment", [(0, 1)])
        latter.append((handed.astype(jnp.float32) + projected).astype(jnp.bfloat16))
    first, latter = jnp.concatenate(first, axis=1), jnp.concatenate(latter, axis=1)
    return jnp.where(lax.axis_index("segment") == 0, first, latter)[None]


def solution(mesh):
    fine = Mesh(mesh.devices.reshape(2, NZ, NX, NY), ("segment",) + SEQ)
    in_specs = (
        P(SEQ, None),
        P("segment", SEQ, None),
        P("segment", SEQ, None),
        P("segment", SEQ, None),
        P("segment", None),
        P("segment", None),
        P("segment", SEQ, None, None),
        P(),
        P("segment", SEQ, None),
    )
    return jax.shard_map(
        per_device, mesh=fine, in_specs=in_specs, out_specs=P("segment", SEQ, None), check_vma=False
    )
```

time: 387 us -> 334 us (0.86)
  Pallas kernels: 106 us -> 83 us
  blocking collectives: 18.6 us -> 0 us
  starting transfers between devices: 79.5 us -> 63.7 us
  waiting for transfers between devices: 120 us -> 124 us
    all_to_all x5, waiting for transfers between devices: 40.2 us -> 105 us  [served(): lax.all_to_all(sent, ('x', 'y'), split_axis=0, concat_axis=0, tiled=True)]
    ppermute x8, waiting for transfers between devices: 56.4 us -> 10.9 us  [step(): return (lax.ppermute(pair[0], 'z', up), lax.ppermute(pair[1], 'z', down))]
    ppermute x8 -> x0, starting transfers between devices: 29.4 us -> none  [the longest x4 23.9 us: ring_steps(): a, b = (lax.ppermute(a, axis, up), lax.ppermute(b, axis, down))]
    pallas_call x10, Pallas kernels: 94.1 us -> 71 us  [the longest x5 37.3 us: listed_part(): pl.pallas_call(lambda *refs: listed_kernel((width // heads) ** (-0.5), he...]
    all_gather x1 -> x0, blocking collectives: 18.6 us -> none  [per_device(): asked = lax.all_gather(mine, ('x', 'y'), axis=0)]
    ppermute x8 -> x0, waiting for transfers between devices: 7.92 us -> none  [the longest x2 4.81 us: ring_steps(): lax.ppermute(a[:half], axis, up)]
    all_gather x1, waiting for transfers between devices: 8.32 us -> 1.24 us  [per_device(): weight = lax.all_gather(after(weight, ring), 'z', axis=0, tiled=True)]
    all_to_all x0 -> x1, starting transfers between devices: none -> 6.75 us  [per_device(): lax.all_to_all(wanted, ('x', 'y'), split_axis=0, concat_axis=0, tiled=True)]
  transfers between devices with their start and end apart: 24 -> 17, of which waited for: 11 -> 10; matrix products, arithmetic and copies ran while one was open for 5% -> 4% of each run, Pallas kernels for 26% -> 25%
where the time goes in v3:
time: 334 us; the launch traced here: 333 us
  waiting for transfers between devices  124 us (37%)
  Pallas kernels  83 us (25%)
  starting transfers between devices  63.7 us (19%)
  local copies, waits for them, and re-layouts  32.7 us (10%)
  between operations  14.7 us (4%)
  matrix products  7.48 us (2%)
  other arithmetic  7.2 us (2%)
    all_to_all x5, waiting for transfers between devices, served(): lax.all_to_all(sent, ('x', 'y'), split_axis=0, concat_axis=0, tiled=True)  105 us
    all_to_all x5, starting transfers between devices, served(): lax.all_to_all(sent, ('x', 'y'), split_axis=0, concat_axis=0, tiled=True)  39.5 us
    pallas_call x5, Pallas kernels, listed_part(): pl.pallas_call(lambda *refs: listed_kernel((width // heads) ** (-0.5), he...  37.3 us
    pallas_call x5, Pallas kernels, pack(): pl.pallas_call(lambda *refs: pack_kernel(slots, half, len(extras), *refs)...  33.7 us
    unnamed x66, local copies, waits for them, and re-layouts  21 us
    ppermute x8, starting transfers between devices, step(): return (lax.ppermute(pair[0], 'z', up), lax.ppermute(pair[1], 'z', down))  14.8 us
    pallas_call x1, Pallas kernels, local_part(): pl.pallas_call(lambda *refs: local_kernel(head_size ** (-0.5), *refs), gr...  12 us
    ppermute x8, waiting for transfers between devices, step(): return (lax.ppermute(pair[0], 'z', up), lax.ppermute(pair[1], 'z', down))  10.9 us
  transfers between devices with their start and end apart: 17, of which 10 were waited for; matrix products, arithmetic and copies ran while one was open for 4% of the time, Pallas kernels for 25%

profile of v3, /device:TPU:1, one launch (start us, length us, event | category | flops | bytes accessed | tf_op | source)
XLA Modules:
  0.0 333.2 jit_solution(4063980979001961201)
XLA Ops:
  10.5 2.5 collective-permute-start
  12.9 3.9 %collective-permute-start.1 = (bf16[32,2,128,128]{3,2,1,0:T(8,128)(2,1)}, bf16[32,2,128,128]{3,2,1,0:T(8,128)(2,1)}, u32[]{:S(2)}, u32[]{:S(2)}) collective-permute-start(bf16[32,2,128,128]{3,2,1,0:T(8,128)(2,1)} %pad_maximum_fusion.refs_1_), channel_id=1, source_target_pairs={{0,112},{16,0},{32,16},{48,32},{64,48},{80,64},{96,80},{112,96},{1... | collective-permute-start | bytes 6291464 | tf_op jit(solution)/shard_map/ppermute | solution.py:245
  18.7 6.8 %all-to-all-start = ((s32[16,8,2]{1,2,0:T(2,128)}), s32[16,8,2]{1,2,0:T(2,128)S(1)}, u32[]{:S(2)}, u32[]{:S(2)}) async-start(s32[16,8,2]{1,2,0:T(2,128)} %select_reduce_fusion), calls=%async_computation | async-start | bytes 32768 | tf_op jit(solution)/shard_map/all_to_all | solution.py:198
  29.0 12.0 %local_part.1.refs_7_ = f32[256,2048]{1,0:T(8,128)} custom-call(f32[16]{0:T(128)} %copy-done.25, f32[16]{0:T(128)} %copy-done.26, bf16[256,2048]{1,0:T(8,128)(2,1)} %bitcast.36, bf16[256,2048]{1,0:T(8,128)(2,1)} %bitcast.47, bf16[256,2048]{1,0:T(8,128)(2,1)} %bitcast.46), custom_call_target="tpu_custom_call" | custom-call | flops 1 | bytes 1 | tf_op jit(solution)/shard_map/local_part/pallas_call | solution.py:89
  42.5 5.9 %pack_blocks.5 = bf16[48,2,128,128]{3,2,1,0:T(8,128)(2,1)S(1)} custom-call(s32[32]{0:T(128)S(1)} %reshape.453.refs_0_, bf16[32,2,128,128]{3,2,1,0:T(8,128)(2,1)} %pad_maximum_fusion.refs_1_, bf16[2,128,128]{2,1,0:T(8,128)(2,1)S(1)} %reshape.454.refs_2_), custom_call_target="tpu_custom_call" | custom-call | flops 49999998976 | bytes 150000000 | tf_op jit(solution)/shard_map/pack_blocks/pallas_call | solution.py:55
  50.4 6.7 %all-to-all-start.1 = ((bf16[48,2,128,128]{3,2,1,0:T(8,128)(2,1)}), bf16[48,2,128,128]{3,2,1,0:T(8,128)(2,1)S(1)}, u32[]{:S(2)}, u32[]{:S(2)}) async-start(bf16[48,2,128,128]{3,2,1,0:T(8,128)(2,1)} %copy-done.13), calls=%async_computation.1 | async-start | bytes 6291456 | tf_op jit(solution)/shard_map/all_to_all | solution.py:233
  57.7 4.8 %collective-permute-done.refs_1_ = bf16[32,2,128,128]{3,2,1,0:T(8,128)(2,1)} collective-permute-done((bf16[32,2,128,128]{3,2,1,0:T(8,128)(2,1)}, bf16[32,2,128,128]{3,2,1,0:T(8,128)(2,1)}, u32[]{:S(2)}, u32[]{:S(2)}) %collective-permute-start) | collective-permute-done | bytes 2097184 | tf_op jit(solution)/shard_map/ppermute | solution.py:245
  62.5 2.7 collective-permute-start.3
  65.2 8.0 %pack_blocks.6 = bf16[64,2,128,128]{3,2,1,0:T(8,128)(2,1)S(1)} custom-call(s32[64]{0:T(128)S(1)} %reshape.455.refs_0_, bf16[32,2,128,128]{3,2,1,0:T(8,128)(2,1)} %collective-permute-done.refs_1_, bf16[32,2,128,128]{3,2,1,0:T(8,128)(2,1)} %collective-permute-done.1.refs_2_), custom_call_target="tpu_custom_call" | custom-call | flops 49999998976 | bytes 150000000 | tf_op jit(solution)/shard_map/pack_blocks/pallas_call | solution.py:55
  75.2 20.8 %all-to-all-done.1.refs_6_ = bf16[48,2,128,128]{3,2,1,0:T(8,128)(2,1)S(1)} async-done(((bf16[48,2,128,128]{3,2,1,0:T(8,128)(2,1)}), bf16[48,2,128,128]{3,2,1,0:T(8,128)(2,1)S(1)}, u32[]{:S(2)}, u32[]{:S(2)}) %all-to-all-start.1) | async-done | bytes 3145760 | tf_op jit(solution)/shard_map/all_to_all | solution.py:233
  96.0 4.5 %all-to-all-start.2 = ((bf16[64,2,128,128]{3,2,1,0:T(8,128)(2,1)}), bf16[64,2,128,128]{3,2,1,0:T(8,128)(2,1)}, u32[]{:S(2)}, u32[]{:S(2)}) async-start(bf16[64,2,128,128]{3,2,1,0:T(8,128)(2,1)} %copy-done.12), calls=%async_computation.2 | async-start | bytes 8388608 | tf_op jit(solution)/shard_map/all_to_all | solution.py:233
  101.6 2.3 reshape_squeeze.11
  103.9 6.0 %collective-permute-done.2.refs_1_ = bf16[32,2,128,128]{3,2,1,0:T(8,128)(2,1)} collective-permute-done((bf16[32,2,128,128]{3,2,1,0:T(8,128)(2,1)}, bf16[32,2,128,128]{3,2,1,0:T(8,128)(2,1)}, u32[]{:S(2)}, u32[]{:S(2)}) %collective-permute-start.2) | collective-permute-done | bytes 2097184 | tf_op jit(solution)/shard_map/ppermute | solution.py:245
  112.7 8.1 %pack_blocks.7 = bf16[64,2,128,128]{3,2,1,0:T(8,128)(2,1)S(1)} custom-call(s32[64]{0:T(128)S(1)} %reshape.456.refs_0_, bf16[32,2,128,128]{3,2,1,0:T(8,128)(2,1)} %collective-permute-done.2.refs_1_, bf16[32,2,128,128]{3,2,1,0:T(8,128)(2,1)} %collective-permute-done.3.refs_2_), custom_call_target="tpu_custom_call" | custom-call | flops 49999998976 | bytes 150000000 | tf_op jit(solution)/shard_map/pack_blocks/pallas_call | solution.py:55
  122.8 5.5 %listed_part.5.refs_7_ = f32[256,2048]{1,0:T(8,128)S(1)} custom-call(s32[128]{0:T(128)S(1)} %select_reduce_fusion.1.refs_0_, s32[2]{0:T(128)S(1)} %get-tuple-element.65.refs_1_, s32[128]{0:T(128)S(1)} %get-tuple-element.55.refs_2_, f32[128]{0:T(128)S(1)} %multiply_subtract_fusion.refs_3_, f32[128]{0:T(128)S(1)} %get-tuple-element.53.refs_4_, ...), custom_call_target="tpu_custom_call" | custom-call | flops 1 | bytes 1 | tf_op jit(solution)/shard_map/listed_part/pallas_call | solution.py:148
  128.3 20.6 %all-to-all-done.2.refs_6_ = bf16[64,2,128,128]{3,2,1,0:T(8,128)(2,1)} async-done(((bf16[64,2,128,128]{3,2,1,0:T(8,128)(2,1)}), bf16[64,2,128,128]{3,2,1,0:T(8,128)(2,1)}, u32[]{:S(2)}, u32[]{:S(2)}) %all-to-all-start.2) | async-done | bytes 4194336 | tf_op jit(solution)/shard_map/all_to_all | solution.py:233
  148.9 9.6 %all-to-all-start.3 = ((bf16[64,2,128,128]{3,2,1,0:T(8,128)(2,1)}), bf16[64,2,128,128]{3,2,1,0:T(8,128)(2,1)}, u32[]{:S(2)}, u32[]{:S(2)}) async-start(bf16[64,2,128,128]{3,2,1,0:T(8,128)(2,1)} %copy-done.10), calls=%async_computation.3 | async-start | bytes 8388608 | tf_op jit(solution)/shard_map/all_to_all | solution.py:233
  161.5 2.7 collective-permute-start.7
  164.3 8.0 %pack_blocks.8 = bf16[64,2,128,128]{3,2,1,0:T(8,128)(2,1)S(1)} custom-call(s32[64]{0:T(128)S(1)} %reshape.457.refs_0_, bf16[32,2,128,128]{3,2,1,0:T(8,128)(2,1)} %collective-permute-done.4.refs_1_, bf16[32,2,128,128]{3,2,1,0:T(8,128)(2,1)} %collective-permute-done.5.refs_2_), custom_call_target="tpu_custom_call" | custom-call | flops 49999998976 | bytes 150000000 | tf_op jit(solution)/shard_map/pack_blocks/pallas_call | solution.py:55
  174.2 8.8 %listed_part.6.refs_7_ = f32[256,2048]{1,0:T(8,128)S(1)} custom-call(s32[128]{0:T(128)S(1)} %select_reduce_fusion.1.refs_0_, s32[2]{0:T(128)S(1)} %get-tuple-element.64.refs_1_, s32[128]{0:T(128)S(1)} %get-tuple-element.55.refs_2_, f32[128]{0:T(128)S(1)} %multiply_subtract_fusion.refs_3_, f32[128]{0:T(128)S(1)} %get-tuple-element.53.refs_4_, ...), custom_call_target="tpu_custom_call" | custom-call | flops 1 | bytes 1 | tf_op jit(solution)/shard_map/listed_part/pallas_call | solution.py:148
  186.4 20.1 %all-to-all-done.3.refs_6_ = bf16[64,2,128,128]{3,2,1,0:T(8,128)(2,1)} async-done(((bf16[64,2,128,128]{3,2,1,0:T(8,128)(2,1)}), bf16[64,2,128,128]{3,2,1,0:T(8,128)(2,1)}, u32[]{:S(2)}, u32[]{:S(2)}) %all-to-all-start.3) | async-done | bytes 4194336 | tf_op jit(solution)/shard_map/all_to_all | solution.py:233
  206.6 8.4 %all-to-all-start.4 = ((bf16[64,2,128,128]{3,2,1,0:T(8,128)(2,1)}), bf16[64,2,128,128]{3,2,1,0:T(8,128)(2,1)}, u32[]{:S(2)}, u32[]{:S(2)}) async-start(bf16[64,2,128,128]{3,2,1,0:T(8,128)(2,1)} %copy-done.11), calls=%async_computation.4 | async-start | bytes 8388608 | tf_op jit(solution)/shard_map/all_to_all | solution.py:233
  215.0 3.7 %pack_blocks.9 = bf16[32,2,128,128]{3,2,1,0:T(8,128)(2,1)S(1)} custom-call(s32[32]{0:T(128)S(1)} %reshape.452.refs_0_, bf16[16,2,128,128]{3,2,1,0:T(8,128)(2,1)S(1)} %copy-done.18, bf16[16,2,128,128]{3,2,1,0:T(8,128)(2,1)S(1)} %copy-done.20), custom_call_target="tpu_custom_call" | custom-call | flops 49999998976 | bytes 150000000 | tf_op jit(solution)/shard_map/pack_blocks/pallas_call | solution.py:55
  220.1 10.2 %listed_part.7.refs_7_ = f32[256,2048]{1,0:T(8,128)S(1)} custom-call(s32[128]{0:T(128)S(1)} %select_reduce_fusion.1.refs_0_, s32[2]{0:T(128)S(1)} %get-tuple-element.63.refs_1_, s32[128]{0:T(128)S(1)} %get-tuple-element.55.refs_2_, f32[128]{0:T(128)S(1)} %multiply_subtract_fusion.refs_3_, f32[128]{0:T(128)S(1)} %get-tuple-element.53.refs_4_, ...), custom_call_target="tpu_custom_call" | custom-call | flops 1 | bytes 1 | tf_op jit(solution)/shard_map/listed_part/pallas_call | solution.py:148
  231.7 30.2 %all-to-all-done.4.refs_6_ = bf16[64,2,128,128]{3,2,1,0:T(8,128)(2,1)} async-done(((bf16[64,2,128,128]{3,2,1,0:T(8,128)(2,1)}), bf16[64,2,128,128]{3,2,1,0:T(8,128)(2,1)}, u32[]{:S(2)}, u32[]{:S(2)}) %all-to-all-start.4) | async-done | bytes 4194336 | tf_op jit(solution)/shard_map/all_to_all | solution.py:233
  261.9 10.3 %all-to-all-start.5 = ((bf16[32,2,128,128]{3,2,1,0:T(8,128)(2,1)}), bf16[32,2,128,128]{3,2,1,0:T(8,128)(2,1)S(1)}, u32[]{:S(2)}, u32[]{:S(2)}) async-start(bf16[32,2,128,128]{3,2,1,0:T(8,128)(2,1)} %copy-done.14), calls=%async_computation.5 | async-start | bytes 4194304 | tf_op jit(solution)/shard_map/all_to_all | solution.py:233
  273.9 8.8 %listed_part.8.refs_7_ = f32[256,2048]{1,0:T(8,128)S(1)} custom-call(s32[128]{0:T(128)S(1)} %select_reduce_fusion.1.refs_0_, s32[2]{0:T(128)S(1)} %get-tuple-element.62.refs_1_, s32[128]{0:T(128)S(1)} %get-tuple-element.55.refs_2_, f32[128]{0:T(128)S(1)} %multiply_subtract_fusion.refs_3_, f32[128]{0:T(128)S(1)} %get-tuple-element.53.refs_4_, ...), custom_call_target="tpu_custom_call" | custom-call | flops 1 | bytes 1 | tf_op jit(solution)/shard_map/listed_part/pallas_call | solution.py:148
  284.0 13.3 %all-to-all-done.5.refs_6_ = bf16[32,2,128,128]{3,2,1,0:T(8,128)(2,1)S(1)} async-done(((bf16[32,2,128,128]{3,2,1,0:T(8,128)(2,1)}), bf16[32,2,128,128]{3,2,1,0:T(8,128)(2,1)S(1)}, u32[]{:S(2)}, u32[]{:S(2)}) %all-to-all-start.5) | async-done | bytes 2097184 | tf_op jit(solution)/shard_map/all_to_all | solution.py:233
  298.9 4.0 %listed_part.9 = bf16[256,2048]{1,0:T(8,128)(2,1)S(1)} custom-call(s32[128]{0:T(128)S(1)} %select_reduce_fusion.1.refs_0_, s32[2]{0:T(128)S(1)} %get-tuple-element.66.refs_1_, s32[128]{0:T(128)S(1)} %get-tuple-element.55.refs_2_, f32[128]{0:T(128)S(1)} %multiply_subtract_fusion.refs_3_, f32[128]{0:T(128)S(1)} %get-tuple-element.53.refs_4_, ...), custom_call_target="tpu_custom_call" | custom-call | flops 1 | bytes 1 | tf_op jit(solution)/shard_map/listed_part/pallas_call | solution.py:148
  305.1 4.0 %add_convert_fusion.3 = (bf16[256,1024]{1,0:T(8,128)(2,1)S(1)}, f32[256,1024]{1,0:T(8,128)S(1)}) fusion(bf16[256,2048]{1,0:T(8,128)(2,1)} %param.10, bf16[256,2048]{1,0:T(8,128)(2,1)} %copy-done.15, bf16[2048,2048]{1,0:T(8,128)(2,1)} %all-gather.2.cloned.1.call-done), kind=kOutput, calls=%fused_computation.10 | convolution fusion | flops 1074528256 | bytes 7340032 | tf_op jit(solution)/shard_map/dot_general | solution.py:279
  309.1 3.5 %add_convert_fusion.2 = (bf16[256,1024]{1,0:T(8,128)(2,1)S(1)}, f32[256,1024]{1,0:T(8,128)S(1)}) fusion(bf16[256,2048]{1,0:T(8,128)(2,1)S(1)} %copy-done.30, bf16[256,2048]{1,0:T(8,128)(2,1)S(1)} %copy-done.16, bf16[2048,2048]{1,0:T(8,128)(2,1)} %all-gather.2.cloned.1.call-done), kind=kOutput, calls=%fused_computation.9 | convolution fusion | flops 1074528256 | bytes 7340032 | tf_op jit(solution)/shard_map/dot_general | solution.py:279
  315.2 6.5 %collective-permute-done.9 = bf16[256,1024]{1,0:T(8,128)(2,1)} collective-permute-done((bf16[256,1024]{1,0:T(8,128)(2,1)S(1)}, bf16[256,1024]{1,0:T(8,128)(2,1)}, u32[]{:S(2)}, u32[]{:S(2)}) %collective-permute-start.9) | collective-permute-done | bytes 524320 | tf_op jit(solution)/shard_map/ppermute | solution.py:281
  (132 shorter events, 45.3 us)
Async XLA Ops:
  8.9 8.0 %copy-start.27 = (s32[1,2,16,4]{2,3,1,0:T(4,128)S(1)}, s32[1,2,16,4]{2,3,1,0:T(4,128)}, u32[]{:S(2)}) copy-start(s32[1,2,16,4]{2,3,1,0:T(4,128)} %param.16) | copy-start | bytes 1540
  8.9 8.4 %copy-start.31 = (s32[8]{0:T(128)S(1)}, s32[8]{0:T(128)}, u32[]{:S(2)}) copy-start(s32[8]{0:T(128)} %constant.157.clone) | copy-start | bytes 100
  8.9 17.0 %copy-start.28 = (f32[1,16]{1,0:T(1,128)S(1)}, f32[1,16]{1,0:T(1,128)}, u32[]{:S(2)}) copy-start(f32[1,16]{1,0:T(1,128)} %param.14) | copy-start | bytes 196
  8.9 17.0 %copy-start.29 = (f32[1,16]{1,0:T(1,128)S(1)}, f32[1,16]{1,0:T(1,128)}, u32[]{:S(2)}) copy-start(f32[1,16]{1,0:T(1,128)} %param.15) | copy-start | bytes 196
  8.9 17.4 %copy-start.21 = (s32[128]{0:T(128)S(1)}, s32[128]{0:T(128)}, u32[]{:S(2)}) copy-start(s32[128]{0:T(128)} %param.17) | copy-start | bytes 1540
  10.5 52.1 %collective-permute-start = (bf16[32,2,128,128]{3,2,1,0:T(8,128)(2,1)}, bf16[32,2,128,128]{3,2,1,0:T(8,128)(2,1)}, u32[]{:S(2)}, u32[]{:S(2)}) collective-permute-start(bf16[32,2,128,128]{3,2,1,0:T(8,128)(2,1)} %pad_maximum_fusion.refs_1_), channel_id=1, source_target_pairs={{0,16},{16,32},{32,48},{48,64},{64,80},{80,96},{96,112},{112,0},{1... | collective-permute-start | bytes 6291464 | tf_op jit(solution)/shard_map/ppermute | solution.py:245
  12.9 49.6 %collective-permute-start.1 = (bf16[32,2,128,128]{3,2,1,0:T(8,128)(2,1)}, bf16[32,2,128,128]{3,2,1,0:T(8,128)(2,1)}, u32[]{:S(2)}, u32[]{:S(2)}) collective-permute-start(bf16[32,2,128,128]{3,2,1,0:T(8,128)(2,1)} %pad_maximum_fusion.refs_1_), channel_id=1, source_target_pairs={{0,112},{16,0},{32,16},{48,32},{64,48},{80,64},{96,80},{112,96},{1... | collective-permute-start | bytes 6291464 | tf_op jit(solution)/shard_map/ppermute | solution.py:245
  18.7 22.4 %all-to-all-start = ((s32[16,8,2]{1,2,0:T(2,128)}), s32[16,8,2]{1,2,0:T(2,128)S(1)}, u32[]{:S(2)}, u32[]{:S(2)}) async-start(s32[16,8,2]{1,2,0:T(2,128)} %select_reduce_fusion), calls=%async_computation | async-start | bytes 32768 | tf_op jit(solution)/shard_map/all_to_all | solution.py:198
  29.0 12.1 %copy-start.23 = (bf16[1,16,2048]{2,1,0:T(8,128)(2,1)S(1)}, bf16[1,16,2048]{2,1,0:T(8,128)(2,1)}, u32[]{:S(2)}) copy-start(bf16[1,16,2048]{2,1,0:T(8,128)(2,1)} %param.18) | copy-start | bytes 196612
  50.4 45.6 %all-to-all-start.1 = ((bf16[48,2,128,128]{3,2,1,0:T(8,128)(2,1)}), bf16[48,2,128,128]{3,2,1,0:T(8,128)(2,1)S(1)}, u32[]{:S(2)}, u32[]{:S(2)}) async-start(bf16[48,2,128,128]{3,2,1,0:T(8,128)(2,1)} %copy-done.13), calls=%async_computation.1 | async-start | bytes 6291456 | tf_op jit(solution)/shard_map/all_to_all | solution.py:233
  62.5 47.4 %collective-permute-start.2 = (bf16[32,2,128,128]{3,2,1,0:T(8,128)(2,1)}, bf16[32,2,128,128]{3,2,1,0:T(8,128)(2,1)}, u32[]{:S(2)}, u32[]{:S(2)}) collective-permute-start(bf16[32,2,128,128]{3,2,1,0:T(8,128)(2,1)} %collective-permute-done.refs_1_), channel_id=1, source_target_pairs={{0,16},{16,32},{32,48},{48,64},{64,80},{80,96},{96,112},{112,0},{1... | collective-permute-start | bytes 6291464 | tf_op jit(solution)/shard_map/ppermute | solution.py:245
  62.5 47.4 %collective-permute-start.3 = (bf16[32,2,128,128]{3,2,1,0:T(8,128)(2,1)}, bf16[32,2,128,128]{3,2,1,0:T(8,128)(2,1)}, u32[]{:S(2)}, u32[]{:S(2)}) collective-permute-start(bf16[32,2,128,128]{3,2,1,0:T(8,128)(2,1)} %collective-permute-done.1.refs_2_), channel_id=1, source_target_pairs={{0,112},{16,0},{32,16},{48,32},{64,48},{80,64},{96,80},{112,96},{1... | collective-permute-start | bytes 6291464 | tf_op jit(solution)/shard_map/ppermute | solution.py:245
  96.0 4.6 %copy-start.1 = (bf16[48,2,128,128]{3,2,1,0:T(8,128)(2,1)}, bf16[48,2,128,128]{3,2,1,0:T(8,128)(2,1)S(1)}, u32[]{:S(2)}) copy-start(bf16[48,2,128,128]{3,2,1,0:T(8,128)(2,1)S(1)} %all-to-all-done.1.refs_6_) | copy-start | bytes 9437188
  96.0 52.9 %all-to-all-start.2 = ((bf16[64,2,128,128]{3,2,1,0:T(8,128)(2,1)}), bf16[64,2,128,128]{3,2,1,0:T(8,128)(2,1)}, u32[]{:S(2)}, u32[]{:S(2)}) async-start(bf16[64,2,128,128]{3,2,1,0:T(8,128)(2,1)} %copy-done.12), calls=%async_computation.2 | async-start | bytes 8388608 | tf_op jit(solution)/shard_map/all_to_all | solution.py:233
  103.9 18.9 %copy-start = (bf16[1,256,2048]{2,1,0:T(8,128)(2,1)S(1)}, bf16[1,256,2048]{2,1,0:T(8,128)(2,1)}, u32[]{:S(2)}) copy-start(bf16[1,256,2048]{2,1,0:T(8,128)(2,1)} %param.11) | copy-start | bytes 3145732
  103.9 18.9 %copy-start.3 = (f32[256,2048]{1,0:T(8,128)S(1)}, f32[256,2048]{1,0:T(8,128)}, u32[]{:S(2)}) copy-start(f32[256,2048]{1,0:T(8,128)} %local_part.1.refs_7_) | copy-start | bytes 6291460
  110.0 48.6 %collective-permute-start.4 = (bf16[32,2,128,128]{3,2,1,0:T(8,128)(2,1)}, bf16[32,2,128,128]{3,2,1,0:T(8,128)(2,1)}, u32[]{:S(2)}, u32[]{:S(2)}) collective-permute-start(bf16[32,2,128,128]{3,2,1,0:T(8,128)(2,1)} %collective-permute-done.2.refs_1_), channel_id=1, source_target_pairs={{0,16},{16,32},{32,48},{48,64},{64,80},{80,96},{96,112},{112,0},{1... | collective-permute-start | bytes 6291464 | tf_op jit(solution)/shard_map/ppermute | solution.py:245
  110.9 47.7 %collective-permute-start.5 = (bf16[32,2,128,128]{3,2,1,0:T(8,128)(2,1)}, bf16[32,2,128,128]{3,2,1,0:T(8,128)(2,1)}, u32[]{:S(2)}, u32[]{:S(2)}) collective-permute-start(bf16[32,2,128,128]{3,2,1,0:T(8,128)(2,1)} %collective-permute-done.3.refs_2_), channel_id=1, source_target_pairs={{0,112},{16,0},{32,16},{48,32},{64,48},{80,64},{96,80},{112,96},{1... | collective-permute-start | bytes 6291464 | tf_op jit(solution)/shard_map/ppermute | solution.py:245
  112.7 10.2 %copy-start.2 = (bf16[48,2,128,128]{3,2,1,0:T(8,128)(2,1)S(1)}, bf16[48,2,128,128]{3,2,1,0:T(8,128)(2,1)}, u32[]{:S(2)}) copy-start(bf16[48,2,128,128]{3,2,1,0:T(8,128)(2,1)} %copy-done.1) | copy-start | bytes 9437188
  148.9 57.6 %all-to-all-start.3 = ((bf16[64,2,128,128]{3,2,1,0:T(8,128)(2,1)}), bf16[64,2,128,128]{3,2,1,0:T(8,128)(2,1)}, u32[]{:S(2)}, u32[]{:S(2)}) async-start(bf16[64,2,128,128]{3,2,1,0:T(8,128)(2,1)} %copy-done.10), calls=%async_computation.3 | async-start | bytes 8388608 | tf_op jit(solution)/shard_map/all_to_all | solution.py:233
  158.5 146.5 %all-gather.2.cloned.1.call-start = ((), (), s32[]{:S(2)}) async-start(), calls=%async_computation.6 | async-start | bytes 9437184 | tf_op jit(solution)/shard_map/all_gather | solution.py:266
  159.9 24.5 %collective-permute-start.6 = (bf16[16,2,128,128]{3,2,1,0:T(8,128)(2,1)S(1)}, bf16[16,2,128,128]{3,2,1,0:T(8,128)(2,1)S(1)}, u32[]{:S(2)}, u32[]{:S(2)}) collective-permute-start(bf16[16,2,128,128]{3,2,1,0:T(8,128)(2,1)S(1)} %slice.58), channel_id=1, source_target_pairs={{0,16},{16,32},{32,48},{48,64},{64,80},{80,96},{96,112},{112,0},{1... | collective-permute-start | bytes 3145736 | tf_op jit(solution)/shard_map/ppermute | solution.py:245
  161.5 23.8 %collective-permute-start.7 = (bf16[16,2,128,128]{3,2,1,0:T(8,128)(2,1)S(1)}, bf16[16,2,128,128]{3,2,1,0:T(8,128)(2,1)S(1)}, u32[]{:S(2)}, u32[]{:S(2)}) collective-permute-start(bf16[16,2,128,128]{3,2,1,0:T(8,128)(2,1)S(1)} %slice.59), channel_id=1, source_target_pairs={{0,112},{16,0},{32,16},{48,32},{64,48},{80,64},{96,80},{112,96},{1... | collective-permute-start | bytes 3145736 | tf_op jit(solution)/shard_map/ppermute | solution.py:245
  174.2 32.3 %copy-start.24 = (s32[16,2]{1,0:T(8,128)S(1)}, s32[16,2]{1,0:T(8,128)}, u32[]{:S(2)}) copy-start(s32[16,2]{1,0:T(8,128)} %get-tuple-element.50) | copy-start | bytes 388
  206.6 8.4 %copy-start.18 = (bf16[16,2,128,128]{3,2,1,0:T(8,128)(2,1)S(1)}, bf16[16,2,128,128]{3,2,1,0:T(8,128)(2,1)}, u32[]{:S(2)}) copy-start(bf16[16,2,128,128]{3,2,1,0:T(8,128)(2,1)} %copy-done.17) | copy-start | bytes 3145732
  206.6 8.4 %copy-start.20 = (bf16[16,2,128,128]{3,2,1,0:T(8,128)(2,1)S(1)}, bf16[16,2,128,128]{3,2,1,0:T(8,128)(2,1)}, u32[]{:S(2)}) copy-start(bf16[16,2,128,128]{3,2,1,0:T(8,128)(2,1)} %copy-done.19) | copy-start | bytes 3145732
  206.6 55.3 %all-to-all-start.4 = ((bf16[64,2,128,128]{3,2,1,0:T(8,128)(2,1)}), bf16[64,2,128,128]{3,2,1,0:T(8,128)(2,1)}, u32[]{:S(2)}, u32[]{:S(2)}) async-start(bf16[64,2,128,128]{3,2,1,0:T(8,128)(2,1)} %copy-done.11), calls=%async_computation.4 | async-start | bytes 8388608 | tf_op jit(solution)/shard_map/all_to_all | solution.py:233
  215.0 5.1 %copy-start.7 = (f32[256,2048]{1,0:T(8,128)S(1)}, f32[256,2048]{1,0:T(8,128)}, u32[]{:S(2)}) copy-start(f32[256,2048]{1,0:T(8,128)} %copy-done.6) | copy-start | bytes 6291460
  261.9 35.4 %all-to-all-start.5 = ((bf16[32,2,128,128]{3,2,1,0:T(8,128)(2,1)}), bf16[32,2,128,128]{3,2,1,0:T(8,128)(2,1)S(1)}, u32[]{:S(2)}, u32[]{:S(2)}) async-start(bf16[32,2,128,128]{3,2,1,0:T(8,128)(2,1)} %copy-done.14), calls=%async_computation.5 | async-start | bytes 4194304 | tf_op jit(solution)/shard_map/all_to_all | solution.py:233
  305.1 4.0 %copy-start.30 = (bf16[256,2048]{1,0:T(8,128)(2,1)S(1)}, bf16[256,2048]{1,0:T(8,128)(2,1)}, u32[]{:S(2)}) copy-start(bf16[256,2048]{1,0:T(8,128)(2,1)} %param.10) | copy-start | bytes 3145732
  312.6 9.1 %collective-permute-start.9 = (bf16[256,1024]{1,0:T(8,128)(2,1)S(1)}, bf16[256,1024]{1,0:T(8,128)(2,1)}, u32[]{:S(2)}, u32[]{:S(2)}) collective-permute-start(bf16[256,1024]{1,0:T(8,128)(2,1)S(1)} %get-tuple-element.69), channel_id=1, source_target_pairs={{0,128},{1,129},{2,130},{3,131},{4,132},{5,133},{6,134},{7,135},{8... | collective-permute-start | bytes 1572872 | tf_op jit(solution)/shard_map/ppermute | solution.py:281
  313.9 9.9 %collective-permute-start.8 = (bf16[256,1024]{1,0:T(8,128)(2,1)S(1)}, bf16[256,1024]{1,0:T(8,128)(2,1)}, u32[]{:S(2)}, u32[]{:S(2)}) collective-permute-start(bf16[256,1024]{1,0:T(8,128)(2,1)S(1)} %get-tuple-element.67), channel_id=1, source_target_pairs={{0,128},{1,129},{2,130},{3,131},{4,132},{5,133},{6,134},{7,135},{8... | collective-permute-start | bytes 1572872 | tf_op jit(solution)/shard_map/ppermute | solution.py:281
  (17 other events, 31.2 us)
Sparse Core Ops, SparseCore 0:
  206.6 98.4 all-gather.1

commit v4 on v3

--- a/solution.py
+++ b/solution.py
@@ -247,7 +247,7 @@
     ring = step((kv, kv))
     packed = chosen(0, kv, extra=out_weight.reshape(kv.shape[1:]))
     got = served(packed)
-    acc = local_part(offset, slope, q, k, v, heads)
+    acc = local_part(offset, slope, after(q, packed), k, v, heads)
     ring = after(ring, packed, acc)
     for n in (1, 2, 3):
         later = step(ring) if n < 3 else step((ring[0][:half], ring[1][half:]))

time: 334 us -> 321 us (0.961)
  waiting for transfers between devices: 124 us -> 109 us
    all_to_all x5, waiting for transfers between devices: 105 us -> 63.8 us  [served(): lax.all_to_all(sent, ('x', 'y'), split_axis=0, concat_axis=0, tiled=True)]
    ppermute x8, waiting for transfers between devices: 10.9 us -> 34.6 us  [step(): return (lax.ppermute(pair[0], 'z', up), lax.ppermute(pair[1], 'z', down))]
  transfers between devices with their start and end apart: 17 -> 17, of which waited for: 10 -> 12; matrix products, arithmetic and copies ran while one was open for 4% -> 4% of each run, Pallas kernels for 25% -> 26%
where the time goes in v4:
time: 321 us; the launch traced here: 318 us
  waiting for transfers between devices  109 us (34%)
  Pallas kernels  81.5 us (25%)
  starting transfers between devices  65.7 us (20%)
  local copies, waits for them, and re-layouts  32.6 us (10%)
  between operations  14.7 us (5%)
  matrix products  7.48 us (2%)
  other arithmetic  7.2 us (2%)
    all_to_all x5, waiting for transfers between devices, served(): lax.all_to_all(sent, ('x', 'y'), split_axis=0, concat_axis=0, tiled=True)  63.8 us
    all_to_all x5, starting transfers between devices, served(): lax.all_to_all(sent, ('x', 'y'), split_axis=0, concat_axis=0, tiled=True)  41.6 us
    pallas_call x5, Pallas kernels, listed_part(): pl.pallas_call(lambda *refs: listed_kernel((width // heads) ** (-0.5), he...  35.8 us
    ppermute x8, waiting for transfers between devices, step(): return (lax.ppermute(pair[0], 'z', up), lax.ppermute(pair[1], 'z', down))  34.6 us
    pallas_call x5, Pallas kernels, pack(): pl.pallas_call(lambda *refs: pack_kernel(slots, half, len(extras), *refs)...  33.7 us
    unnamed x66, local copies, waits for them, and re-layouts  21 us
    ppermute x8, starting transfers between devices, step(): return (lax.ppermute(pair[0], 'z', up), lax.ppermute(pair[1], 'z', down))  14.8 us
    pallas_call x1, Pallas kernels, local_part(): pl.pallas_call(lambda *refs: local_kernel(head_size ** (-0.5), *refs), gr...  12.1 us
  transfers between devices with their start and end apart: 17, of which 12 were waited for; matrix products, arithmetic and copies ran while one was open for 4% of the time, Pallas kernels for 26%

profile of v4, /device:TPU:1, one launch (start us, length us, event | category | flops | bytes accessed | tf_op | source)
XLA Modules:
  0.0 318.0 jit_solution(4170498361056188871)
XLA Ops:
  12.9 3.9 %collective-permute-start.1 = (bf16[32,2,128,128]{3,2,1,0:T(8,128)(2,1)}, bf16[32,2,128,128]{3,2,1,0:T(8,128)(2,1)}, u32[]{:S(2)}, u32[]{:S(2)}) collective-permute-start(bf16[32,2,128,128]{3,2,1,0:T(8,128)(2,1)} %pad_maximum_fusion.refs_1_), channel_id=1, source_target_pairs={{0,112},{16,0},{32,16},{48,32},{64,48},{80,64},{96,80},{112,96},{1... | collective-permute-start | bytes 6291464 | tf_op jit(solution)/shard_map/ppermute | solution.py:245
  18.7 6.8 %all-to-all-start = ((s32[16,8,2]{1,2,0:T(2,128)}), s32[16,8,2]{1,2,0:T(2,128)S(1)}, u32[]{:S(2)}, u32[]{:S(2)}) async-start(s32[16,8,2]{1,2,0:T(2,128)} %select_reduce_fusion), calls=%async_computation | async-start | bytes 32768 | tf_op jit(solution)/shard_map/all_to_all | solution.py:198
  29.0 2.9 all-to-all-done
  33.3 5.9 %pack_blocks.5 = bf16[48,2,128,128]{3,2,1,0:T(8,128)(2,1)S(1)} custom-call(s32[32]{0:T(128)S(1)} %reshape.453.refs_0_, bf16[32,2,128,128]{3,2,1,0:T(8,128)(2,1)} %pad_maximum_fusion.refs_1_, bf16[2,128,128]{2,1,0:T(8,128)(2,1)S(1)} %reshape.454.refs_2_), custom_call_target="tpu_custom_call" | custom-call | flops 49999998976 | bytes 150000000 | tf_op jit(solution)/shard_map/pack_blocks/pallas_call | solution.py:55
  40.8 3.8 %all-to-all-start.1 = ((bf16[48,2,128,128]{3,2,1,0:T(8,128)(2,1)}), bf16[48,2,128,128]{3,2,1,0:T(8,128)(2,1)S(1)}, u32[]{:S(2)}, u32[]{:S(2)}) async-start(bf16[48,2,128,128]{3,2,1,0:T(8,128)(2,1)} %copy-done.13), calls=%async_computation.1 | async-start | bytes 6291456 | tf_op jit(solution)/shard_map/all_to_all | solution.py:233
  44.6 12.1 %local_part.1.refs_7_ = f32[256,2048]{1,0:T(8,128)} custom-call(f32[16]{0:T(128)} %copy-done.25, f32[16]{0:T(128)} %copy-done.26, bf16[256,2048]{1,0:T(8,128)(2,1)} %bitcast.36, bf16[256,2048]{1,0:T(8,128)(2,1)} %bitcast.47, bf16[256,2048]{1,0:T(8,128)(2,1)} %bitcast.46), custom_call_target="tpu_custom_call" | custom-call | flops 1 | bytes 1 | tf_op jit(solution)/shard_map/local_part/pallas_call | solution.py:89
  57.7 4.8 %collective-permute-done.refs_1_ = bf16[32,2,128,128]{3,2,1,0:T(8,128)(2,1)} collective-permute-done((bf16[32,2,128,128]{3,2,1,0:T(8,128)(2,1)}, bf16[32,2,128,128]{3,2,1,0:T(8,128)(2,1)}, u32[]{:S(2)}, u32[]{:S(2)}) %collective-permute-start) | collective-permute-done | bytes 2097184 | tf_op jit(solution)/shard_map/ppermute | solution.py:245
  62.6 2.7 collective-permute-start.3
  65.2 8.0 %pack_blocks.6 = bf16[64,2,128,128]{3,2,1,0:T(8,128)(2,1)S(1)} custom-call(s32[64]{0:T(128)S(1)} %reshape.455.refs_0_, bf16[32,2,128,128]{3,2,1,0:T(8,128)(2,1)} %collective-permute-done.refs_1_, bf16[32,2,128,128]{3,2,1,0:T(8,128)(2,1)} %collective-permute-done.1.refs_2_), custom_call_target="tpu_custom_call" | custom-call | flops 49999998976 | bytes 150000000 | tf_op jit(solution)/shard_map/pack_blocks/pallas_call | solution.py:55
  75.3 5.6 %all-to-all-done.1.refs_6_ = bf16[48,2,128,128]{3,2,1,0:T(8,128)(2,1)S(1)} async-done(((bf16[48,2,128,128]{3,2,1,0:T(8,128)(2,1)}), bf16[48,2,128,128]{3,2,1,0:T(8,128)(2,1)S(1)}, u32[]{:S(2)}, u32[]{:S(2)}) %all-to-all-start.1) | async-done | bytes 3145760 | tf_op jit(solution)/shard_map/all_to_all | solution.py:233
  80.9 7.1 %all-to-all-start.2 = ((bf16[64,2,128,128]{3,2,1,0:T(8,128)(2,1)}), bf16[64,2,128,128]{3,2,1,0:T(8,128)(2,1)}, u32[]{:S(2)}, u32[]{:S(2)}) async-start(bf16[64,2,128,128]{3,2,1,0:T(8,128)(2,1)} %copy-done.12), calls=%async_computation.2 | async-start | bytes 8388608 | tf_op jit(solution)/shard_map/all_to_all | solution.py:233
  91.3 18.7 %collective-permute-done.2.refs_1_ = bf16[32,2,128,128]{3,2,1,0:T(8,128)(2,1)} collective-permute-done((bf16[32,2,128,128]{3,2,1,0:T(8,128)(2,1)}, bf16[32,2,128,128]{3,2,1,0:T(8,128)(2,1)}, u32[]{:S(2)}, u32[]{:S(2)}) %collective-permute-start.2) | collective-permute-done | bytes 2097184 | tf_op jit(solution)/shard_map/ppermute | solution.py:245
  112.7 8.1 %pack_blocks.7 = bf16[64,2,128,128]{3,2,1,0:T(8,128)(2,1)S(1)} custom-call(s32[64]{0:T(128)S(1)} %reshape.456.refs_0_, bf16[32,2,128,128]{3,2,1,0:T(8,128)(2,1)} %collective-permute-done.2.refs_1_, bf16[32,2,128,128]{3,2,1,0:T(8,128)(2,1)} %collective-permute-done.3.refs_2_), custom_call_target="tpu_custom_call" | custom-call | flops 49999998976 | bytes 150000000 | tf_op jit(solution)/shard_map/pack_blocks/pallas_call | solution.py:55
  122.8 4.0 %listed_part.5.refs_7_ = f32[256,2048]{1,0:T(8,128)S(1)} custom-call(s32[128]{0:T(128)S(1)} %select_reduce_fusion.1.refs_0_, s32[2]{0:T(128)S(1)} %get-tuple-element.67.refs_1_, s32[128]{0:T(128)S(1)} %get-tuple-element.57.refs_2_, f32[128]{0:T(128)S(1)} %multiply_subtract_fusion.refs_3_, f32[128]{0:T(128)S(1)} %get-tuple-element.55.refs_4_, ...), custom_call_target="tpu_custom_call" | custom-call | flops 1 | bytes 1 | tf_op jit(solution)/shard_map/listed_part/pallas_call | solution.py:148
  126.8 8.8 %all-to-all-done.2.refs_6_ = bf16[64,2,128,128]{3,2,1,0:T(8,128)(2,1)} async-done(((bf16[64,2,128,128]{3,2,1,0:T(8,128)(2,1)}), bf16[64,2,128,128]{3,2,1,0:T(8,128)(2,1)}, u32[]{:S(2)}, u32[]{:S(2)}) %all-to-all-start.2) | async-done | bytes 4194336 | tf_op jit(solution)/shard_map/all_to_all | solution.py:233
  135.6 9.8 %all-to-all-start.3 = ((bf16[64,2,128,128]{3,2,1,0:T(8,128)(2,1)}), bf16[64,2,128,128]{3,2,1,0:T(8,128)(2,1)}, u32[]{:S(2)}, u32[]{:S(2)}) async-start(bf16[64,2,128,128]{3,2,1,0:T(8,128)(2,1)} %copy-done.10), calls=%async_computation.3 | async-start | bytes 8388608 | tf_op jit(solution)/shard_map/all_to_all | solution.py:233
  145.4 11.1 %collective-permute-done.4.refs_1_ = bf16[32,2,128,128]{3,2,1,0:T(8,128)(2,1)} collective-permute-done((bf16[32,2,128,128]{3,2,1,0:T(8,128)(2,1)}, bf16[32,2,128,128]{3,2,1,0:T(8,128)(2,1)}, u32[]{:S(2)}, u32[]{:S(2)}) %collective-permute-start.4) | collective-permute-done | bytes 2097184 | tf_op jit(solution)/shard_map/ppermute | solution.py:245
  162.2 8.0 %pack_blocks.8 = bf16[64,2,128,128]{3,2,1,0:T(8,128)(2,1)S(1)} custom-call(s32[64]{0:T(128)S(1)} %reshape.457.refs_0_, bf16[32,2,128,128]{3,2,1,0:T(8,128)(2,1)} %collective-permute-done.4.refs_1_, bf16[32,2,128,128]{3,2,1,0:T(8,128)(2,1)} %collective-permute-done.5.refs_2_), custom_call_target="tpu_custom_call" | custom-call | flops 49999998976 | bytes 150000000 | tf_op jit(solution)/shard_map/pack_blocks/pallas_call | solution.py:55
  172.1 8.8 %listed_part.6.refs_7_ = f32[256,2048]{1,0:T(8,128)S(1)} custom-call(s32[128]{0:T(128)S(1)} %select_reduce_fusion.1.refs_0_, s32[2]{0:T(128)S(1)} %get-tuple-element.66.refs_1_, s32[128]{0:T(128)S(1)} %get-tuple-element.57.refs_2_, f32[128]{0:T(128)S(1)} %multiply_subtract_fusion.refs_3_, f32[128]{0:T(128)S(1)} %get-tuple-element.55.refs_4_, ...), custom_call_target="tpu_custom_call" | custom-call | flops 1 | bytes 1 | tf_op jit(solution)/shard_map/listed_part/pallas_call | solution.py:148
  184.2 7.3 %all-to-all-done.3.refs_6_ = bf16[64,2,128,128]{3,2,1,0:T(8,128)(2,1)} async-done(((bf16[64,2,128,128]{3,2,1,0:T(8,128)(2,1)}), bf16[64,2,128,128]{3,2,1,0:T(8,128)(2,1)}, u32[]{:S(2)}, u32[]{:S(2)}) %all-to-all-start.3) | async-done | bytes 4194336 | tf_op jit(solution)/shard_map/all_to_all | solution.py:233
  191.6 10.7 %all-to-all-start.4 = ((bf16[64,2,128,128]{3,2,1,0:T(8,128)(2,1)}), bf16[64,2,128,128]{3,2,1,0:T(8,128)(2,1)}, u32[]{:S(2)}, u32[]{:S(2)}) async-start(bf16[64,2,128,128]{3,2,1,0:T(8,128)(2,1)} %copy-done.11), calls=%async_computation.4 | async-start | bytes 8388608 | tf_op jit(solution)/shard_map/all_to_all | solution.py:233
  202.4 3.7 %pack_blocks.9 = bf16[32,2,128,128]{3,2,1,0:T(8,128)(2,1)S(1)} custom-call(s32[32]{0:T(128)S(1)} %reshape.452.refs_0_, bf16[16,2,128,128]{3,2,1,0:T(8,128)(2,1)S(1)} %copy-done.18, bf16[16,2,128,128]{3,2,1,0:T(8,128)(2,1)S(1)} %copy-done.20), custom_call_target="tpu_custom_call" | custom-call | flops 49999998976 | bytes 150000000 | tf_op jit(solution)/shard_map/pack_blocks/pallas_call | solution.py:55
  207.5 10.3 %listed_part.7.refs_7_ = f32[256,2048]{1,0:T(8,128)S(1)} custom-call(s32[128]{0:T(128)S(1)} %select_reduce_fusion.1.refs_0_, s32[2]{0:T(128)S(1)} %get-tuple-element.65.refs_1_, s32[128]{0:T(128)S(1)} %get-tuple-element.57.refs_2_, f32[128]{0:T(128)S(1)} %multiply_subtract_fusion.refs_3_, f32[128]{0:T(128)S(1)} %get-tuple-element.55.refs_4_, ...), custom_call_target="tpu_custom_call" | custom-call | flops 1 | bytes 1 | tf_op jit(solution)/shard_map/listed_part/pallas_call | solution.py:148
  219.2 29.2 %all-to-all-done.4.refs_6_ = bf16[64,2,128,128]{3,2,1,0:T(8,128)(2,1)} async-done(((bf16[64,2,128,128]{3,2,1,0:T(8,128)(2,1)}), bf16[64,2,128,128]{3,2,1,0:T(8,128)(2,1)}, u32[]{:S(2)}, u32[]{:S(2)}) %all-to-all-start.4) | async-done | bytes 4194336 | tf_op jit(solution)/shard_map/all_to_all | solution.py:233
  248.4 10.2 %all-to-all-start.5 = ((bf16[32,2,128,128]{3,2,1,0:T(8,128)(2,1)}), bf16[32,2,128,128]{3,2,1,0:T(8,128)(2,1)S(1)}, u32[]{:S(2)}, u32[]{:S(2)}) async-start(bf16[32,2,128,128]{3,2,1,0:T(8,128)(2,1)} %copy-done.14), calls=%async_computation.5 | async-start | bytes 4194304 | tf_op jit(solution)/shard_map/all_to_all | solution.py:233
  260.2 8.7 %listed_part.8.refs_7_ = f32[256,2048]{1,0:T(8,128)S(1)} custom-call(s32[128]{0:T(128)S(1)} %select_reduce_fusion.1.refs_0_, s32[2]{0:T(128)S(1)} %get-tuple-element.64.refs_1_, s32[128]{0:T(128)S(1)} %get-tuple-element.57.refs_2_, f32[128]{0:T(128)S(1)} %multiply_subtract_fusion.refs_3_, f32[128]{0:T(128)S(1)} %get-tuple-element.55.refs_4_, ...), custom_call_target="tpu_custom_call" | custom-call | flops 1 | bytes 1 | tf_op jit(solution)/shard_map/listed_part/pallas_call | solution.py:148
  270.3 13.0 %all-to-all-done.5.refs_6_ = bf16[32,2,128,128]{3,2,1,0:T(8,128)(2,1)S(1)} async-done(((bf16[32,2,128,128]{3,2,1,0:T(8,128)(2,1)}), bf16[32,2,128,128]{3,2,1,0:T(8,128)(2,1)S(1)}, u32[]{:S(2)}, u32[]{:S(2)}) %all-to-all-start.5) | async-done | bytes 2097184 | tf_op jit(solution)/shard_map/all_to_all | solution.py:233
  284.9 3.9 %listed_part.9 = bf16[256,2048]{1,0:T(8,128)(2,1)S(1)} custom-call(s32[128]{0:T(128)S(1)} %select_reduce_fusion.1.refs_0_, s32[2]{0:T(128)S(1)} %get-tuple-element.68.refs_1_, s32[128]{0:T(128)S(1)} %get-tuple-element.57.refs_2_, f32[128]{0:T(128)S(1)} %multiply_subtract_fusion.refs_3_, f32[128]{0:T(128)S(1)} %get-tuple-element.55.refs_4_, ...), custom_call_target="tpu_custom_call" | custom-call | flops 1 | bytes 1 | tf_op jit(solution)/shard_map/listed_part/pallas_call | solution.py:148
  289.8 2.8 all-gather.2.cloned.1.call-done
  292.6 4.0 %add_convert_fusion.3 = (bf16[256,1024]{1,0:T(8,128)(2,1)S(1)}, f32[256,1024]{1,0:T(8,128)S(1)}) fusion(bf16[256,2048]{1,0:T(8,128)(2,1)} %param.10, bf16[256,2048]{1,0:T(8,128)(2,1)} %copy-done.15, bf16[2048,2048]{1,0:T(8,128)(2,1)} %all-gather.2.cloned.1.call-done), kind=kOutput, calls=%fused_computation.10 | convolution fusion | flops 1074528256 | bytes 7340032 | tf_op jit(solution)/shard_map/dot_general | solution.py:279
  296.6 3.5 %add_convert_fusion.2 = (bf16[256,1024]{1,0:T(8,128)(2,1)S(1)}, f32[256,1024]{1,0:T(8,128)S(1)}) fusion(bf16[256,2048]{1,0:T(8,128)(2,1)S(1)} %copy-done.30, bf16[256,2048]{1,0:T(8,128)(2,1)S(1)} %copy-done.16, bf16[2048,2048]{1,0:T(8,128)(2,1)} %all-gather.2.cloned.1.call-done), kind=kOutput, calls=%fused_computation.9 | convolution fusion | flops 1074528256 | bytes 7340032 | tf_op jit(solution)/shard_map/dot_general | solution.py:279
  302.7 3.8 %collective-permute-done.9 = bf16[256,1024]{1,0:T(8,128)(2,1)} collective-permute-done((bf16[256,1024]{1,0:T(8,128)(2,1)S(1)}, bf16[256,1024]{1,0:T(8,128)(2,1)}, u32[]{:S(2)}, u32[]{:S(2)}) %collective-permute-start.9) | collective-permute-done | bytes 524320 | tf_op jit(solution)/shard_map/ppermute | solution.py:281
  (132 shorter events, 51.5 us)
Async XLA Ops:
  8.9 8.0 %copy-start.27 = (s32[1,2,16,4]{2,3,1,0:T(4,128)S(1)}, s32[1,2,16,4]{2,3,1,0:T(4,128)}, u32[]{:S(2)}) copy-start(s32[1,2,16,4]{2,3,1,0:T(4,128)} %param.16) | copy-start | bytes 1540
  8.9 8.5 %copy-start.31 = (s32[8]{0:T(128)S(1)}, s32[8]{0:T(128)}, u32[]{:S(2)}) copy-start(s32[8]{0:T(128)} %constant.157.clone) | copy-start | bytes 100
  8.9 17.0 %copy-start.28 = (f32[1,16]{1,0:T(1,128)S(1)}, f32[1,16]{1,0:T(1,128)}, u32[]{:S(2)}) copy-start(f32[1,16]{1,0:T(1,128)} %param.14) | copy-start | bytes 196
  8.9 17.0 %copy-start.29 = (f32[1,16]{1,0:T(1,128)S(1)}, f32[1,16]{1,0:T(1,128)}, u32[]{:S(2)}) copy-start(f32[1,16]{1,0:T(1,128)} %param.15) | copy-start | bytes 196
  8.9 17.4 %copy-start.21 = (s32[128]{0:T(128)S(1)}, s32[128]{0:T(128)}, u32[]{:S(2)}) copy-start(s32[128]{0:T(128)} %param.17) | copy-start | bytes 1540
  8.9 20.0 %copy-start.23 = (bf16[1,16,2048]{2,1,0:T(8,128)(2,1)S(1)}, bf16[1,16,2048]{2,1,0:T(8,128)(2,1)}, u32[]{:S(2)}) copy-start(bf16[1,16,2048]{2,1,0:T(8,128)(2,1)} %param.18) | copy-start | bytes 196612
  10.5 52.1 %collective-permute-start = (bf16[32,2,128,128]{3,2,1,0:T(8,128)(2,1)}, bf16[32,2,128,128]{3,2,1,0:T(8,128)(2,1)}, u32[]{:S(2)}, u32[]{:S(2)}) collective-permute-start(bf16[32,2,128,128]{3,2,1,0:T(8,128)(2,1)} %pad_maximum_fusion.refs_1_), channel_id=1, source_target_pairs={{0,16},{16,32},{32,48},{48,64},{64,80},{80,96},{96,112},{112,0},{1... | collective-permute-start | bytes 6291464 | tf_op jit(solution)/shard_map/ppermute | solution.py:245
  12.9 49.6 %collective-permute-start.1 = (bf16[32,2,128,128]{3,2,1,0:T(8,128)(2,1)}, bf16[32,2,128,128]{3,2,1,0:T(8,128)(2,1)}, u32[]{:S(2)}, u32[]{:S(2)}) collective-permute-start(bf16[32,2,128,128]{3,2,1,0:T(8,128)(2,1)} %pad_maximum_fusion.refs_1_), channel_id=1, source_target_pairs={{0,112},{16,0},{32,16},{48,32},{64,48},{80,64},{96,80},{112,96},{1... | collective-permute-start | bytes 6291464 | tf_op jit(solution)/shard_map/ppermute | solution.py:245
  18.7 13.2 %all-to-all-start = ((s32[16,8,2]{1,2,0:T(2,128)}), s32[16,8,2]{1,2,0:T(2,128)S(1)}, u32[]{:S(2)}, u32[]{:S(2)}) async-start(s32[16,8,2]{1,2,0:T(2,128)} %select_reduce_fusion), calls=%async_computation | async-start | bytes 32768 | tf_op jit(solution)/shard_map/all_to_all | solution.py:198
  25.9 13.2 %copy-start.25 = (f32[16]{0:T(128)}, f32[16]{0:T(128)S(1)}, u32[]{:S(2)}) copy-start(f32[16]{0:T(128)S(1)} %get-tuple-element.73.refs_0_) | copy-start | bytes 196
  25.9 13.2 %copy-start.26 = (f32[16]{0:T(128)}, f32[16]{0:T(128)S(1)}, u32[]{:S(2)}) copy-start(f32[16]{0:T(128)S(1)} %get-tuple-element.74.refs_1_) | copy-start | bytes 196
  40.8 40.1 %all-to-all-start.1 = ((bf16[48,2,128,128]{3,2,1,0:T(8,128)(2,1)}), bf16[48,2,128,128]{3,2,1,0:T(8,128)(2,1)S(1)}, u32[]{:S(2)}, u32[]{:S(2)}) async-start(bf16[48,2,128,128]{3,2,1,0:T(8,128)(2,1)} %copy-done.13), calls=%async_computation.1 | async-start | bytes 6291456 | tf_op jit(solution)/shard_map/all_to_all | solution.py:233
  62.6 47.4 %collective-permute-start.2 = (bf16[32,2,128,128]{3,2,1,0:T(8,128)(2,1)}, bf16[32,2,128,128]{3,2,1,0:T(8,128)(2,1)}, u32[]{:S(2)}, u32[]{:S(2)}) collective-permute-start(bf16[32,2,128,128]{3,2,1,0:T(8,128)(2,1)} %collective-permute-done.refs_1_), channel_id=1, source_target_pairs={{0,16},{16,32},{32,48},{48,64},{64,80},{80,96},{96,112},{112,0},{1... | collective-permute-start | bytes 6291464 | tf_op jit(solution)/shard_map/ppermute | solution.py:245
  62.6 47.4 %collective-permute-start.3 = (bf16[32,2,128,128]{3,2,1,0:T(8,128)(2,1)}, bf16[32,2,128,128]{3,2,1,0:T(8,128)(2,1)}, u32[]{:S(2)}, u32[]{:S(2)}) collective-permute-start(bf16[32,2,128,128]{3,2,1,0:T(8,128)(2,1)} %collective-permute-done.1.refs_2_), channel_id=1, source_target_pairs={{0,112},{16,0},{32,16},{48,32},{64,48},{80,64},{96,80},{112,96},{1... | collective-permute-start | bytes 6291464 | tf_op jit(solution)/shard_map/ppermute | solution.py:245
  80.9 7.1 %copy-start.1 = (bf16[48,2,128,128]{3,2,1,0:T(8,128)(2,1)}, bf16[48,2,128,128]{3,2,1,0:T(8,128)(2,1)S(1)}, u32[]{:S(2)}) copy-start(bf16[48,2,128,128]{3,2,1,0:T(8,128)(2,1)S(1)} %all-to-all-done.1.refs_6_) | copy-start | bytes 9437188
  80.9 54.7 %all-to-all-start.2 = ((bf16[64,2,128,128]{3,2,1,0:T(8,128)(2,1)}), bf16[64,2,128,128]{3,2,1,0:T(8,128)(2,1)}, u32[]{:S(2)}, u32[]{:S(2)}) async-start(bf16[64,2,128,128]{3,2,1,0:T(8,128)(2,1)} %copy-done.12), calls=%async_computation.2 | async-start | bytes 8388608 | tf_op jit(solution)/shard_map/all_to_all | solution.py:233
  91.3 31.5 %copy-start = (bf16[1,256,2048]{2,1,0:T(8,128)(2,1)S(1)}, bf16[1,256,2048]{2,1,0:T(8,128)(2,1)}, u32[]{:S(2)}) copy-start(bf16[1,256,2048]{2,1,0:T(8,128)(2,1)} %param.11) | copy-start | bytes 3145732
  91.3 31.5 %copy-start.3 = (f32[256,2048]{1,0:T(8,128)S(1)}, f32[256,2048]{1,0:T(8,128)}, u32[]{:S(2)}) copy-start(f32[256,2048]{1,0:T(8,128)} %local_part.1.refs_7_) | copy-start | bytes 6291460
  110.0 46.5 %collective-permute-start.4 = (bf16[32,2,128,128]{3,2,1,0:T(8,128)(2,1)}, bf16[32,2,128,128]{3,2,1,0:T(8,128)(2,1)}, u32[]{:S(2)}, u32[]{:S(2)}) collective-permute-start(bf16[32,2,128,128]{3,2,1,0:T(8,128)(2,1)} %collective-permute-done.2.refs_1_), channel_id=1, source_target_pairs={{0,16},{16,32},{32,48},{48,64},{64,80},{80,96},{96,112},{112,0},{1... | collective-permute-start | bytes 6291464 | tf_op jit(solution)/shard_map/ppermute | solution.py:245
  110.9 45.6 %collective-permute-start.5 = (bf16[32,2,128,128]{3,2,1,0:T(8,128)(2,1)}, bf16[32,2,128,128]{3,2,1,0:T(8,128)(2,1)}, u32[]{:S(2)}, u32[]{:S(2)}) collective-permute-start(bf16[32,2,128,128]{3,2,1,0:T(8,128)(2,1)} %collective-permute-done.3.refs_2_), channel_id=1, source_target_pairs={{0,112},{16,0},{32,16},{48,32},{64,48},{80,64},{96,80},{112,96},{1... | collective-permute-start | bytes 6291464 | tf_op jit(solution)/shard_map/ppermute | solution.py:245
  112.7 10.2 %copy-start.2 = (bf16[48,2,128,128]{3,2,1,0:T(8,128)(2,1)S(1)}, bf16[48,2,128,128]{3,2,1,0:T(8,128)(2,1)}, u32[]{:S(2)}) copy-start(bf16[48,2,128,128]{3,2,1,0:T(8,128)(2,1)} %copy-done.1) | copy-start | bytes 9437188
  135.6 55.9 %all-to-all-start.3 = ((bf16[64,2,128,128]{3,2,1,0:T(8,128)(2,1)}), bf16[64,2,128,128]{3,2,1,0:T(8,128)(2,1)}, u32[]{:S(2)}, u32[]{:S(2)}) async-start(bf16[64,2,128,128]{3,2,1,0:T(8,128)(2,1)} %copy-done.10), calls=%async_computation.3 | async-start | bytes 8388608 | tf_op jit(solution)/shard_map/all_to_all | solution.py:233
  145.4 147.2 %all-gather.2.cloned.1.call-start = ((), (), s32[]{:S(2)}) async-start(), calls=%async_computation.6 | async-start | bytes 9437184 | tf_op jit(solution)/shard_map/all_gather | solution.py:266
  157.8 24.4 %collective-permute-start.6 = (bf16[16,2,128,128]{3,2,1,0:T(8,128)(2,1)S(1)}, bf16[16,2,128,128]{3,2,1,0:T(8,128)(2,1)S(1)}, u32[]{:S(2)}, u32[]{:S(2)}) collective-permute-start(bf16[16,2,128,128]{3,2,1,0:T(8,128)(2,1)S(1)} %slice.58), channel_id=1, source_target_pairs={{0,16},{16,32},{32,48},{48,64},{64,80},{80,96},{96,112},{112,0},{1... | collective-permute-start | bytes 3145736 | tf_op jit(solution)/shard_map/ppermute | solution.py:245
  159.9 23.4 %collective-permute-start.7 = (bf16[16,2,128,128]{3,2,1,0:T(8,128)(2,1)S(1)}, bf16[16,2,128,128]{3,2,1,0:T(8,128)(2,1)S(1)}, u32[]{:S(2)}, u32[]{:S(2)}) collective-permute-start(bf16[16,2,128,128]{3,2,1,0:T(8,128)(2,1)S(1)} %slice.59), channel_id=1, source_target_pairs={{0,112},{16,0},{32,16},{48,32},{64,48},{80,64},{96,80},{112,96},{1... | collective-permute-start | bytes 3145736 | tf_op jit(solution)/shard_map/ppermute | solution.py:245
  172.1 19.4 %copy-start.24 = (s32[16,2]{1,0:T(8,128)S(1)}, s32[16,2]{1,0:T(8,128)}, u32[]{:S(2)}) copy-start(s32[16,2]{1,0:T(8,128)} %get-tuple-element.52) | copy-start | bytes 388
  191.6 10.8 %copy-start.18 = (bf16[16,2,128,128]{3,2,1,0:T(8,128)(2,1)S(1)}, bf16[16,2,128,128]{3,2,1,0:T(8,128)(2,1)}, u32[]{:S(2)}) copy-start(bf16[16,2,128,128]{3,2,1,0:T(8,128)(2,1)} %copy-done.17) | copy-start | bytes 3145732
  191.6 10.8 %copy-start.20 = (bf16[16,2,128,128]{3,2,1,0:T(8,128)(2,1)S(1)}, bf16[16,2,128,128]{3,2,1,0:T(8,128)(2,1)}, u32[]{:S(2)}) copy-start(bf16[16,2,128,128]{3,2,1,0:T(8,128)(2,1)} %copy-done.19) | copy-start | bytes 3145732
  191.6 56.7 %all-to-all-start.4 = ((bf16[64,2,128,128]{3,2,1,0:T(8,128)(2,1)}), bf16[64,2,128,128]{3,2,1,0:T(8,128)(2,1)}, u32[]{:S(2)}, u32[]{:S(2)}) async-start(bf16[64,2,128,128]{3,2,1,0:T(8,128)(2,1)} %copy-done.11), calls=%async_computation.4 | async-start | bytes 8388608 | tf_op jit(solution)/shard_map/all_to_all | solution.py:233
  248.4 35.0 %all-to-all-start.5 = ((bf16[32,2,128,128]{3,2,1,0:T(8,128)(2,1)}), bf16[32,2,128,128]{3,2,1,0:T(8,128)(2,1)S(1)}, u32[]{:S(2)}, u32[]{:S(2)}) async-start(bf16[32,2,128,128]{3,2,1,0:T(8,128)(2,1)} %copy-done.14), calls=%async_computation.5 | async-start | bytes 4194304 | tf_op jit(solution)/shard_map/all_to_all | solution.py:233
  300.1 6.4 %collective-permute-start.9 = (bf16[256,1024]{1,0:T(8,128)(2,1)S(1)}, bf16[256,1024]{1,0:T(8,128)(2,1)}, u32[]{:S(2)}, u32[]{:S(2)}) collective-permute-start(bf16[256,1024]{1,0:T(8,128)(2,1)S(1)} %get-tuple-element.71), channel_id=1, source_target_pairs={{0,128},{1,129},{2,130},{3,131},{4,132},{5,133},{6,134},{7,135},{8... | collective-permute-start | bytes 1572872 | tf_op jit(solution)/shard_map/ppermute | solution.py:281
  301.4 7.2 %collective-permute-start.8 = (bf16[256,1024]{1,0:T(8,128)(2,1)S(1)}, bf16[256,1024]{1,0:T(8,128)(2,1)}, u32[]{:S(2)}, u32[]{:S(2)}) collective-permute-start(bf16[256,1024]{1,0:T(8,128)(2,1)S(1)} %get-tuple-element.69), channel_id=1, source_target_pairs={{0,128},{1,129},{2,130},{3,131},{4,132},{5,133},{6,134},{7,135},{8... | collective-permute-start | bytes 1572872 | tf_op jit(solution)/shard_map/ppermute | solution.py:281
  (17 other events, 34.2 us)
Sparse Core Ops, SparseCore 0:
  191.6 100.9 all-gather.1

commit v5 on v4

--- a/solution.py
+++ b/solution.py
@@ -1,3 +1,5 @@
+import functools
+
 import jax
 import jax.numpy as jnp
 from jax import lax
@@ -11,6 +13,7 @@
 CHUNKS = ((0,), (-1, 1), (-2, 2), (-3, 3), (4,))
 ORDER = sum(CHUNKS, ())
 LIGHT = pl.CostEstimate(flops=1, bytes_accessed=1, transcendentals=0)
+LONG = pl.CostEstimate(flops=100_000_000_000, bytes_accessed=150_000_000, transcendentals=0)
 HEAVY = pl.CostEstimate(flops=50_000_000_000, bytes_accessed=150_000_000, transcendentals=0)
 
 
@@ -97,17 +100,17 @@
     )(offsets, slopes, q, k, v)
 
 
-GROUP = 8
-
-
-def listed_kernel(
-    scale, heads, listed, order_ref, bound_ref, slot_ref, near_ref, far_ref, q_ref, got_ref,
-    acc_ref, out_ref, total
+GROUP = 4
+PARTS = 8
+TILE = 256
+
+
+def add_listed(
+    scale, heads, listed, order_ref, bound_ref, slot_ref, near_ref, far_ref, q_ref, got_ref, total
 ):
     blk, head_size = got_ref.shape[2:]
     items = order_ref.shape[0]
     begin, end = bound_ref[0], bound_ref[1]
-    total[...] = acc_ref[...]
 
     @pl.loop(0, (end - begin + GROUP - 1) // GROUP)
     def _(group):
@@ -138,23 +141,106 @@
             def _(at=at, part=part):
                 total[at] += part
 
-    out_ref[...] = total[...].astype(out_ref.dtype)
-
-
-def listed_part(order, bounds, slot, near, far, q, got, acc, heads, listed, dtype):
+
+def listed_kernel(sizes, *refs):
+    acc_ref, out_ref, total = refs[-3:]
+    total[...] = acc_ref[...]
+    add_listed(*sizes, *refs[:-3], total)
+    out_ref[...] = total[...]
+
+
+def listed_part(order, bounds, slot, near, far, q, got, acc, heads, listed, hint):
     tokens, width = q.shape
     smem = pl.BlockSpec(memory_space=pltpu.SMEM)
     vmem = pl.BlockSpec(memory_space=pltpu.VMEM)
     return pl.pallas_call(
-        lambda *refs: listed_kernel((width // heads) ** (-0.5), heads, listed, *refs),
-        out_shape=jax.ShapeDtypeStruct((tokens, width), dtype),
+        lambda *refs: listed_kernel(((width // heads) ** (-0.5), heads, listed), *refs),
+        out_shape=jax.ShapeDtypeStruct((tokens, width), jnp.float32),
         in_specs=[smem] * 5 + [vmem] * 3,
         out_specs=vmem,
         scratch_shapes=[pltpu.VMEM((tokens, width), jnp.float32)],
-        compiler_params=pltpu.CompilerParams(vmem_limit_bytes=32 * 1024 * 1024),
-        cost_estimate=LIGHT,
+        compiler_params=pltpu.CompilerParams(vmem_limit_bytes=60 * 1024 * 1024),
+        cost_estimate=hint,
         name="listed_part",
     )(order, bounds, slot, near, far, q, got, acc)
+
+
+def weight_copies(weight_ref, held, sems, skip):
+    rows = held.shape[0] // PARTS
+    return [
+        pltpu.make_async_copy(
+            weight_ref.at[n * rows:(n + 1) * rows, skip:skip + held.shape[1]],
+            held.at[n * rows:(n + 1) * rows, :],
+            sems.at[n],
+        )
+        for n in range(PARTS)
+    ]
+
+
+def project_columns(skip, copies, segment_ref, attended_ref, residual_ref, base_ref, first_ref, held):
+    for copy in copies:
+        copy.wait()
+    for n in range(0, held.shape[1], TILE):
+        base = jnp.dot(attended_ref[...], held[:, n:n + TILE], preferred_element_type=jnp.float32)
+        residual = residual_ref[:, skip + n:skip + n + TILE].astype(jnp.float32)
+        base = base + jnp.where(segment_ref[0] == 0, residual, 0.0)
+        base_ref[:, n:n + TILE] = base
+        first_ref[:, n:n + TILE] = base.astype(first_ref.dtype)
+
+
+def last_kernel(skip, sizes, *refs):
+    acc_ref, segment_ref, weight_ref, residual_ref = refs[7:11]
+    attended_ref, base_ref, first_ref, total, held, sems = refs[11:]
+    copies = weight_copies(weight_ref, held, sems, skip)
+    for copy in copies:
+        copy.start()
+    total[...] = acc_ref[...]
+    add_listed(*sizes, *refs[:7], total)
+    attended_ref[...] = total[...].astype(attended_ref.dtype)
+    project_columns(
+        skip, copies, segment_ref, attended_ref, residual_ref, base_ref, first_ref, held
+    )
+
+
+def next_kernel(skip, attended_ref, segment_ref, weight_ref, residual_ref, base_ref, first_ref, held, sems):
+    copies = weight_copies(weight_ref, held, sems, skip)
+    for copy in copies:
+        copy.start()
+    project_columns(
+        skip, copies, segment_ref, attended_ref, residual_ref, base_ref, first_ref, held
+    )
+
+
+def project(part, cut, segment, weight, residual, attended=None, pieces=None, sizes=None):
+    tokens, width = residual.shape
+    skip = part * cut
+    smem = pl.BlockSpec(memory_space=pltpu.SMEM)
+    vmem = pl.BlockSpec(memory_space=pltpu.VMEM)
+    out_shape = [
+        jax.ShapeDtypeStruct((tokens, cut), jnp.float32),
+        jax.ShapeDtypeStruct((tokens, cut), residual.dtype),
+    ]
+    scratch = [
+        pltpu.VMEM((width, cut), weight.dtype),
+        pltpu.SemaphoreType.DMA((PARTS,)),
+    ]
+    if pieces is None:
+        kernel, operands, in_specs = functools.partial(next_kernel, skip), (attended,), [vmem]
+    else:
+        kernel, operands = functools.partial(last_kernel, skip, sizes), pieces
+        in_specs = [smem] * 5 + [vmem] * 3
+        scratch.insert(0, pltpu.VMEM((tokens, width), jnp.float32))
+        out_shape.insert(0, jax.ShapeDtypeStruct((tokens, width), residual.dtype))
+    return pl.pallas_call(
+        kernel,
+        out_shape=out_shape,
+        in_specs=in_specs + [smem, pl.BlockSpec(memory_space=pl.ANY), vmem],
+        out_specs=[vmem] * len(out_shape),
+        scratch_shapes=scratch,
+        compiler_params=pltpu.CompilerParams(vmem_limit_bytes=60 * 1024 * 1024),
+        cost_estimate=LONG if pieces else LIGHT,
+        name="project",
+    )(*operands, segment, weight, residual)
 
 
 def after(x, *others):
@@ -235,10 +321,11 @@
     def chosen(n, *sources, cut=0, extra=None):
         return pack(part_of(selected, n), sources, cut, extra)
 
-    def added(n, got, acc, dtype=jnp.float32):
+    def added(n, got, acc):
         bounds = edges[n:n + 2]
         return listed_part(
-            order, bounds, slot, near_item, far_item, q, got, acc, heads, listed, dtype
+            order, bounds, slot, near_item, far_item, q, got, acc, heads, listed,
+            LONG if n > 2 else LIGHT,
         )
 
     def step(pair):
@@ -258,30 +345,32 @@
             weight = got.reshape((PLANE, slots + 1) + kv.shape[1:])[:, slots]
             weight = weight.reshape(-1, width)
         if n == 3:
-            later = after(later, acc)
-            packed = after(packed, later)
+            weight = lax.all_gather(after(weight, ring), "z", axis=0, tiled=True)
         before, sent = got, after(packed, got)
         got = served(sent)
         ring = after(later, sent, acc)
-    weight = lax.all_gather(after(weight, ring), "z", axis=0, tiled=True)
     packed = chosen(4, *ring, cut=half)
     acc = added(2, before, after(acc, packed))
     sent = after(packed, got, acc)
     acc = added(3, got, after(acc, sent))
-    attended = added(4, served(sent), acc, jnp.bfloat16)
-
-    first, latter = [], []
+    last = served(sent)
+
     cut = width // 2
-    for n in range(2):
-        columns = slice(n * cut, (n + 1) * cut)
-        if n:
-            attended = after(attended, first[-1])
-        projected = jnp.dot(attended, weight[:, columns], preferred_element_type=jnp.float32)
-        first.append((residual_in[:, columns].astype(jnp.float32) + projected).astype(jnp.bfloat16))
-        handed = lax.ppermute(first[-1], "segment", [(0, 1)])
-        latter.append((handed.astype(jnp.float32) + projected).astype(jnp.bfloat16))
-    first, latter = jnp.concatenate(first, axis=1), jnp.concatenate(latter, axis=1)
-    return jnp.where(lax.axis_index("segment") == 0, first, latter)[None]
+    segment = lax.axis_index("segment").reshape(1)
+    pieces = (order, edges[4:6], slot, near_item, far_item, q, last, acc)
+    sizes = (head_size ** (-0.5), heads, listed)
+    attended, left, sent = project(
+        0, cut, segment, weight, residual_in, pieces=pieces, sizes=sizes
+    )
+    left_handed = lax.ppermute(sent, "segment", [(0, 1)])
+    attended = after(attended, sent)
+    right = jnp.dot(attended, weight[:, cut:], preferred_element_type=jnp.float32)
+    residual = residual_in[:, cut:].astype(jnp.float32)
+    right = right + jnp.where(segment == 0, residual, 0.0)
+    right_handed = lax.ppermute(right.astype(jnp.bfloat16), "segment", [(0, 1)])
+    handed = ((left_handed, left), (right_handed, right))
+    out = [(part.astype(jnp.float32) + rest).astype(jnp.bfloat16) for part, rest in handed]
+    return jnp.concatenate(out, axis=1)[None]
 
 
 def solution(mesh):

time: 321 us -> 314 us (0.978)
  Pallas kernels: 81.5 us -> 92.9 us
  local copies, waits for them, and re-layouts: 32.6 us -> 23.6 us
  matrix products: 7.48 us -> 3.82 us
    pallas_call x5, Pallas kernels: 35.8 us -> 53.2 us  [the longest x4 43.5 us: listed_part(): pl.pallas_call(lambda *refs: listed_kernel(((width // heads) ** (-0.5), h...]
    ppermute x8, waiting for transfers between devices: 34.6 us -> 44.9 us  [step(): return (lax.ppermute(pair[0], 'z', up), lax.ppermute(pair[1], 'z', down))]
    unnamed x66 -> x39, local copies, waits for them, and re-layouts: 21 us -> 13.4 us
    all_to_all x5, waiting for transfers between devices: 63.8 us -> 56.8 us  [served(): lax.all_to_all(sent, ('x', 'y'), split_axis=0, concat_axis=0, tiled=True)]
    pallas_call x5, Pallas kernels: 33.7 us -> 27.5 us  [pack(): pl.pallas_call(lambda *refs: pack_kernel(slots, half, len(extras), *refs)...]
    dot_general x2 -> x1, matrix products: 7.48 us -> 3.82 us  [per_device(): jnp.dot(attended, weight[:, cut:], preferred_element_type=jnp.float32)]
  transfers between devices with their start and end apart: 17 -> 17, of which waited for: 12 -> 10; matrix products, arithmetic and copies ran while one was open for 4% -> 5% of each run, Pallas kernels for 26% -> 27%
where the time goes in v5:
time: 314 us; the launch traced here: 313 us
  waiting for transfers between devices  109 us (35%)
  Pallas kernels  92.9 us (30%)
  starting transfers between devices  63.1 us (20%)
  local copies, waits for them, and re-layouts  23.6 us (8%)
  between operations  14.5 us (5%)
  other arithmetic  5.57 us (2%)
  matrix products  3.82 us (1%)
    all_to_all x5, waiting for transfers between devices, served(): lax.all_to_all(sent, ('x', 'y'), split_axis=0, concat_axis=0, tiled=True)  56.8 us
    ppermute x8, waiting for transfers between devices, step(): return (lax.ppermute(pair[0], 'z', up), lax.ppermute(pair[1], 'z', down))  44.9 us
    pallas_call x4, Pallas kernels, listed_part(): pl.pallas_call(lambda *refs: listed_kernel(((width // heads) ** (-0.5), h...  43.5 us
    all_to_all x5, starting transfers between devices, served(): lax.all_to_all(sent, ('x', 'y'), split_axis=0, concat_axis=0, tiled=True)  39 us
    pallas_call x5, Pallas kernels, pack(): pl.pallas_call(lambda *refs: pack_kernel(slots, half, len(extras), *refs)...  27.5 us
    ppermute x8, starting transfers between devices, step(): return (lax.ppermute(pair[0], 'z', up), lax.ppermute(pair[1], 'z', down))  14.6 us
    unnamed x39, local copies, waits for them, and re-layouts  13.4 us
    pallas_call x1, Pallas kernels, local_part(): pl.pallas_call(lambda *refs: local_kernel(head_size ** (-0.5), *refs), gr...  12.1 us
  transfers between devices with their start and end apart: 17, of which 10 were waited for; matrix products, arithmetic and copies ran while one was open for 5% of the time, Pallas kernels for 27%

profile of v5, /device:TPU:1, one launch (start us, length us, event | category | flops | bytes accessed | tf_op | source)
XLA Modules:
  0.0 312.6 jit_solution(11874918085144556586)
XLA Ops:
  9.2 2.5 collective-permute-start
  11.7 4.0 %collective-permute-start.1 = (bf16[32,2,128,128]{3,2,1,0:T(8,128)(2,1)S(1)}, bf16[32,2,128,128]{3,2,1,0:T(8,128)(2,1)}, u32[]{:S(2)}, u32[]{:S(2)}) collective-permute-start(bf16[32,2,128,128]{3,2,1,0:T(8,128)(2,1)S(1)} %pad_maximum_fusion.refs_1_), channel_id=1, source_target_pairs={{0,112},{16,0},{32,16},{48,32},{64,48},{80,64},{96,80},{112,96},{1... | collective-permute-start | bytes 6291464 | tf_op jit(solution)/shard_map/ppermute | solution.py:332
  18.1 6.8 %all-to-all-start = ((s32[16,8,2]{1,2,0:T(2,128)}), s32[16,8,2]{1,2,0:T(2,128)S(1)}, u32[]{:S(2)}, u32[]{:S(2)}) async-start(s32[16,8,2]{1,2,0:T(2,128)} %select_reduce_fusion), calls=%async_computation | async-start | bytes 32768 | tf_op jit(solution)/shard_map/all_to_all | solution.py:284
  32.0 2.2 pack_blocks.5
  34.3 5.8 %all-to-all-start.1 = ((bf16[48,2,128,128]{3,2,1,0:T(8,128)(2,1)}), bf16[48,2,128,128]{3,2,1,0:T(8,128)(2,1)}, u32[]{:S(2)}, u32[]{:S(2)}) async-start(bf16[48,2,128,128]{3,2,1,0:T(8,128)(2,1)} %pack_blocks.5), calls=%async_computation.1 | async-start | bytes 6291456 | tf_op jit(solution)/shard_map/all_to_all | solution.py:319
  40.1 12.1 %local_part.1.refs_7_ = f32[256,2048]{1,0:T(8,128)} custom-call(f32[16]{0:T(128)} %copy-done.10, f32[16]{0:T(128)} %copy-done.11, bf16[256,2048]{1,0:T(8,128)(2,1)} %bitcast.37, bf16[256,2048]{1,0:T(8,128)(2,1)} %bitcast.47, bf16[256,2048]{1,0:T(8,128)(2,1)} %bitcast.46), custom_call_target="tpu_custom_call" | custom-call | flops 1 | bytes 1 | tf_op jit(solution)/shard_map/local_part/pallas_call | solution.py:92
  53.4 7.7 %collective-permute-done.refs_1_ = bf16[32,2,128,128]{3,2,1,0:T(8,128)(2,1)} collective-permute-done((bf16[32,2,128,128]{3,2,1,0:T(8,128)(2,1)S(1)}, bf16[32,2,128,128]{3,2,1,0:T(8,128)(2,1)}, u32[]{:S(2)}, u32[]{:S(2)}) %collective-permute-start) | collective-permute-done | bytes 2097184 | tf_op jit(solution)/shard_map/ppermute | solution.py:332
  61.1 2.7 collective-permute-start.3
  63.8 8.0 %pack_blocks.6 = bf16[64,2,128,128]{3,2,1,0:T(8,128)(2,1)S(1)} custom-call(s32[64]{0:T(128)S(1)} %reshape.404.refs_0_, bf16[32,2,128,128]{3,2,1,0:T(8,128)(2,1)} %collective-permute-done.refs_1_, bf16[32,2,128,128]{3,2,1,0:T(8,128)(2,1)} %collective-permute-done.1.refs_2_), custom_call_target="tpu_custom_call" | custom-call | flops 49999998976 | bytes 150000000 | tf_op jit(solution)/shard_map/pack_blocks/pallas_call | solution.py:58
  73.7 5.3 %all-to-all-done.1.refs_6_ = bf16[48,2,128,128]{3,2,1,0:T(8,128)(2,1)} async-done(((bf16[48,2,128,128]{3,2,1,0:T(8,128)(2,1)}), bf16[48,2,128,128]{3,2,1,0:T(8,128)(2,1)}, u32[]{:S(2)}, u32[]{:S(2)}) %all-to-all-start.1) | async-done | bytes 3145760 | tf_op jit(solution)/shard_map/all_to_all | solution.py:319
  79.1 4.6 %all-to-all-start.2 = ((bf16[64,2,128,128]{3,2,1,0:T(8,128)(2,1)}), bf16[64,2,128,128]{3,2,1,0:T(8,128)(2,1)}, u32[]{:S(2)}, u32[]{:S(2)}) async-start(bf16[64,2,128,128]{3,2,1,0:T(8,128)(2,1)} %copy-done.1), calls=%async_computation.2 | async-start | bytes 8388608 | tf_op jit(solution)/shard_map/all_to_all | solution.py:319
  86.3 22.3 %collective-permute-done.2.refs_1_ = bf16[32,2,128,128]{3,2,1,0:T(8,128)(2,1)S(1)} collective-permute-done((bf16[32,2,128,128]{3,2,1,0:T(8,128)(2,1)}, bf16[32,2,128,128]{3,2,1,0:T(8,128)(2,1)S(1)}, u32[]{:S(2)}, u32[]{:S(2)}) %collective-permute-start.2) | collective-permute-done | bytes 2097184 | tf_op jit(solution)/shard_map/ppermute | solution.py:332
  109.9 2.7 collective-permute-start.5
  114.2 7.3 %pack_blocks.7 = bf16[64,2,128,128]{3,2,1,0:T(8,128)(2,1)S(1)} custom-call(s32[64]{0:T(128)S(1)} %reshape.405.refs_0_, bf16[32,2,128,128]{3,2,1,0:T(8,128)(2,1)S(1)} %copy-done.4, bf16[32,2,128,128]{3,2,1,0:T(8,128)(2,1)} %collective-permute-done.3.refs_2_), custom_call_target="tpu_custom_call" | custom-call | flops 49999998976 | bytes 150000000 | tf_op jit(solution)/shard_map/pack_blocks/pallas_call | solution.py:58
  123.5 8.7 %listed_part.4.refs_7_ = f32[256,2048]{1,0:T(8,128)} custom-call(s32[128]{0:T(128)} %select_reduce_fusion.1.refs_0_, s32[2]{0:T(128)} %get-tuple-element.67.refs_1_, s32[128]{0:T(128)} %get-tuple-element.57.refs_2_, f32[128]{0:T(128)} %multiply_subtract_fusion.refs_3_, f32[128]{0:T(128)} %get-tuple-element.55.refs_4_, bf16[256,2048]{1,0:T(8,128)(2,1)} %bitcast.38, ...), custom_call_target="tpu_custom_call" | custom-call | flops 1 | bytes 1 | tf_op jit(solution)/shard_map/listed_part/pallas_call | solution.py:156
  132.2 9.4 %all-to-all-start.3 = ((bf16[64,2,128,128]{3,2,1,0:T(8,128)(2,1)}), bf16[64,2,128,128]{3,2,1,0:T(8,128)(2,1)}, u32[]{:S(2)}, u32[]{:S(2)}) async-start(bf16[64,2,128,128]{3,2,1,0:T(8,128)(2,1)} %copy-done), calls=%async_computation.3 | async-start | bytes 8388608 | tf_op jit(solution)/shard_map/all_to_all | solution.py:319
  141.6 14.9 %collective-permute-done.4.refs_1_ = bf16[32,2,128,128]{3,2,1,0:T(8,128)(2,1)S(1)} collective-permute-done((bf16[32,2,128,128]{3,2,1,0:T(8,128)(2,1)}, bf16[32,2,128,128]{3,2,1,0:T(8,128)(2,1)S(1)}, u32[]{:S(2)}, u32[]{:S(2)}) %collective-permute-start.4) | collective-permute-done | bytes 2097184 | tf_op jit(solution)/shard_map/ppermute | solution.py:332
  157.5 2.3 slice.52
  159.9 2.7 collective-permute-start.7
  162.6 7.3 %pack_blocks.8 = bf16[64,2,128,128]{3,2,1,0:T(8,128)(2,1)S(1)} custom-call(s32[64]{0:T(128)S(1)} %reshape.406.refs_0_, bf16[32,2,128,128]{3,2,1,0:T(8,128)(2,1)S(1)} %collective-permute-done.4.refs_1_, bf16[32,2,128,128]{3,2,1,0:T(8,128)(2,1)} %collective-permute-done.5.refs_2_), custom_call_target="tpu_custom_call" | custom-call | flops 49999998976 | bytes 150000000 | tf_op jit(solution)/shard_map/pack_blocks/pallas_call | solution.py:58
  172.0 10.7 %listed_part.5.refs_7_ = f32[256,2048]{1,0:T(8,128)} custom-call(s32[128]{0:T(128)} %select_reduce_fusion.1.refs_0_, s32[2]{0:T(128)} %get-tuple-element.66.refs_1_, s32[128]{0:T(128)} %get-tuple-element.57.refs_2_, f32[128]{0:T(128)} %multiply_subtract_fusion.refs_3_, f32[128]{0:T(128)} %get-tuple-element.55.refs_4_, bf16[256,2048]{1,0:T(8,128)(2,1)} %bitcast.39, ...), custom_call_target="tpu_custom_call" | custom-call | flops 1 | bytes 1 | tf_op jit(solution)/shard_map/listed_part/pallas_call | solution.py:156
  182.7 6.1 %all-to-all-done.3.refs_6_ = bf16[64,2,128,128]{3,2,1,0:T(8,128)(2,1)} async-done(((bf16[64,2,128,128]{3,2,1,0:T(8,128)(2,1)}), bf16[64,2,128,128]{3,2,1,0:T(8,128)(2,1)}, u32[]{:S(2)}, u32[]{:S(2)}) %all-to-all-start.3) | async-done | bytes 4194336 | tf_op jit(solution)/shard_map/all_to_all | solution.py:319
  188.8 8.9 %all-to-all-start.4 = ((bf16[64,2,128,128]{3,2,1,0:T(8,128)(2,1)}), bf16[64,2,128,128]{3,2,1,0:T(8,128)(2,1)}, u32[]{:S(2)}, u32[]{:S(2)}) async-start(bf16[64,2,128,128]{3,2,1,0:T(8,128)(2,1)} %copy-done.2), calls=%async_computation.4 | async-start | bytes 8388608 | tf_op jit(solution)/shard_map/all_to_all | solution.py:319
  197.8 2.6 pack_blocks.9
  200.4 12.5 %listed_part.6.refs_7_ = f32[256,2048]{1,0:T(8,128)} custom-call(s32[128]{0:T(128)} %select_reduce_fusion.1.refs_0_, s32[2]{0:T(128)} %get-tuple-element.65.refs_1_, s32[128]{0:T(128)} %get-tuple-element.57.refs_2_, f32[128]{0:T(128)} %multiply_subtract_fusion.refs_3_, f32[128]{0:T(128)} %get-tuple-element.55.refs_4_, bf16[256,2048]{1,0:T(8,128)(2,1)} %bitcast.40, ...), custom_call_target="tpu_custom_call" | custom-call | flops 1 | bytes 1 | tf_op jit(solution)/shard_map/listed_part/pallas_call | solution.py:156
  212.9 31.8 %all-to-all-done.4.refs_6_ = bf16[64,2,128,128]{3,2,1,0:T(8,128)(2,1)} async-done(((bf16[64,2,128,128]{3,2,1,0:T(8,128)(2,1)}), bf16[64,2,128,128]{3,2,1,0:T(8,128)(2,1)}, u32[]{:S(2)}, u32[]{:S(2)}) %all-to-all-start.4) | async-done | bytes 4194336 | tf_op jit(solution)/shard_map/all_to_all | solution.py:319
  244.7 10.4 %all-to-all-start.5 = ((bf16[32,2,128,128]{3,2,1,0:T(8,128)(2,1)}), bf16[32,2,128,128]{3,2,1,0:T(8,128)(2,1)S(1)}, u32[]{:S(2)}, u32[]{:S(2)}) async-start(bf16[32,2,128,128]{3,2,1,0:T(8,128)(2,1)} %pack_blocks.9), calls=%async_computation.5 | async-start | bytes 4194304 | tf_op jit(solution)/shard_map/all_to_all | solution.py:319
  255.0 11.5 %listed_part.7.refs_7_ = f32[256,2048]{1,0:T(8,128)} custom-call(s32[128]{0:T(128)} %select_reduce_fusion.1.refs_0_, s32[2]{0:T(128)} %get-tuple-element.64.refs_1_, s32[128]{0:T(128)} %get-tuple-element.57.refs_2_, f32[128]{0:T(128)} %multiply_subtract_fusion.refs_3_, f32[128]{0:T(128)} %get-tuple-element.55.refs_4_, bf16[256,2048]{1,0:T(8,128)(2,1)} %bitcast.41, ...), custom_call_target="tpu_custom_call" | custom-call | flops 99999997952 | bytes 150000000 | tf_op jit(solution)/shard_map/listed_part/pallas_call | solution.py:156
  266.6 13.5 %all-to-all-done.5.refs_6_ = bf16[32,2,128,128]{3,2,1,0:T(8,128)(2,1)S(1)} async-done(((bf16[32,2,128,128]{3,2,1,0:T(8,128)(2,1)}), bf16[32,2,128,128]{3,2,1,0:T(8,128)(2,1)S(1)}, u32[]{:S(2)}, u32[]{:S(2)}) %all-to-all-start.5) | async-done | bytes 2097184 | tf_op jit(solution)/shard_map/all_to_all | solution.py:319
  281.4 9.8 %project.1 = (bf16[256,2048]{1,0:T(8,128)(2,1)}, f32[256,1024]{1,0:T(8,128)}, bf16[256,1024]{1,0:T(8,128)(2,1)}) custom-call(s32[128]{0:T(128)} %select_reduce_fusion.1.refs_0_, s32[2]{0:T(128)} %get-tuple-element.68.refs_1_, s32[128]{0:T(128)} %get-tuple-element.57.refs_2_, f32[128]{0:T(128)} %multiply_subtract_fusion.refs_3_, ...), custom_call_target="tpu_custom_call" | custom-call | flops 99999997952 | bytes 150000000 | tf_op jit(solution)/shard_map/project/pallas_call | solution.py:234
  291.3 3.8 %fusion.24 = (bf16[256,1024]{1,0:T(8,128)(2,1)S(1)}, f32[256,1024]{1,0:T(8,128)S(1)}) fusion(bf16[256,2048]{1,0:T(8,128)(2,1)S(1)} %copy-done.15, pred[]{:T(512)} %bitcast.14, bf16[256,2048]{1,0:T(8,128)(2,1)} %get-tuple-element.50, bf16[2048,2048]{1,0:T(8,128)(2,1)} %all-gather.2.cloned.1.call-done.refs_9_), kind=kOutput, calls=%fused_computation.82 | convolution fusion | flops 1074790400 | bytes 7340544 | tf_op jit(solution)/shard_map/dot_general | solution.py:367
  297.8 5.4 %collective-permute-done.9 = bf16[256,1024]{1,0:T(8,128)(2,1)S(1)} collective-permute-done((bf16[256,1024]{1,0:T(8,128)(2,1)S(1)}, bf16[256,1024]{1,0:T(8,128)(2,1)S(1)}, u32[]{:S(2)}, u32[]{:S(2)}) %collective-permute-start.9) | collective-permute-done | bytes 524320 | tf_op jit(solution)/shard_map/ppermute | solution.py:370
  (103 shorter events, 31.7 us)
Async XLA Ops:
  6.5 1.8 copy-start.6
  8.9 6.9 %copy-start.12 = (s32[1,2,16,4]{2,3,1,0:T(4,128)S(1)}, s32[1,2,16,4]{2,3,1,0:T(4,128)}, u32[]{:S(2)}) copy-start(s32[1,2,16,4]{2,3,1,0:T(4,128)} %param.16) | copy-start | bytes 1540
  8.9 7.8 %copy-start.17 = (s32[8]{0:T(128)S(1)}, s32[8]{0:T(128)}, u32[]{:S(2)}) copy-start(s32[8]{0:T(128)} %constant.160.clone) | copy-start | bytes 100
  8.9 16.9 %copy-start.13 = (f32[1,16]{1,0:T(1,128)S(1)}, f32[1,16]{1,0:T(1,128)}, u32[]{:S(2)}) copy-start(f32[1,16]{1,0:T(1,128)} %param.14) | copy-start | bytes 196
  8.9 16.9 %copy-start.14 = (f32[1,16]{1,0:T(1,128)S(1)}, f32[1,16]{1,0:T(1,128)}, u32[]{:S(2)}) copy-start(f32[1,16]{1,0:T(1,128)} %param.15) | copy-start | bytes 196
  8.9 17.3 %copy-start.5 = (s32[128]{0:T(128)S(1)}, s32[128]{0:T(128)}, u32[]{:S(2)}) copy-start(s32[128]{0:T(128)} %param.17) | copy-start | bytes 1540
  9.0 21.4 %copy-start.9 = (bf16[1,16,2048]{2,1,0:T(8,128)(2,1)S(1)}, bf16[1,16,2048]{2,1,0:T(8,128)(2,1)}, u32[]{:S(2)}) copy-start(bf16[1,16,2048]{2,1,0:T(8,128)(2,1)} %param.18) | copy-start | bytes 196612
  9.2 51.9 %collective-permute-start = (bf16[32,2,128,128]{3,2,1,0:T(8,128)(2,1)S(1)}, bf16[32,2,128,128]{3,2,1,0:T(8,128)(2,1)}, u32[]{:S(2)}, u32[]{:S(2)}) collective-permute-start(bf16[32,2,128,128]{3,2,1,0:T(8,128)(2,1)S(1)} %pad_maximum_fusion.refs_1_), channel_id=1, source_target_pairs={{0,16},{16,32},{32,48},{48,64},{64,80},{80,96},{96,112},{112,0},{1... | collective-permute-start | bytes 6291464 | tf_op jit(solution)/shard_map/ppermute | solution.py:332
  11.7 49.4 %collective-permute-start.1 = (bf16[32,2,128,128]{3,2,1,0:T(8,128)(2,1)S(1)}, bf16[32,2,128,128]{3,2,1,0:T(8,128)(2,1)}, u32[]{:S(2)}, u32[]{:S(2)}) collective-permute-start(bf16[32,2,128,128]{3,2,1,0:T(8,128)(2,1)S(1)} %pad_maximum_fusion.refs_1_), channel_id=1, source_target_pairs={{0,112},{16,0},{32,16},{48,32},{64,48},{80,64},{96,80},{112,96},{1... | collective-permute-start | bytes 6291464 | tf_op jit(solution)/shard_map/ppermute | solution.py:332
  18.1 13.2 %all-to-all-start = ((s32[16,8,2]{1,2,0:T(2,128)}), s32[16,8,2]{1,2,0:T(2,128)S(1)}, u32[]{:S(2)}, u32[]{:S(2)}) async-start(s32[16,8,2]{1,2,0:T(2,128)} %select_reduce_fusion), calls=%async_computation | async-start | bytes 32768 | tf_op jit(solution)/shard_map/all_to_all | solution.py:284
  25.8 8.4 %copy-start.10 = (f32[16]{0:T(128)}, f32[16]{0:T(128)S(1)}, u32[]{:S(2)}) copy-start(f32[16]{0:T(128)S(1)} %get-tuple-element.71.refs_0_) | copy-start | bytes 196
  25.9 8.4 %copy-start.11 = (f32[16]{0:T(128)}, f32[16]{0:T(128)S(1)}, u32[]{:S(2)}) copy-start(f32[16]{0:T(128)S(1)} %get-tuple-element.72.refs_1_) | copy-start | bytes 196
  34.3 44.8 %all-to-all-start.1 = ((bf16[48,2,128,128]{3,2,1,0:T(8,128)(2,1)}), bf16[48,2,128,128]{3,2,1,0:T(8,128)(2,1)}, u32[]{:S(2)}, u32[]{:S(2)}) async-start(bf16[48,2,128,128]{3,2,1,0:T(8,128)(2,1)} %pack_blocks.5), calls=%async_computation.1 | async-start | bytes 6291456 | tf_op jit(solution)/shard_map/all_to_all | solution.py:319
  61.1 47.4 %collective-permute-start.2 = (bf16[32,2,128,128]{3,2,1,0:T(8,128)(2,1)}, bf16[32,2,128,128]{3,2,1,0:T(8,128)(2,1)S(1)}, u32[]{:S(2)}, u32[]{:S(2)}) collective-permute-start(bf16[32,2,128,128]{3,2,1,0:T(8,128)(2,1)} %collective-permute-done.refs_1_), channel_id=1, source_target_pairs={{0,16},{16,32},{32,48},{48,64},{64,80},{80,96},{96,112},{112,0},{1... | collective-permute-start | bytes 6291464 | tf_op jit(solution)/shard_map/ppermute | solution.py:332
  61.1 48.8 %collective-permute-start.3 = (bf16[32,2,128,128]{3,2,1,0:T(8,128)(2,1)}, bf16[32,2,128,128]{3,2,1,0:T(8,128)(2,1)}, u32[]{:S(2)}, u32[]{:S(2)}) collective-permute-start(bf16[32,2,128,128]{3,2,1,0:T(8,128)(2,1)} %collective-permute-done.1.refs_2_), channel_id=1, source_target_pairs={{0,112},{16,0},{32,16},{48,32},{64,48},{80,64},{96,80},{112,96},{1... | collective-permute-start | bytes 6291464 | tf_op jit(solution)/shard_map/ppermute | solution.py:332
  71.8 1.9 copy-start.1
  79.1 53.2 %all-to-all-start.2 = ((bf16[64,2,128,128]{3,2,1,0:T(8,128)(2,1)}), bf16[64,2,128,128]{3,2,1,0:T(8,128)(2,1)}, u32[]{:S(2)}, u32[]{:S(2)}) async-start(bf16[64,2,128,128]{3,2,1,0:T(8,128)(2,1)} %copy-done.1), calls=%async_computation.2 | async-start | bytes 8388608 | tf_op jit(solution)/shard_map/all_to_all | solution.py:319
  109.9 46.6 %collective-permute-start.4 = (bf16[32,2,128,128]{3,2,1,0:T(8,128)(2,1)}, bf16[32,2,128,128]{3,2,1,0:T(8,128)(2,1)S(1)}, u32[]{:S(2)}, u32[]{:S(2)}) collective-permute-start(bf16[32,2,128,128]{3,2,1,0:T(8,128)(2,1)} %copy-done.3), channel_id=1, source_target_pairs={{0,16},{16,32},{32,48},{48,64},{64,80},{80,96},{96,112},{112,0},{1... | collective-permute-start | bytes 6291464 | tf_op jit(solution)/shard_map/ppermute | solution.py:332
  109.9 46.6 %collective-permute-start.5 = (bf16[32,2,128,128]{3,2,1,0:T(8,128)(2,1)}, bf16[32,2,128,128]{3,2,1,0:T(8,128)(2,1)}, u32[]{:S(2)}, u32[]{:S(2)}) collective-permute-start(bf16[32,2,128,128]{3,2,1,0:T(8,128)(2,1)} %collective-permute-done.3.refs_2_), channel_id=1, source_target_pairs={{0,112},{16,0},{32,16},{48,32},{64,48},{80,64},{96,80},{112,96},{1... | collective-permute-start | bytes 6291464 | tf_op jit(solution)/shard_map/ppermute | solution.py:332
  121.5 2.0 copy-start
  132.2 56.6 %all-to-all-start.3 = ((bf16[64,2,128,128]{3,2,1,0:T(8,128)(2,1)}), bf16[64,2,128,128]{3,2,1,0:T(8,128)(2,1)}, u32[]{:S(2)}, u32[]{:S(2)}) async-start(bf16[64,2,128,128]{3,2,1,0:T(8,128)(2,1)} %copy-done), calls=%async_computation.3 | async-start | bytes 8388608 | tf_op jit(solution)/shard_map/all_to_all | solution.py:319
  141.6 138.5 %all-gather.2.cloned.1.call-start = ((), (), s32[]{:S(2)}) async-start(), calls=%async_computation.6 | async-start | bytes 9437184 | tf_op jit(solution)/shard_map/all_gather | solution.py:348
  157.5 40.2 %collective-permute-start.6 = (bf16[16,2,128,128]{3,2,1,0:T(8,128)(2,1)}, bf16[16,2,128,128]{3,2,1,0:T(8,128)(2,1)S(1)}, u32[]{:S(2)}, u32[]{:S(2)}) collective-permute-start(bf16[16,2,128,128]{3,2,1,0:T(8,128)(2,1)} %slice.51), channel_id=1, source_target_pairs={{0,16},{16,32},{32,48},{48,64},{64,80},{80,96},{96,112},{112,0},{1... | collective-permute-start | bytes 3145736 | tf_op jit(solution)/shard_map/ppermute | solution.py:332
  159.9 37.9 %collective-permute-start.7 = (bf16[16,2,128,128]{3,2,1,0:T(8,128)(2,1)}, bf16[16,2,128,128]{3,2,1,0:T(8,128)(2,1)}, u32[]{:S(2)}, u32[]{:S(2)}) collective-permute-start(bf16[16,2,128,128]{3,2,1,0:T(8,128)(2,1)} %slice.52), channel_id=1, source_target_pairs={{0,112},{16,0},{32,16},{48,32},{64,48},{80,64},{96,80},{112,96},{1... | collective-permute-start | bytes 3145736 | tf_op jit(solution)/shard_map/ppermute | solution.py:332
  169.9 2.0 copy-start.2
  188.8 55.8 %all-to-all-start.4 = ((bf16[64,2,128,128]{3,2,1,0:T(8,128)(2,1)}), bf16[64,2,128,128]{3,2,1,0:T(8,128)(2,1)}, u32[]{:S(2)}, u32[]{:S(2)}) async-start(bf16[64,2,128,128]{3,2,1,0:T(8,128)(2,1)} %copy-done.2), calls=%async_computation.4 | async-start | bytes 8388608 | tf_op jit(solution)/shard_map/all_to_all | solution.py:319
  244.7 35.4 %all-to-all-start.5 = ((bf16[32,2,128,128]{3,2,1,0:T(8,128)(2,1)}), bf16[32,2,128,128]{3,2,1,0:T(8,128)(2,1)S(1)}, u32[]{:S(2)}, u32[]{:S(2)}) async-start(bf16[32,2,128,128]{3,2,1,0:T(8,128)(2,1)} %pack_blocks.9), calls=%async_computation.5 | async-start | bytes 4194304 | tf_op jit(solution)/shard_map/all_to_all | solution.py:319
  281.4 9.8 %copy-start.15 = (bf16[256,2048]{1,0:T(8,128)(2,1)S(1)}, bf16[256,2048]{1,0:T(8,128)(2,1)}, u32[]{:S(2)}) copy-start(bf16[256,2048]{1,0:T(8,128)(2,1)} %refs_10_.1) | copy-start | bytes 3145732
  291.3 5.3 %copy-start.16 = (bf16[256,1024]{1,0:T(8,128)(2,1)S(1)}, bf16[256,1024]{1,0:T(8,128)(2,1)}, u32[]{:S(2)}) copy-start(bf16[256,1024]{1,0:T(8,128)(2,1)} %get-tuple-element.47) | copy-start | bytes 1572868
  295.1 9.5 %copy-start.8 = (f32[256,1024]{1,0:T(8,128)S(1)}, f32[256,1024]{1,0:T(8,128)}, u32[]{:S(2)}) copy-start(f32[256,1024]{1,0:T(8,128)} %get-tuple-element.48) | copy-start | bytes 3145732
  295.1 8.1 %collective-permute-start.9 = (bf16[256,1024]{1,0:T(8,128)(2,1)S(1)}, bf16[256,1024]{1,0:T(8,128)(2,1)S(1)}, u32[]{:S(2)}, u32[]{:S(2)}) collective-permute-start(bf16[256,1024]{1,0:T(8,128)(2,1)S(1)} %get-tuple-element.69), channel_id=1, source_target_pairs={{0,128},{1,129},{2,130},{3,131},{4,132},{5,133},{6,134},{7,135},{8... | collective-permute-start | bytes 1572872 | tf_op jit(solution)/shard_map/ppermute | solution.py:370
  296.5 8.0 %collective-permute-start.8 = (bf16[256,1024]{1,0:T(8,128)(2,1)S(1)}, bf16[256,1024]{1,0:T(8,128)(2,1)S(1)}, u32[]{:S(2)}, u32[]{:S(2)}) collective-permute-start(bf16[256,1024]{1,0:T(8,128)(2,1)S(1)} %copy-done.16), channel_id=1, source_target_pairs={{0,128},{1,129},{2,130},{3,131},{4,132},{5,133},{6,134},{7,135},{8... | collective-permute-start | bytes 1572872 | tf_op jit(solution)/shard_map/ppermute | solution.py:365
  (3 other events, 4.3 us)
Sparse Core Ops, SparseCore 0:
  162.7 101.7 all-gather.1

commit v6 on v5

--- a/solution.py
+++ b/solution.py
@@ -62,7 +62,7 @@
         + [pl.BlockSpec(memory_space=pltpu.VMEM)] * (len(sources) + len(extras)),
         out_specs=pl.BlockSpec(memory_space=pl.ANY),
         scratch_shapes=[pltpu.SemaphoreType.DMA],
-        compiler_params=pltpu.CompilerParams(vmem_limit_bytes=24 * 1024 * 1024),
+        compiler_params=pltpu.CompilerParams(vmem_limit_bytes=(24 if extras else 60) * 1024 * 1024),
         cost_estimate=HEAVY,
         name="pack_blocks",
     )(sel.reshape(sel.size), *sources, *extras)
@@ -355,7 +355,7 @@
     acc = added(3, got, after(acc, sent))
     last = served(sent)
 
-    cut = width // 2
+    cut = width * 3 // 4
     segment = lax.axis_index("segment").reshape(1)
     pieces = (order, edges[4:6], slot, near_item, far_item, q, last, acc)
     sizes = (head_size ** (-0.5), heads, listed)

time: 314 us -> 313 us (level)
  waiting for transfers between devices: 109 us -> 123 us
  Pallas kernels: 92.9 us -> 83.8 us
  local copies, waits for them, and re-layouts: 23.6 us -> 18.6 us
    all_to_all x5, waiting for transfers between devices: 56.8 us -> 73.2 us  [served(): lax.all_to_all(sent, ('x', 'y'), split_axis=0, concat_axis=0, tiled=True)]
    pallas_call x5, Pallas kernels: 27.5 us -> 17.8 us  [pack(): pl.pallas_call(lambda *refs: pack_kernel(slots, half, len(extras), *refs)...]
    unnamed x39 -> x31, local copies, waits for them, and re-layouts: 13.4 us -> 8.04 us
  transfers between devices with their start and end apart: 17 -> 17, of which waited for: 10 -> 10; matrix products, arithmetic and copies ran while one was open for 5% -> 6% of each run, Pallas kernels for 27% -> 24%
where the time goes in v6:
time: 313 us; the launch traced here: 312 us
  waiting for transfers between devices  123 us (39%)
  Pallas kernels  83.8 us (27%)
  starting transfers between devices  63.5 us (20%)
  local copies, waits for them, and re-layouts  18.6 us (6%)
  between operations  14.5 us (5%)
  other arithmetic  5.67 us (2%)
    all_to_all x5, waiting for transfers between devices, served(): lax.all_to_all(sent, ('x', 'y'), split_axis=0, concat_axis=0, tiled=True)  73.2 us
    pallas_call x4, Pallas kernels, listed_part(): pl.pallas_call(lambda *refs: listed_kernel(((width // heads) ** (-0.5), h...  44.2 us
    ppermute x8, waiting for transfers between devices, step(): return (lax.ppermute(pair[0], 'z', up), lax.ppermute(pair[1], 'z', down))  42.2 us
    all_to_all x5, starting transfers between devices, served(): lax.all_to_all(sent, ('x', 'y'), split_axis=0, concat_axis=0, tiled=True)  39.3 us
    pallas_call x5, Pallas kernels, pack(): pl.pallas_call(lambda *refs: pack_kernel(slots, half, len(extras), *refs)...  17.8 us
    ppermute x8, starting transfers between devices, step(): return (lax.ppermute(pair[0], 'z', up), lax.ppermute(pair[1], 'z', down))  14.9 us
    pallas_call x1, Pallas kernels, local_part(): pl.pallas_call(lambda *refs: local_kernel(head_size ** (-0.5), *refs), gr...  12.1 us
    pallas_call x1, Pallas kernels, project(): pl.pallas_call(kernel, out_shape=out_shape, in_specs=in_specs + [smem, pl...  9.67 us
  transfers between devices with their start and end apart: 17, of which 10 were waited for; matrix products, arithmetic and copies ran while one was open for 6% of the time, Pallas kernels for 24%

profile of v6, /device:TPU:1, one launch (start us, length us, event | category | flops | bytes accessed | tf_op | source)
XLA Modules:
  0.0 312.1 jit_solution(342725026482790566)
XLA Ops:
  9.2 2.5 collective-permute-start
  11.7 4.0 %collective-permute-start.1 = (bf16[32,2,128,128]{3,2,1,0:T(8,128)(2,1)S(1)}, bf16[32,2,128,128]{3,2,1,0:T(8,128)(2,1)}, u32[]{:S(2)}, u32[]{:S(2)}) collective-permute-start(bf16[32,2,128,128]{3,2,1,0:T(8,128)(2,1)S(1)} %pad_maximum_fusion.refs_1_), channel_id=1, source_target_pairs={{0,112},{16,0},{32,16},{48,32},{64,48},{80,64},{96,80},{112,96},{1... | collective-permute-start | bytes 6291464 | tf_op jit(solution)/shard_map/ppermute | solution.py:332
  18.1 6.8 %all-to-all-start = ((s32[16,8,2]{1,2,0:T(2,128)}), s32[16,8,2]{1,2,0:T(2,128)S(1)}, u32[]{:S(2)}, u32[]{:S(2)}) async-start(s32[16,8,2]{1,2,0:T(2,128)} %select_reduce_fusion), calls=%async_computation | async-start | bytes 32768 | tf_op jit(solution)/shard_map/all_to_all | solution.py:284
  32.1 2.2 pack_blocks.5
  34.3 6.0 %all-to-all-start.1 = ((bf16[48,2,128,128]{3,2,1,0:T(8,128)(2,1)}), bf16[48,2,128,128]{3,2,1,0:T(8,128)(2,1)}, u32[]{:S(2)}, u32[]{:S(2)}) async-start(bf16[48,2,128,128]{3,2,1,0:T(8,128)(2,1)} %pack_blocks.5), calls=%async_computation.1 | async-start | bytes 6291456 | tf_op jit(solution)/shard_map/all_to_all | solution.py:319
  40.3 12.1 %local_part.1.refs_7_ = f32[256,2048]{1,0:T(8,128)} custom-call(f32[16]{0:T(128)} %copy-done.6, f32[16]{0:T(128)} %copy-done.7, bf16[256,2048]{1,0:T(8,128)(2,1)} %bitcast.37, bf16[256,2048]{1,0:T(8,128)(2,1)} %bitcast.47, bf16[256,2048]{1,0:T(8,128)(2,1)} %bitcast.46), custom_call_target="tpu_custom_call" | custom-call | flops 1 | bytes 1 | tf_op jit(solution)/shard_map/local_part/pallas_call | solution.py:92
  55.7 5.4 %collective-permute-done.refs_1_ = bf16[32,2,128,128]{3,2,1,0:T(8,128)(2,1)} collective-permute-done((bf16[32,2,128,128]{3,2,1,0:T(8,128)(2,1)S(1)}, bf16[32,2,128,128]{3,2,1,0:T(8,128)(2,1)}, u32[]{:S(2)}, u32[]{:S(2)}) %collective-permute-start) | collective-permute-done | bytes 2097184 | tf_op jit(solution)/shard_map/ppermute | solution.py:332
  61.1 2.7 collective-permute-start.3
  63.8 4.2 %pack_blocks.6 = bf16[64,2,128,128]{3,2,1,0:T(8,128)(2,1)} custom-call(s32[64]{0:T(128)} %reshape.404.refs_0_, bf16[32,2,128,128]{3,2,1,0:T(8,128)(2,1)} %collective-permute-done.refs_1_, bf16[32,2,128,128]{3,2,1,0:T(8,128)(2,1)} %collective-permute-done.1.refs_2_), custom_call_target="tpu_custom_call" | custom-call | flops 49999998976 | bytes 150000000 | tf_op jit(solution)/shard_map/pack_blocks/pallas_call | solution.py:58
  68.0 11.3 %all-to-all-done.1.refs_6_ = bf16[48,2,128,128]{3,2,1,0:T(8,128)(2,1)} async-done(((bf16[48,2,128,128]{3,2,1,0:T(8,128)(2,1)}), bf16[48,2,128,128]{3,2,1,0:T(8,128)(2,1)}, u32[]{:S(2)}, u32[]{:S(2)}) %all-to-all-start.1) | async-done | bytes 3145760 | tf_op jit(solution)/shard_map/all_to_all | solution.py:319
  79.3 4.6 %all-to-all-start.2 = ((bf16[64,2,128,128]{3,2,1,0:T(8,128)(2,1)}), bf16[64,2,128,128]{3,2,1,0:T(8,128)(2,1)}, u32[]{:S(2)}, u32[]{:S(2)}) async-start(bf16[64,2,128,128]{3,2,1,0:T(8,128)(2,1)} %pack_blocks.6), calls=%async_computation.2 | async-start | bytes 8388608 | tf_op jit(solution)/shard_map/all_to_all | solution.py:319
  86.4 22.1 %collective-permute-done.2.refs_1_ = bf16[32,2,128,128]{3,2,1,0:T(8,128)(2,1)S(1)} collective-permute-done((bf16[32,2,128,128]{3,2,1,0:T(8,128)(2,1)}, bf16[32,2,128,128]{3,2,1,0:T(8,128)(2,1)S(1)}, u32[]{:S(2)}, u32[]{:S(2)}) %collective-permute-start.2) | collective-permute-done | bytes 2097184 | tf_op jit(solution)/shard_map/ppermute | solution.py:332
  109.9 2.7 collective-permute-start.5
  112.6 4.2 %pack_blocks.7 = bf16[64,2,128,128]{3,2,1,0:T(8,128)(2,1)} custom-call(s32[64]{0:T(128)} %reshape.405.refs_0_, bf16[32,2,128,128]{3,2,1,0:T(8,128)(2,1)} %copy-done.11, bf16[32,2,128,128]{3,2,1,0:T(8,128)(2,1)} %collective-permute-done.3.refs_2_), custom_call_target="tpu_custom_call" | custom-call | flops 49999998976 | bytes 150000000 | tf_op jit(solution)/shard_map/pack_blocks/pallas_call | solution.py:58
  116.8 7.9 %listed_part.4.refs_7_ = f32[256,2048]{1,0:T(8,128)} custom-call(s32[128]{0:T(128)} %select_reduce_fusion.1.refs_0_, s32[2]{0:T(128)} %get-tuple-element.67.refs_1_, s32[128]{0:T(128)} %get-tuple-element.57.refs_2_, f32[128]{0:T(128)} %multiply_subtract_fusion.refs_3_, f32[128]{0:T(128)} %get-tuple-element.55.refs_4_, bf16[256,2048]{1,0:T(8,128)(2,1)} %bitcast.38, ...), custom_call_target="tpu_custom_call" | custom-call | flops 1 | bytes 1 | tf_op jit(solution)/shard_map/listed_part/pallas_call | solution.py:156
  124.7 7.6 %all-to-all-done.2.refs_6_ = bf16[64,2,128,128]{3,2,1,0:T(8,128)(2,1)} async-done(((bf16[64,2,128,128]{3,2,1,0:T(8,128)(2,1)}), bf16[64,2,128,128]{3,2,1,0:T(8,128)(2,1)}, u32[]{:S(2)}, u32[]{:S(2)}) %all-to-all-start.2) | async-done | bytes 4194336 | tf_op jit(solution)/shard_map/all_to_all | solution.py:319
  132.3 9.5 %all-to-all-start.3 = ((bf16[64,2,128,128]{3,2,1,0:T(8,128)(2,1)}), bf16[64,2,128,128]{3,2,1,0:T(8,128)(2,1)}, u32[]{:S(2)}, u32[]{:S(2)}) async-start(bf16[64,2,128,128]{3,2,1,0:T(8,128)(2,1)} %pack_blocks.7), calls=%async_computation.3 | async-start | bytes 8388608 | tf_op jit(solution)/shard_map/all_to_all | solution.py:319
  141.8 14.7 %collective-permute-done.4.refs_1_ = bf16[32,2,128,128]{3,2,1,0:T(8,128)(2,1)S(1)} collective-permute-done((bf16[32,2,128,128]{3,2,1,0:T(8,128)(2,1)}, bf16[32,2,128,128]{3,2,1,0:T(8,128)(2,1)S(1)}, u32[]{:S(2)}, u32[]{:S(2)}) %collective-permute-start.4) | collective-permute-done | bytes 2097184 | tf_op jit(solution)/shard_map/ppermute | solution.py:332
  159.1 2.9 collective-permute-start.7
  162.1 4.3 %pack_blocks.8 = bf16[64,2,128,128]{3,2,1,0:T(8,128)(2,1)} custom-call(s32[64]{0:T(128)} %reshape.406.refs_0_, bf16[32,2,128,128]{3,2,1,0:T(8,128)(2,1)} %copy-done.4, bf16[32,2,128,128]{3,2,1,0:T(8,128)(2,1)} %collective-permute-done.5.refs_2_), custom_call_target="tpu_custom_call" | custom-call | flops 49999998976 | bytes 150000000 | tf_op jit(solution)/shard_map/pack_blocks/pallas_call | solution.py:58
  166.4 12.4 %listed_part.5.refs_7_ = f32[256,2048]{1,0:T(8,128)} custom-call(s32[128]{0:T(128)} %select_reduce_fusion.1.refs_0_, s32[2]{0:T(128)} %get-tuple-element.66.refs_1_, s32[128]{0:T(128)} %get-tuple-element.57.refs_2_, f32[128]{0:T(128)} %multiply_subtract_fusion.refs_3_, f32[128]{0:T(128)} %get-tuple-element.55.refs_4_, bf16[256,2048]{1,0:T(8,128)(2,1)} %bitcast.39, ...), custom_call_target="tpu_custom_call" | custom-call | flops 1 | bytes 1 | tf_op jit(solution)/shard_map/listed_part/pallas_call | solution.py:156
  178.8 10.2 %all-to-all-done.3.refs_6_ = bf16[64,2,128,128]{3,2,1,0:T(8,128)(2,1)} async-done(((bf16[64,2,128,128]{3,2,1,0:T(8,128)(2,1)}), bf16[64,2,128,128]{3,2,1,0:T(8,128)(2,1)}, u32[]{:S(2)}, u32[]{:S(2)}) %all-to-all-start.3) | async-done | bytes 4194336 | tf_op jit(solution)/shard_map/all_to_all | solution.py:319
  189.0 8.9 %all-to-all-start.4 = ((bf16[64,2,128,128]{3,2,1,0:T(8,128)(2,1)}), bf16[64,2,128,128]{3,2,1,0:T(8,128)(2,1)}, u32[]{:S(2)}, u32[]{:S(2)}) async-start(bf16[64,2,128,128]{3,2,1,0:T(8,128)(2,1)} %pack_blocks.8), calls=%async_computation.4 | async-start | bytes 8388608 | tf_op jit(solution)/shard_map/all_to_all | solution.py:319
  198.9 2.9 pack_blocks.9
  201.9 12.4 %listed_part.6.refs_7_ = f32[256,2048]{1,0:T(8,128)} custom-call(s32[128]{0:T(128)} %select_reduce_fusion.1.refs_0_, s32[2]{0:T(128)} %get-tuple-element.65.refs_1_, s32[128]{0:T(128)} %get-tuple-element.57.refs_2_, f32[128]{0:T(128)} %multiply_subtract_fusion.refs_3_, f32[128]{0:T(128)} %get-tuple-element.55.refs_4_, bf16[256,2048]{1,0:T(8,128)(2,1)} %bitcast.40, ...), custom_call_target="tpu_custom_call" | custom-call | flops 1 | bytes 1 | tf_op jit(solution)/shard_map/listed_part/pallas_call | solution.py:156
  214.3 30.6 %all-to-all-done.4.refs_6_ = bf16[64,2,128,128]{3,2,1,0:T(8,128)(2,1)} async-done(((bf16[64,2,128,128]{3,2,1,0:T(8,128)(2,1)}), bf16[64,2,128,128]{3,2,1,0:T(8,128)(2,1)}, u32[]{:S(2)}, u32[]{:S(2)}) %all-to-all-start.4) | async-done | bytes 4194336 | tf_op jit(solution)/shard_map/all_to_all | solution.py:319
  244.8 10.4 %all-to-all-start.5 = ((bf16[32,2,128,128]{3,2,1,0:T(8,128)(2,1)}), bf16[32,2,128,128]{3,2,1,0:T(8,128)(2,1)S(1)}, u32[]{:S(2)}, u32[]{:S(2)}) async-start(bf16[32,2,128,128]{3,2,1,0:T(8,128)(2,1)} %pack_blocks.9), calls=%async_computation.5 | async-start | bytes 4194304 | tf_op jit(solution)/shard_map/all_to_all | solution.py:319
  255.2 11.5 %listed_part.7.refs_7_ = f32[256,2048]{1,0:T(8,128)} custom-call(s32[128]{0:T(128)} %select_reduce_fusion.1.refs_0_, s32[2]{0:T(128)} %get-tuple-element.64.refs_1_, s32[128]{0:T(128)} %get-tuple-element.57.refs_2_, f32[128]{0:T(128)} %multiply_subtract_fusion.refs_3_, f32[128]{0:T(128)} %get-tuple-element.55.refs_4_, bf16[256,2048]{1,0:T(8,128)(2,1)} %bitcast.41, ...), custom_call_target="tpu_custom_call" | custom-call | flops 99999997952 | bytes 150000000 | tf_op jit(solution)/shard_map/listed_part/pallas_call | solution.py:156
  266.7 13.5 %all-to-all-done.5.refs_6_ = bf16[32,2,128,128]{3,2,1,0:T(8,128)(2,1)S(1)} async-done(((bf16[32,2,128,128]{3,2,1,0:T(8,128)(2,1)}), bf16[32,2,128,128]{3,2,1,0:T(8,128)(2,1)S(1)}, u32[]{:S(2)}, u32[]{:S(2)}) %all-to-all-start.5) | async-done | bytes 2097184 | tf_op jit(solution)/shard_map/all_to_all | solution.py:319
  281.7 9.7 %project.1 = (bf16[256,2048]{1,0:T(8,128)(2,1)}, f32[256,1536]{1,0:T(8,128)}, bf16[256,1536]{1,0:T(8,128)(2,1)}) custom-call(s32[128]{0:T(128)} %select_reduce_fusion.1.refs_0_, s32[2]{0:T(128)} %get-tuple-element.68.refs_1_, s32[128]{0:T(128)} %get-tuple-element.57.refs_2_, f32[128]{0:T(128)} %multiply_subtract_fusion.refs_3_, ...), custom_call_target="tpu_custom_call" | custom-call | flops 99999997952 | bytes 150000000 | tf_op jit(solution)/shard_map/project/pallas_call | solution.py:234
  292.6 2.7 fusion.24
  296.7 7.2 %collective-permute-done.9 = bf16[256,512]{1,0:T(8,128)(2,1)S(1)} collective-permute-done((bf16[256,512]{1,0:T(8,128)(2,1)S(1)}, bf16[256,512]{1,0:T(8,128)(2,1)S(1)}, u32[]{:S(2)}, u32[]{:S(2)}) %collective-permute-start.9) | collective-permute-done | bytes 262176 | tf_op jit(solution)/shard_map/ppermute | solution.py:370
  (95 shorter events, 27.6 us)
Async XLA Ops:
  6.5 1.8 copy-start.1
  8.9 6.9 %copy-start.8 = (s32[1,2,16,4]{2,3,1,0:T(4,128)S(1)}, s32[1,2,16,4]{2,3,1,0:T(4,128)}, u32[]{:S(2)}) copy-start(s32[1,2,16,4]{2,3,1,0:T(4,128)} %param.16) | copy-start | bytes 1540
  8.9 7.9 %copy-start.13 = (s32[8]{0:T(128)S(1)}, s32[8]{0:T(128)}, u32[]{:S(2)}) copy-start(s32[8]{0:T(128)} %constant.160.clone) | copy-start | bytes 100
  8.9 17.0 %copy-start.9 = (f32[1,16]{1,0:T(1,128)S(1)}, f32[1,16]{1,0:T(1,128)}, u32[]{:S(2)}) copy-start(f32[1,16]{1,0:T(1,128)} %param.14) | copy-start | bytes 196
  8.9 17.0 %copy-start.10 = (f32[1,16]{1,0:T(1,128)S(1)}, f32[1,16]{1,0:T(1,128)}, u32[]{:S(2)}) copy-start(f32[1,16]{1,0:T(1,128)} %param.15) | copy-start | bytes 196
  8.9 17.4 %copy-start = (s32[128]{0:T(128)S(1)}, s32[128]{0:T(128)}, u32[]{:S(2)}) copy-start(s32[128]{0:T(128)} %param.17) | copy-start | bytes 1540
  8.9 21.6 %copy-start.5 = (bf16[1,16,2048]{2,1,0:T(8,128)(2,1)S(1)}, bf16[1,16,2048]{2,1,0:T(8,128)(2,1)}, u32[]{:S(2)}) copy-start(bf16[1,16,2048]{2,1,0:T(8,128)(2,1)} %param.18) | copy-start | bytes 196612
  9.2 51.9 %collective-permute-start = (bf16[32,2,128,128]{3,2,1,0:T(8,128)(2,1)S(1)}, bf16[32,2,128,128]{3,2,1,0:T(8,128)(2,1)}, u32[]{:S(2)}, u32[]{:S(2)}) collective-permute-start(bf16[32,2,128,128]{3,2,1,0:T(8,128)(2,1)S(1)} %pad_maximum_fusion.refs_1_), channel_id=1, source_target_pairs={{0,16},{16,32},{32,48},{48,64},{64,80},{80,96},{96,112},{112,0},{1... | collective-permute-start | bytes 6291464 | tf_op jit(solution)/shard_map/ppermute | solution.py:332
  11.7 49.4 %collective-permute-start.1 = (bf16[32,2,128,128]{3,2,1,0:T(8,128)(2,1)S(1)}, bf16[32,2,128,128]{3,2,1,0:T(8,128)(2,1)}, u32[]{:S(2)}, u32[]{:S(2)}) collective-permute-start(bf16[32,2,128,128]{3,2,1,0:T(8,128)(2,1)S(1)} %pad_maximum_fusion.refs_1_), channel_id=1, source_target_pairs={{0,112},{16,0},{32,16},{48,32},{64,48},{80,64},{96,80},{112,96},{1... | collective-permute-start | bytes 6291464 | tf_op jit(solution)/shard_map/ppermute | solution.py:332
  18.1 13.2 %all-to-all-start = ((s32[16,8,2]{1,2,0:T(2,128)}), s32[16,8,2]{1,2,0:T(2,128)S(1)}, u32[]{:S(2)}, u32[]{:S(2)}) async-start(s32[16,8,2]{1,2,0:T(2,128)} %select_reduce_fusion), calls=%async_computation | async-start | bytes 32768 | tf_op jit(solution)/shard_map/all_to_all | solution.py:284
  25.9 8.4 %copy-start.6 = (f32[16]{0:T(128)}, f32[16]{0:T(128)S(1)}, u32[]{:S(2)}) copy-start(f32[16]{0:T(128)S(1)} %get-tuple-element.71.refs_0_) | copy-start | bytes 196
  25.9 8.4 %copy-start.7 = (f32[16]{0:T(128)}, f32[16]{0:T(128)S(1)}, u32[]{:S(2)}) copy-start(f32[16]{0:T(128)S(1)} %get-tuple-element.72.refs_1_) | copy-start | bytes 196
  34.3 44.9 %all-to-all-start.1 = ((bf16[48,2,128,128]{3,2,1,0:T(8,128)(2,1)}), bf16[48,2,128,128]{3,2,1,0:T(8,128)(2,1)}, u32[]{:S(2)}, u32[]{:S(2)}) async-start(bf16[48,2,128,128]{3,2,1,0:T(8,128)(2,1)} %pack_blocks.5), calls=%async_computation.1 | async-start | bytes 6291456 | tf_op jit(solution)/shard_map/all_to_all | solution.py:319
  61.1 47.4 %collective-permute-start.2 = (bf16[32,2,128,128]{3,2,1,0:T(8,128)(2,1)}, bf16[32,2,128,128]{3,2,1,0:T(8,128)(2,1)S(1)}, u32[]{:S(2)}, u32[]{:S(2)}) collective-permute-start(bf16[32,2,128,128]{3,2,1,0:T(8,128)(2,1)} %collective-permute-done.refs_1_), channel_id=1, source_target_pairs={{0,16},{16,32},{32,48},{48,64},{64,80},{80,96},{96,112},{112,0},{1... | collective-permute-start | bytes 6291464 | tf_op jit(solution)/shard_map/ppermute | solution.py:332
  61.1 48.8 %collective-permute-start.3 = (bf16[32,2,128,128]{3,2,1,0:T(8,128)(2,1)}, bf16[32,2,128,128]{3,2,1,0:T(8,128)(2,1)}, u32[]{:S(2)}, u32[]{:S(2)}) collective-permute-start(bf16[32,2,128,128]{3,2,1,0:T(8,128)(2,1)} %collective-permute-done.1.refs_2_), channel_id=1, source_target_pairs={{0,112},{16,0},{32,16},{48,32},{64,48},{80,64},{96,80},{112,96},{1... | collective-permute-start | bytes 6291464 | tf_op jit(solution)/shard_map/ppermute | solution.py:332
  79.3 53.0 %all-to-all-start.2 = ((bf16[64,2,128,128]{3,2,1,0:T(8,128)(2,1)}), bf16[64,2,128,128]{3,2,1,0:T(8,128)(2,1)}, u32[]{:S(2)}, u32[]{:S(2)}) async-start(bf16[64,2,128,128]{3,2,1,0:T(8,128)(2,1)} %pack_blocks.6), calls=%async_computation.2 | async-start | bytes 8388608 | tf_op jit(solution)/shard_map/all_to_all | solution.py:319
  108.5 1.4 copy-start.11
  109.9 46.6 %collective-permute-start.4 = (bf16[32,2,128,128]{3,2,1,0:T(8,128)(2,1)}, bf16[32,2,128,128]{3,2,1,0:T(8,128)(2,1)S(1)}, u32[]{:S(2)}, u32[]{:S(2)}) collective-permute-start(bf16[32,2,128,128]{3,2,1,0:T(8,128)(2,1)} %copy-done.11), channel_id=1, source_target_pairs={{0,16},{16,32},{32,48},{48,64},{64,80},{80,96},{96,112},{112,0},{1... | collective-permute-start | bytes 6291464 | tf_op jit(solution)/shard_map/ppermute | solution.py:332
  109.9 46.6 %collective-permute-start.5 = (bf16[32,2,128,128]{3,2,1,0:T(8,128)(2,1)}, bf16[32,2,128,128]{3,2,1,0:T(8,128)(2,1)}, u32[]{:S(2)}, u32[]{:S(2)}) collective-permute-start(bf16[32,2,128,128]{3,2,1,0:T(8,128)(2,1)} %collective-permute-done.3.refs_2_), channel_id=1, source_target_pairs={{0,112},{16,0},{32,16},{48,32},{64,48},{80,64},{96,80},{112,96},{1... | collective-permute-start | bytes 6291464 | tf_op jit(solution)/shard_map/ppermute | solution.py:332
  132.3 56.7 %all-to-all-start.3 = ((bf16[64,2,128,128]{3,2,1,0:T(8,128)(2,1)}), bf16[64,2,128,128]{3,2,1,0:T(8,128)(2,1)}, u32[]{:S(2)}, u32[]{:S(2)}) async-start(bf16[64,2,128,128]{3,2,1,0:T(8,128)(2,1)} %pack_blocks.7), calls=%async_computation.3 | async-start | bytes 8388608 | tf_op jit(solution)/shard_map/all_to_all | solution.py:319
  141.8 138.5 %all-gather.2.cloned.1.call-start = ((), (), s32[]{:S(2)}) async-start(), calls=%async_computation.6 | async-start | bytes 9437184 | tf_op jit(solution)/shard_map/all_gather | solution.py:348
  156.5 1.3 copy-start.4
  157.8 40.1 %collective-permute-start.6 = (bf16[16,2,128,128]{3,2,1,0:T(8,128)(2,1)S(1)}, bf16[16,2,128,128]{3,2,1,0:T(8,128)(2,1)}, u32[]{:S(2)}, u32[]{:S(2)}) collective-permute-start(bf16[16,2,128,128]{3,2,1,0:T(8,128)(2,1)S(1)} %slice.51), channel_id=1, source_target_pairs={{0,16},{16,32},{32,48},{48,64},{64,80},{80,96},{96,112},{112,0},{1... | collective-permute-start | bytes 3145736 | tf_op jit(solution)/shard_map/ppermute | solution.py:332
  159.1 38.8 %collective-permute-start.7 = (bf16[16,2,128,128]{3,2,1,0:T(8,128)(2,1)S(1)}, bf16[16,2,128,128]{3,2,1,0:T(8,128)(2,1)S(1)}, u32[]{:S(2)}, u32[]{:S(2)}) collective-permute-start(bf16[16,2,128,128]{3,2,1,0:T(8,128)(2,1)S(1)} %slice.52), channel_id=1, source_target_pairs={{0,112},{16,0},{32,16},{48,32},{64,48},{80,64},{96,80},{112,96},{1... | collective-permute-start | bytes 3145736 | tf_op jit(solution)/shard_map/ppermute | solution.py:332
  189.0 55.8 %all-to-all-start.4 = ((bf16[64,2,128,128]{3,2,1,0:T(8,128)(2,1)}), bf16[64,2,128,128]{3,2,1,0:T(8,128)(2,1)}, u32[]{:S(2)}, u32[]{:S(2)}) async-start(bf16[64,2,128,128]{3,2,1,0:T(8,128)(2,1)} %pack_blocks.8), calls=%async_computation.4 | async-start | bytes 8388608 | tf_op jit(solution)/shard_map/all_to_all | solution.py:319
  197.9 1.0 copy-start.12
  244.8 35.4 %all-to-all-start.5 = ((bf16[32,2,128,128]{3,2,1,0:T(8,128)(2,1)}), bf16[32,2,128,128]{3,2,1,0:T(8,128)(2,1)S(1)}, u32[]{:S(2)}, u32[]{:S(2)}) async-start(bf16[32,2,128,128]{3,2,1,0:T(8,128)(2,1)} %pack_blocks.9), calls=%async_computation.5 | async-start | bytes 4194304 | tf_op jit(solution)/shard_map/all_to_all | solution.py:319
  280.3 1.4 copy-start.2
  291.3 12.6 %collective-permute-start.8 = (bf16[256,1536]{1,0:T(8,128)(2,1)}, bf16[256,1536]{1,0:T(8,128)(2,1)S(1)}, u32[]{:S(2)}, u32[]{:S(2)}) collective-permute-start(bf16[256,1536]{1,0:T(8,128)(2,1)} %get-tuple-element.47), channel_id=1, source_target_pairs={{0,128},{1,129},{2,130},{3,131},{4,132},{5,133},{6,134},{7,135},{8... | collective-permute-start | bytes 2359304 | tf_op jit(solution)/shard_map/ppermute | solution.py:365
  292.6 11.3 %copy-start.3 = (f32[256,1536]{1,0:T(8,128)S(1)}, f32[256,1536]{1,0:T(8,128)}, u32[]{:S(2)}) copy-start(f32[256,1536]{1,0:T(8,128)} %get-tuple-element.48) | copy-start | bytes 4718596
  295.4 8.5 %collective-permute-start.9 = (bf16[256,512]{1,0:T(8,128)(2,1)S(1)}, bf16[256,512]{1,0:T(8,128)(2,1)S(1)}, u32[]{:S(2)}, u32[]{:S(2)}) collective-permute-start(bf16[256,512]{1,0:T(8,128)(2,1)S(1)} %get-tuple-element.69), channel_id=1, source_target_pairs={{0,128},{1,129},{2,130},{3,131},{4,132},{5,133},{6,134},{7,135},{8... | collective-permute-start | bytes 786440 | tf_op jit(solution)/shard_map/ppermute | solution.py:370
Sparse Core Ops, SparseCore 0:
  162.2 101.4 all-gather.1

commit v7 on v6

--- a/solution.py
+++ b/solution.py
@@ -237,7 +237,7 @@
         in_specs=in_specs + [smem, pl.BlockSpec(memory_space=pl.ANY), vmem],
         out_specs=[vmem] * len(out_shape),
         scratch_shapes=scratch,
-        compiler_params=pltpu.CompilerParams(vmem_limit_bytes=60 * 1024 * 1024),
+        compiler_params=pltpu.CompilerParams(vmem_limit_bytes=63 * 1024 * 1024),
         cost_estimate=LONG if pieces else LIGHT,
         name="project",
     )(*operands, segment, weight, residual)

time: 313 us -> 313 us (level)
    unnamed x31 -> x29, local copies, waits for them, and re-layouts: 8.04 us -> 6.66 us
  transfers between devices with their start and end apart: 17 -> 17, of which waited for: 10 -> 10; matrix products, arithmetic and copies ran while one was open for 6% -> 6% of each run, Pallas kernels for 24% -> 23%
where the time goes in v7:
time: 313 us; the launch traced here: 312 us
  waiting for transfers between devices  125 us (40%)
  Pallas kernels  83.1 us (27%)
  starting transfers between devices  63.7 us (20%)
  local copies, waits for them, and re-layouts  17.3 us (6%)
  between operations  14.6 us (5%)
  other arithmetic  5.65 us (2%)
    all_to_all x5, waiting for transfers between devices, served(): lax.all_to_all(sent, ('x', 'y'), split_axis=0, concat_axis=0, tiled=True)  75.2 us
    pallas_call x4, Pallas kernels, listed_part(): pl.pallas_call(lambda *refs: listed_kernel(((width // heads) ** (-0.5), h...  42.6 us
    ppermute x8, waiting for transfers between devices, step(): return (lax.ppermute(pair[0], 'z', up), lax.ppermute(pair[1], 'z', down))  41.8 us
    all_to_all x5, starting transfers between devices, served(): lax.all_to_all(sent, ('x', 'y'), split_axis=0, concat_axis=0, tiled=True)  39.5 us
    pallas_call x5, Pallas kernels, pack(): pl.pallas_call(lambda *refs: pack_kernel(slots, half, len(extras), *refs)...  17.8 us
    ppermute x8, starting transfers between devices, step(): return (lax.ppermute(pair[0], 'z', up), lax.ppermute(pair[1], 'z', down))  14.9 us
    pallas_call x1, Pallas kernels, local_part(): pl.pallas_call(lambda *refs: local_kernel(head_size ** (-0.5), *refs), gr...  12.1 us
    pallas_call x1, Pallas kernels, project(): pl.pallas_call(kernel, out_shape=out_shape, in_specs=in_specs + [smem, pl...  10.6 us
  transfers between devices with their start and end apart: 17, of which 10 were waited for; matrix products, arithmetic and copies ran while one was open for 6% of the time, Pallas kernels for 23%

profile of v7, /device:TPU:1, one launch (start us, length us, event | category | flops | bytes accessed | tf_op | source)
XLA Modules:
  0.0 311.9 jit_solution(18260927189311190706)
XLA Ops:
  9.2 2.5 collective-permute-start
  11.7 4.0 %collective-permute-start.1 = (bf16[32,2,128,128]{3,2,1,0:T(8,128)(2,1)S(1)}, bf16[32,2,128,128]{3,2,1,0:T(8,128)(2,1)}, u32[]{:S(2)}, u32[]{:S(2)}) collective-permute-start(bf16[32,2,128,128]{3,2,1,0:T(8,128)(2,1)S(1)} %pad_maximum_fusion.refs_1_), channel_id=1, source_target_pairs={{0,112},{16,0},{32,16},{48,32},{64,48},{80,64},{96,80},{112,96},{1... | collective-permute-start | bytes 6291464 | tf_op jit(solution)/shard_map/ppermute | solution.py:332
  18.1 6.8 %all-to-all-start = ((s32[16,8,2]{1,2,0:T(2,128)}), s32[16,8,2]{1,2,0:T(2,128)S(1)}, u32[]{:S(2)}, u32[]{:S(2)}) async-start(s32[16,8,2]{1,2,0:T(2,128)} %select_reduce_fusion), calls=%async_computation | async-start | bytes 32768 | tf_op jit(solution)/shard_map/all_to_all | solution.py:284
  32.0 2.2 pack_blocks.5
  34.3 6.1 %all-to-all-start.1 = ((bf16[48,2,128,128]{3,2,1,0:T(8,128)(2,1)}), bf16[48,2,128,128]{3,2,1,0:T(8,128)(2,1)}, u32[]{:S(2)}, u32[]{:S(2)}) async-start(bf16[48,2,128,128]{3,2,1,0:T(8,128)(2,1)} %pack_blocks.5), calls=%async_computation.1 | async-start | bytes 6291456 | tf_op jit(solution)/shard_map/all_to_all | solution.py:319
  40.4 12.1 %local_part.1.refs_7_ = f32[256,2048]{1,0:T(8,128)} custom-call(f32[16]{0:T(128)} %copy-done.5, f32[16]{0:T(128)} %copy-done.6, bf16[256,2048]{1,0:T(8,128)(2,1)} %bitcast.37, bf16[256,2048]{1,0:T(8,128)(2,1)} %bitcast.47, bf16[256,2048]{1,0:T(8,128)(2,1)} %bitcast.46), custom_call_target="tpu_custom_call" | custom-call | flops 1 | bytes 1 | tf_op jit(solution)/shard_map/local_part/pallas_call | solution.py:92
  55.9 5.2 %collective-permute-done.refs_1_ = bf16[32,2,128,128]{3,2,1,0:T(8,128)(2,1)} collective-permute-done((bf16[32,2,128,128]{3,2,1,0:T(8,128)(2,1)S(1)}, bf16[32,2,128,128]{3,2,1,0:T(8,128)(2,1)}, u32[]{:S(2)}, u32[]{:S(2)}) %collective-permute-start) | collective-permute-done | bytes 2097184 | tf_op jit(solution)/shard_map/ppermute | solution.py:332
  61.1 2.7 collective-permute-start.3
  63.8 4.2 %pack_blocks.6 = bf16[64,2,128,128]{3,2,1,0:T(8,128)(2,1)} custom-call(s32[64]{0:T(128)} %reshape.404.refs_0_, bf16[32,2,128,128]{3,2,1,0:T(8,128)(2,1)} %collective-permute-done.refs_1_, bf16[32,2,128,128]{3,2,1,0:T(8,128)(2,1)} %collective-permute-done.1.refs_2_), custom_call_target="tpu_custom_call" | custom-call | flops 49999998976 | bytes 150000000 | tf_op jit(solution)/shard_map/pack_blocks/pallas_call | solution.py:58
  68.0 11.4 %all-to-all-done.1.refs_6_ = bf16[48,2,128,128]{3,2,1,0:T(8,128)(2,1)} async-done(((bf16[48,2,128,128]{3,2,1,0:T(8,128)(2,1)}), bf16[48,2,128,128]{3,2,1,0:T(8,128)(2,1)}, u32[]{:S(2)}, u32[]{:S(2)}) %all-to-all-start.1) | async-done | bytes 3145760 | tf_op jit(solution)/shard_map/all_to_all | solution.py:319
  79.4 4.6 %all-to-all-start.2 = ((bf16[64,2,128,128]{3,2,1,0:T(8,128)(2,1)}), bf16[64,2,128,128]{3,2,1,0:T(8,128)(2,1)}, u32[]{:S(2)}, u32[]{:S(2)}) async-start(bf16[64,2,128,128]{3,2,1,0:T(8,128)(2,1)} %pack_blocks.6), calls=%async_computation.2 | async-start | bytes 8388608 | tf_op jit(solution)/shard_map/all_to_all | solution.py:319
  86.5 22.0 %collective-permute-done.2.refs_1_ = bf16[32,2,128,128]{3,2,1,0:T(8,128)(2,1)S(1)} collective-permute-done((bf16[32,2,128,128]{3,2,1,0:T(8,128)(2,1)}, bf16[32,2,128,128]{3,2,1,0:T(8,128)(2,1)S(1)}, u32[]{:S(2)}, u32[]{:S(2)}) %collective-permute-start.2) | collective-permute-done | bytes 2097184 | tf_op jit(solution)/shard_map/ppermute | solution.py:332
  109.9 2.7 collective-permute-start.5
  112.6 4.2 %pack_blocks.7 = bf16[64,2,128,128]{3,2,1,0:T(8,128)(2,1)} custom-call(s32[64]{0:T(128)} %reshape.405.refs_0_, bf16[32,2,128,128]{3,2,1,0:T(8,128)(2,1)} %copy-done.10, bf16[32,2,128,128]{3,2,1,0:T(8,128)(2,1)} %collective-permute-done.3.refs_2_), custom_call_target="tpu_custom_call" | custom-call | flops 49999998976 | bytes 150000000 | tf_op jit(solution)/shard_map/pack_blocks/pallas_call | solution.py:58
  116.8 7.9 %listed_part.4.refs_7_ = f32[256,2048]{1,0:T(8,128)} custom-call(s32[128]{0:T(128)} %select_reduce_fusion.1.refs_0_, s32[2]{0:T(128)} %get-tuple-element.67.refs_1_, s32[128]{0:T(128)} %get-tuple-element.57.refs_2_, f32[128]{0:T(128)} %multiply_subtract_fusion.refs_3_, f32[128]{0:T(128)} %get-tuple-element.55.refs_4_, bf16[256,2048]{1,0:T(8,128)(2,1)} %bitcast.38, ...), custom_call_target="tpu_custom_call" | custom-call | flops 1 | bytes 1 | tf_op jit(solution)/shard_map/listed_part/pallas_call | solution.py:156
  124.7 7.7 %all-to-all-done.2.refs_6_ = bf16[64,2,128,128]{3,2,1,0:T(8,128)(2,1)} async-done(((bf16[64,2,128,128]{3,2,1,0:T(8,128)(2,1)}), bf16[64,2,128,128]{3,2,1,0:T(8,128)(2,1)}, u32[]{:S(2)}, u32[]{:S(2)}) %all-to-all-start.2) | async-done | bytes 4194336 | tf_op jit(solution)/shard_map/all_to_all | solution.py:319
  132.4 9.5 %all-to-all-start.3 = ((bf16[64,2,128,128]{3,2,1,0:T(8,128)(2,1)}), bf16[64,2,128,128]{3,2,1,0:T(8,128)(2,1)}, u32[]{:S(2)}, u32[]{:S(2)}) async-start(bf16[64,2,128,128]{3,2,1,0:T(8,128)(2,1)} %pack_blocks.7), calls=%async_computation.3 | async-start | bytes 8388608 | tf_op jit(solution)/shard_map/all_to_all | solution.py:319
  141.9 14.6 %collective-permute-done.4.refs_1_ = bf16[32,2,128,128]{3,2,1,0:T(8,128)(2,1)S(1)} collective-permute-done((bf16[32,2,128,128]{3,2,1,0:T(8,128)(2,1)}, bf16[32,2,128,128]{3,2,1,0:T(8,128)(2,1)S(1)}, u32[]{:S(2)}, u32[]{:S(2)}) %collective-permute-start.4) | collective-permute-done | bytes 2097184 | tf_op jit(solution)/shard_map/ppermute | solution.py:332
  159.1 2.9 collective-permute-start.7
  162.1 4.3 %pack_blocks.8 = bf16[64,2,128,128]{3,2,1,0:T(8,128)(2,1)} custom-call(s32[64]{0:T(128)} %reshape.406.refs_0_, bf16[32,2,128,128]{3,2,1,0:T(8,128)(2,1)} %copy-done.3, bf16[32,2,128,128]{3,2,1,0:T(8,128)(2,1)} %collective-permute-done.5.refs_2_), custom_call_target="tpu_custom_call" | custom-call | flops 49999998976 | bytes 150000000 | tf_op jit(solution)/shard_map/pack_blocks/pallas_call | solution.py:58
  166.4 12.4 %listed_part.5.refs_7_ = f32[256,2048]{1,0:T(8,128)} custom-call(s32[128]{0:T(128)} %select_reduce_fusion.1.refs_0_, s32[2]{0:T(128)} %get-tuple-element.66.refs_1_, s32[128]{0:T(128)} %get-tuple-element.57.refs_2_, f32[128]{0:T(128)} %multiply_subtract_fusion.refs_3_, f32[128]{0:T(128)} %get-tuple-element.55.refs_4_, bf16[256,2048]{1,0:T(8,128)(2,1)} %bitcast.39, ...), custom_call_target="tpu_custom_call" | custom-call | flops 1 | bytes 1 | tf_op jit(solution)/shard_map/listed_part/pallas_call | solution.py:156
  178.8 10.3 %all-to-all-done.3.refs_6_ = bf16[64,2,128,128]{3,2,1,0:T(8,128)(2,1)} async-done(((bf16[64,2,128,128]{3,2,1,0:T(8,128)(2,1)}), bf16[64,2,128,128]{3,2,1,0:T(8,128)(2,1)}, u32[]{:S(2)}, u32[]{:S(2)}) %all-to-all-start.3) | async-done | bytes 4194336 | tf_op jit(solution)/shard_map/all_to_all | solution.py:319
  189.1 8.9 %all-to-all-start.4 = ((bf16[64,2,128,128]{3,2,1,0:T(8,128)(2,1)}), bf16[64,2,128,128]{3,2,1,0:T(8,128)(2,1)}, u32[]{:S(2)}, u32[]{:S(2)}) async-start(bf16[64,2,128,128]{3,2,1,0:T(8,128)(2,1)} %pack_blocks.8), calls=%async_computation.4 | async-start | bytes 8388608 | tf_op jit(solution)/shard_map/all_to_all | solution.py:319
  199.0 2.9 pack_blocks.9
  202.0 12.4 %listed_part.6.refs_7_ = f32[256,2048]{1,0:T(8,128)} custom-call(s32[128]{0:T(128)} %select_reduce_fusion.1.refs_0_, s32[2]{0:T(128)} %get-tuple-element.65.refs_1_, s32[128]{0:T(128)} %get-tuple-element.57.refs_2_, f32[128]{0:T(128)} %multiply_subtract_fusion.refs_3_, f32[128]{0:T(128)} %get-tuple-element.55.refs_4_, bf16[256,2048]{1,0:T(8,128)(2,1)} %bitcast.40, ...), custom_call_target="tpu_custom_call" | custom-call | flops 1 | bytes 1 | tf_op jit(solution)/shard_map/listed_part/pallas_call | solution.py:156
  214.4 30.6 %all-to-all-done.4.refs_6_ = bf16[64,2,128,128]{3,2,1,0:T(8,128)(2,1)} async-done(((bf16[64,2,128,128]{3,2,1,0:T(8,128)(2,1)}), bf16[64,2,128,128]{3,2,1,0:T(8,128)(2,1)}, u32[]{:S(2)}, u32[]{:S(2)}) %all-to-all-start.4) | async-done | bytes 4194336 | tf_op jit(solution)/shard_map/all_to_all | solution.py:319
  244.9 10.4 %all-to-all-start.5 = ((bf16[32,2,128,128]{3,2,1,0:T(8,128)(2,1)}), bf16[32,2,128,128]{3,2,1,0:T(8,128)(2,1)}, u32[]{:S(2)}, u32[]{:S(2)}) async-start(bf16[32,2,128,128]{3,2,1,0:T(8,128)(2,1)} %pack_blocks.9), calls=%async_computation.5 | async-start | bytes 4194304 | tf_op jit(solution)/shard_map/all_to_all | solution.py:319
  255.4 9.8 %listed_part.7.refs_7_ = f32[256,2048]{1,0:T(8,128)} custom-call(s32[128]{0:T(128)} %select_reduce_fusion.1.refs_0_, s32[2]{0:T(128)} %get-tuple-element.64.refs_1_, s32[128]{0:T(128)} %get-tuple-element.57.refs_2_, f32[128]{0:T(128)} %multiply_subtract_fusion.refs_3_, f32[128]{0:T(128)} %get-tuple-element.55.refs_4_, bf16[256,2048]{1,0:T(8,128)(2,1)} %bitcast.41, ...), custom_call_target="tpu_custom_call" | custom-call | flops 99999997952 | bytes 150000000 | tf_op jit(solution)/shard_map/listed_part/pallas_call | solution.py:156
  265.2 15.3 %all-to-all-done.5.refs_6_ = bf16[32,2,128,128]{3,2,1,0:T(8,128)(2,1)} async-done(((bf16[32,2,128,128]{3,2,1,0:T(8,128)(2,1)}), bf16[32,2,128,128]{3,2,1,0:T(8,128)(2,1)}, u32[]{:S(2)}, u32[]{:S(2)}) %all-to-all-start.5) | async-done | bytes 2097184 | tf_op jit(solution)/shard_map/all_to_all | solution.py:319
  280.5 10.6 %project.1 = (bf16[256,2048]{1,0:T(8,128)(2,1)}, f32[256,1536]{1,0:T(8,128)}, bf16[256,1536]{1,0:T(8,128)(2,1)}) custom-call(s32[128]{0:T(128)} %select_reduce_fusion.1.refs_0_, s32[2]{0:T(128)} %get-tuple-element.68.refs_1_, s32[128]{0:T(128)} %get-tuple-element.57.refs_2_, f32[128]{0:T(128)} %multiply_subtract_fusion.refs_3_, ...), custom_call_target="tpu_custom_call" | custom-call | flops 99999997952 | bytes 150000000 | tf_op jit(solution)/shard_map/project/pallas_call | solution.py:234
  292.4 2.7 fusion.24
  296.5 7.2 %collective-permute-done.9 = bf16[256,512]{1,0:T(8,128)(2,1)S(1)} collective-permute-done((bf16[256,512]{1,0:T(8,128)(2,1)S(1)}, bf16[256,512]{1,0:T(8,128)(2,1)S(1)}, u32[]{:S(2)}, u32[]{:S(2)}) %collective-permute-start.9) | collective-permute-done | bytes 262176 | tf_op jit(solution)/shard_map/ppermute | solution.py:370
  (93 shorter events, 26.2 us)
Async XLA Ops:
  6.5 1.8 copy-start.1
  8.9 6.9 %copy-start.7 = (s32[1,2,16,4]{2,3,1,0:T(4,128)S(1)}, s32[1,2,16,4]{2,3,1,0:T(4,128)}, u32[]{:S(2)}) copy-start(s32[1,2,16,4]{2,3,1,0:T(4,128)} %param.16) | copy-start | bytes 1540
  8.9 7.8 %copy-start.12 = (s32[8]{0:T(128)S(1)}, s32[8]{0:T(128)}, u32[]{:S(2)}) copy-start(s32[8]{0:T(128)} %constant.160.clone) | copy-start | bytes 100
  8.9 16.9 %copy-start.8 = (f32[1,16]{1,0:T(1,128)S(1)}, f32[1,16]{1,0:T(1,128)}, u32[]{:S(2)}) copy-start(f32[1,16]{1,0:T(1,128)} %param.14) | copy-start | bytes 196
  8.9 16.9 %copy-start.9 = (f32[1,16]{1,0:T(1,128)S(1)}, f32[1,16]{1,0:T(1,128)}, u32[]{:S(2)}) copy-start(f32[1,16]{1,0:T(1,128)} %param.15) | copy-start | bytes 196
  8.9 17.4 %copy-start = (s32[128]{0:T(128)S(1)}, s32[128]{0:T(128)}, u32[]{:S(2)}) copy-start(s32[128]{0:T(128)} %param.17) | copy-start | bytes 1540
  8.9 21.7 %copy-start.4 = (bf16[1,16,2048]{2,1,0:T(8,128)(2,1)S(1)}, bf16[1,16,2048]{2,1,0:T(8,128)(2,1)}, u32[]{:S(2)}) copy-start(bf16[1,16,2048]{2,1,0:T(8,128)(2,1)} %param.18) | copy-start | bytes 196612
  9.2 51.9 %collective-permute-start = (bf16[32,2,128,128]{3,2,1,0:T(8,128)(2,1)S(1)}, bf16[32,2,128,128]{3,2,1,0:T(8,128)(2,1)}, u32[]{:S(2)}, u32[]{:S(2)}) collective-permute-start(bf16[32,2,128,128]{3,2,1,0:T(8,128)(2,1)S(1)} %pad_maximum_fusion.refs_1_), channel_id=1, source_target_pairs={{0,16},{16,32},{32,48},{48,64},{64,80},{80,96},{96,112},{112,0},{1... | collective-permute-start | bytes 6291464 | tf_op jit(solution)/shard_map/ppermute | solution.py:332
  11.7 49.4 %collective-permute-start.1 = (bf16[32,2,128,128]{3,2,1,0:T(8,128)(2,1)S(1)}, bf16[32,2,128,128]{3,2,1,0:T(8,128)(2,1)}, u32[]{:S(2)}, u32[]{:S(2)}) collective-permute-start(bf16[32,2,128,128]{3,2,1,0:T(8,128)(2,1)S(1)} %pad_maximum_fusion.refs_1_), channel_id=1, source_target_pairs={{0,112},{16,0},{32,16},{48,32},{64,48},{80,64},{96,80},{112,96},{1... | collective-permute-start | bytes 6291464 | tf_op jit(solution)/shard_map/ppermute | solution.py:332
  18.1 13.2 %all-to-all-start = ((s32[16,8,2]{1,2,0:T(2,128)}), s32[16,8,2]{1,2,0:T(2,128)S(1)}, u32[]{:S(2)}, u32[]{:S(2)}) async-start(s32[16,8,2]{1,2,0:T(2,128)} %select_reduce_fusion), calls=%async_computation | async-start | bytes 32768 | tf_op jit(solution)/shard_map/all_to_all | solution.py:284
  25.9 8.4 %copy-start.5 = (f32[16]{0:T(128)}, f32[16]{0:T(128)S(1)}, u32[]{:S(2)}) copy-start(f32[16]{0:T(128)S(1)} %get-tuple-element.71.refs_0_) | copy-start | bytes 196
  25.9 8.4 %copy-start.6 = (f32[16]{0:T(128)}, f32[16]{0:T(128)S(1)}, u32[]{:S(2)}) copy-start(f32[16]{0:T(128)S(1)} %get-tuple-element.72.refs_1_) | copy-start | bytes 196
  34.3 45.1 %all-to-all-start.1 = ((bf16[48,2,128,128]{3,2,1,0:T(8,128)(2,1)}), bf16[48,2,128,128]{3,2,1,0:T(8,128)(2,1)}, u32[]{:S(2)}, u32[]{:S(2)}) async-start(bf16[48,2,128,128]{3,2,1,0:T(8,128)(2,1)} %pack_blocks.5), calls=%async_computation.1 | async-start | bytes 6291456 | tf_op jit(solution)/shard_map/all_to_all | solution.py:319
  61.1 47.4 %collective-permute-start.2 = (bf16[32,2,128,128]{3,2,1,0:T(8,128)(2,1)}, bf16[32,2,128,128]{3,2,1,0:T(8,128)(2,1)S(1)}, u32[]{:S(2)}, u32[]{:S(2)}) collective-permute-start(bf16[32,2,128,128]{3,2,1,0:T(8,128)(2,1)} %collective-permute-done.refs_1_), channel_id=1, source_target_pairs={{0,16},{16,32},{32,48},{48,64},{64,80},{80,96},{96,112},{112,0},{1... | collective-permute-start | bytes 6291464 | tf_op jit(solution)/shard_map/ppermute | solution.py:332
  61.1 48.8 %collective-permute-start.3 = (bf16[32,2,128,128]{3,2,1,0:T(8,128)(2,1)}, bf16[32,2,128,128]{3,2,1,0:T(8,128)(2,1)}, u32[]{:S(2)}, u32[]{:S(2)}) collective-permute-start(bf16[32,2,128,128]{3,2,1,0:T(8,128)(2,1)} %collective-permute-done.1.refs_2_), channel_id=1, source_target_pairs={{0,112},{16,0},{32,16},{48,32},{64,48},{80,64},{96,80},{112,96},{1... | collective-permute-start | bytes 6291464 | tf_op jit(solution)/shard_map/ppermute | solution.py:332
  79.4 53.0 %all-to-all-start.2 = ((bf16[64,2,128,128]{3,2,1,0:T(8,128)(2,1)}), bf16[64,2,128,128]{3,2,1,0:T(8,128)(2,1)}, u32[]{:S(2)}, u32[]{:S(2)}) async-start(bf16[64,2,128,128]{3,2,1,0:T(8,128)(2,1)} %pack_blocks.6), calls=%async_computation.2 | async-start | bytes 8388608 | tf_op jit(solution)/shard_map/all_to_all | solution.py:319
  108.5 1.4 copy-start.10
  109.9 46.6 %collective-permute-start.4 = (bf16[32,2,128,128]{3,2,1,0:T(8,128)(2,1)}, bf16[32,2,128,128]{3,2,1,0:T(8,128)(2,1)S(1)}, u32[]{:S(2)}, u32[]{:S(2)}) collective-permute-start(bf16[32,2,128,128]{3,2,1,0:T(8,128)(2,1)} %copy-done.10), channel_id=1, source_target_pairs={{0,16},{16,32},{32,48},{48,64},{64,80},{80,96},{96,112},{112,0},{1... | collective-permute-start | bytes 6291464 | tf_op jit(solution)/shard_map/ppermute | solution.py:332
  109.9 46.6 %collective-permute-start.5 = (bf16[32,2,128,128]{3,2,1,0:T(8,128)(2,1)}, bf16[32,2,128,128]{3,2,1,0:T(8,128)(2,1)}, u32[]{:S(2)}, u32[]{:S(2)}) collective-permute-start(bf16[32,2,128,128]{3,2,1,0:T(8,128)(2,1)} %collective-permute-done.3.refs_2_), channel_id=1, source_target_pairs={{0,112},{16,0},{32,16},{48,32},{64,48},{80,64},{96,80},{112,96},{1... | collective-permute-start | bytes 6291464 | tf_op jit(solution)/shard_map/ppermute | solution.py:332
  132.4 56.7 %all-to-all-start.3 = ((bf16[64,2,128,128]{3,2,1,0:T(8,128)(2,1)}), bf16[64,2,128,128]{3,2,1,0:T(8,128)(2,1)}, u32[]{:S(2)}, u32[]{:S(2)}) async-start(bf16[64,2,128,128]{3,2,1,0:T(8,128)(2,1)} %pack_blocks.7), calls=%async_computation.3 | async-start | bytes 8388608 | tf_op jit(solution)/shard_map/all_to_all | solution.py:319
  141.9 138.6 %all-gather.2.cloned.1.call-start = ((), (), s32[]{:S(2)}) async-start(), calls=%async_computation.6 | async-start | bytes 9437184 | tf_op jit(solution)/shard_map/all_gather | solution.py:348
  156.5 1.3 copy-start.3
  157.8 40.2 %collective-permute-start.6 = (bf16[16,2,128,128]{3,2,1,0:T(8,128)(2,1)S(1)}, bf16[16,2,128,128]{3,2,1,0:T(8,128)(2,1)}, u32[]{:S(2)}, u32[]{:S(2)}) collective-permute-start(bf16[16,2,128,128]{3,2,1,0:T(8,128)(2,1)S(1)} %slice.51), channel_id=1, source_target_pairs={{0,16},{16,32},{32,48},{48,64},{64,80},{80,96},{96,112},{112,0},{1... | collective-permute-start | bytes 3145736 | tf_op jit(solution)/shard_map/ppermute | solution.py:332
  159.1 38.9 %collective-permute-start.7 = (bf16[16,2,128,128]{3,2,1,0:T(8,128)(2,1)S(1)}, bf16[16,2,128,128]{3,2,1,0:T(8,128)(2,1)S(1)}, u32[]{:S(2)}, u32[]{:S(2)}) collective-permute-start(bf16[16,2,128,128]{3,2,1,0:T(8,128)(2,1)S(1)} %slice.52), channel_id=1, source_target_pairs={{0,112},{16,0},{32,16},{48,32},{64,48},{80,64},{96,80},{112,96},{1... | collective-permute-start | bytes 3145736 | tf_op jit(solution)/shard_map/ppermute | solution.py:332
  189.1 55.8 %all-to-all-start.4 = ((bf16[64,2,128,128]{3,2,1,0:T(8,128)(2,1)}), bf16[64,2,128,128]{3,2,1,0:T(8,128)(2,1)}, u32[]{:S(2)}, u32[]{:S(2)}) async-start(bf16[64,2,128,128]{3,2,1,0:T(8,128)(2,1)} %pack_blocks.8), calls=%async_computation.4 | async-start | bytes 8388608 | tf_op jit(solution)/shard_map/all_to_all | solution.py:319
  198.0 1.0 copy-start.11
  244.9 35.5 %all-to-all-start.5 = ((bf16[32,2,128,128]{3,2,1,0:T(8,128)(2,1)}), bf16[32,2,128,128]{3,2,1,0:T(8,128)(2,1)}, u32[]{:S(2)}, u32[]{:S(2)}) async-start(bf16[32,2,128,128]{3,2,1,0:T(8,128)(2,1)} %pack_blocks.9), calls=%async_computation.5 | async-start | bytes 4194304 | tf_op jit(solution)/shard_map/all_to_all | solution.py:319
  291.1 12.6 %collective-permute-start.8 = (bf16[256,1536]{1,0:T(8,128)(2,1)}, bf16[256,1536]{1,0:T(8,128)(2,1)S(1)}, u32[]{:S(2)}, u32[]{:S(2)}) collective-permute-start(bf16[256,1536]{1,0:T(8,128)(2,1)} %get-tuple-element.47), channel_id=1, source_target_pairs={{0,128},{1,129},{2,130},{3,131},{4,132},{5,133},{6,134},{7,135},{8... | collective-permute-start | bytes 2359304 | tf_op jit(solution)/shard_map/ppermute | solution.py:365
  292.4 11.3 %copy-start.2 = (f32[256,1536]{1,0:T(8,128)S(1)}, f32[256,1536]{1,0:T(8,128)}, u32[]{:S(2)}) copy-start(f32[256,1536]{1,0:T(8,128)} %get-tuple-element.48) | copy-start | bytes 4718596
  295.2 8.5 %collective-permute-start.9 = (bf16[256,512]{1,0:T(8,128)(2,1)S(1)}, bf16[256,512]{1,0:T(8,128)(2,1)S(1)}, u32[]{:S(2)}, u32[]{:S(2)}) collective-permute-start(bf16[256,512]{1,0:T(8,128)(2,1)S(1)} %get-tuple-element.69), channel_id=1, source_target_pairs={{0,128},{1,129},{2,130},{3,131},{4,132},{5,133},{6,134},{7,135},{8... | collective-permute-start | bytes 786440 | tf_op jit(solution)/shard_map/ppermute | solution.py:370
Sparse Core Ops, SparseCore 0:
  162.2 101.4 all-gather.1
